TPU v7x, 32 devices: a whole 2x2x4 slice. The times are simulated.
32 devices in a mesh: batch: 4 (over x, core), seq: 8 (over z, y).
Axes of the slice: x: 2, y: 2, z: 4, core: 2. Of those that a mesh axis runs over, the one named last changes fastest.
Arguments:
- token_ids: int32 [4, 1024], P('batch', 'seq'), may hold values from 0 to 32127
- embedding: bfloat16 [32128, 768], P(('batch', 'seq')), may hold values from -6 to 6
- gain_attn: bfloat16 [2, 768], P(None, ('batch', 'seq')), may hold values from 0.5 to 1.5
- w_qkv: bfloat16 [2, 768, 2304], P(None, ('batch', 'seq')), may hold values from -0.21875 to 0.21875
- w_proj: bfloat16 [2, 768, 768], P(None, ('batch', 'seq')), may hold values from -1.75 to 1.75
- gain_ffn: bfloat16 [2, 768], P(None, ('batch', 'seq')), may hold values from 0.5 to 1.5
- w_in: bfloat16 [2, 768, 3072], P(None, ('batch', 'seq')), may hold values from -0.21875 to 0.21875
- w_back: bfloat16 [2, 3072, 768], P(None, ('batch', 'seq')), may hold values from -0.109375 to 0.109375
- mix_pre: float32 [2, 12, 12], replicated, may hold values from -2.5 to 2.5
- mix_post: float32 [2, 12, 12], replicated, may hold values from -2.5 to 2.5
- cotangent: bfloat16 [4, 1024, 768], P('batch', 'seq'), may hold values from -6 to 6
Outputs:
- output: bfloat16 [4, 1024, 768], P('batch', 'seq')
- embedding_grad: float32 [32128, 768], P(('batch', 'seq'))
- gain_attn_grad: float32 [2, 768], P(None, ('batch', 'seq'))
- w_qkv_grad: float32 [2, 768, 2304], P(None, ('batch', 'seq'))
- w_proj_grad: float32 [2, 768, 768], P(None, ('batch', 'seq'))
- gain_ffn_grad: float32 [2, 768], P(None, ('batch', 'seq'))
- w_in_grad: float32 [2, 768, 3072], P(None, ('batch', 'seq'))
- w_back_grad: float32 [2, 3072, 768], P(None, ('batch', 'seq'))
- mix_pre_grad: float32 [2, 12, 12], replicated
- mix_post_grad: float32 [2, 12, 12], replicated
Inputs may be any that keep to these rules, and one draw needn't show every extreme that they name: `token_ids`: each id names a row of the embedding table.
All inputs are finite; a program needn't handle non-finite values.
Results may differ from a plain program's by a relative error of at most 0.04.
Values may be sent and summed in bfloat16 or wider, within the bound.
No kernel may reach another device: no remote copies, remote signals or barrier semaphores. Data moves between devices by JAX's collectives and lax.ppermute only.
A program may use at most 256 MiB of HBM per device.

v0:
```python
import jax
import jax.numpy as jnp
from jax import lax
from jax.sharding import PartitionSpec as P

D = 768
H = 12
E = 64
LAYERS = 2


HIGHEST = lax.Precision.HIGHEST
NEGATIVE = -1e30


def rms_norm(values, gain):
    return values * lax.rsqrt(jnp.mean(values * values, axis=-1, keepdims=True) + 1e-06) * gain


def fetch_layer(layer_index, gain_attn, w_qkv, w_proj, gain_ffn, w_in, w_back):
    return (
        lax.all_gather(gain_attn[layer_index], ("batch", "seq"), axis=0, tiled=True),
        lax.all_gather(w_qkv[layer_index], ("batch", "seq"), axis=0, tiled=True),
        lax.all_gather(w_proj[layer_index], ("batch", "seq"), axis=0, tiled=True),
        lax.all_gather(gain_ffn[layer_index], ("batch", "seq"), axis=0, tiled=True),
        lax.all_gather(w_in[layer_index], ("batch", "seq"), axis=0, tiled=True),
        lax.all_gather(w_back[layer_index], ("batch", "seq"), axis=0, tiled=True),
    )


def block_logits(queries, key_block, mixing_pre, query_pos, key_pos):
    scores = jnp.einsum(
        "thd,khd->htk", queries, key_block, preferred_element_type=jnp.float32
    ) * E ** (-0.5)
    logits = jnp.einsum("htk,hg->gtk", scores, mixing_pre, precision=HIGHEST)
    allowed = key_pos[None, :] <= query_pos[:, None]
    return (scores, jnp.where(allowed[None], logits, NEGATIVE))


def split_blocks(keys_full, values_full):
    length = keys_full.shape[0]
    block_rows = min(512, length)
    block_count = length // block_rows
    key_blocks = keys_full.reshape(block_count, block_rows, H, E)
    value_blocks = values_full.reshape(block_count, block_rows, H, E)
    starts = jnp.arange(block_count, dtype=jnp.int32) * block_rows
    offsets = jnp.arange(block_rows, dtype=jnp.int32)
    return (key_blocks, value_blocks, starts, offsets)


def attend_forward(queries, keys_full, values_full, mixing_pre, mixing_post, query_pos):
    key_blocks, value_blocks, starts, offsets = split_blocks(keys_full, values_full)
    rows_here = queries.shape[0]
    last_query = query_pos[-1]

    def max_pass(running, inputs):
        key_block, block_start = inputs

        def max_live(state):
            row_max, row_sum = state
            unused_scores, logits = block_logits(
                queries, key_block, mixing_pre, query_pos, block_start + offsets
            )
            new_max = jnp.maximum(row_max, jnp.max(logits, axis=-1))
            new_sum = row_sum * jnp.exp(row_max - new_max) + jnp.sum(
                jnp.exp(logits - new_max[..., None]), axis=-1
            )
            return (new_max, new_sum)

        return (lax.cond(block_start <= last_query, max_live, lambda state: state, running), None)

    begin = (
        jnp.full((H, rows_here), NEGATIVE, jnp.float32),
        jnp.zeros((H, rows_here), jnp.float32),
    )
    (row_max, row_sum), ignored = lax.scan(max_pass, begin, (key_blocks, starts))
    log_total = row_max + jnp.log(row_sum)

    def value_pass(accumulated, inputs):
        key_block, value_block, block_start = inputs

        def value_live(state):
            unused_scores, logits = block_logits(
                queries, key_block, mixing_pre, query_pos, block_start + offsets
            )
            normalized = jnp.exp(logits - log_total[..., None])
            mixture = jnp.einsum("gtk,gf->ftk", normalized, mixing_post, precision=HIGHEST).astype(
                jnp.bfloat16
            )
            return state + jnp.einsum(
                "ftk,kfd->tfd", mixture, value_block, preferred_element_type=jnp.float32
            )

        return (
            lax.cond(block_start <= last_query, value_live, lambda state: state, accumulated),
            None,
        )

    attended, ignored = lax.scan(
        value_pass, jnp.zeros((rows_here, H, E), jnp.float32), (key_blocks, value_blocks, starts)
    )
    return (attended.reshape(rows_here, D), log_total)


def attend_backward(
    queries, keys_full, values_full, mixing_pre, mixing_post, query_pos, log_total, grad_out
):
    key_blocks, value_blocks, starts, offsets = split_blocks(keys_full, values_full)
    rows_here = queries.shape[0]
    last_query = query_pos[-1]
    piece_shape = (1,)

    def recompute(key_block, value_block, block_start):
        scores, logits = block_logits(
            queries, key_block, mixing_pre, query_pos, block_start + offsets
        )
        normalized = jnp.exp(logits - log_total[..., None])
        grad_mix = jnp.einsum(
            "thd,khd->htk", grad_out, value_block, preferred_element_type=jnp.float32
        )
        grad_prob = jnp.einsum("ftk,gf->gtk", grad_mix, mixing_post, precision=HIGHEST)
        return (scores, normalized, grad_mix, grad_prob)

    def first_pass(running, inputs):
        key_block, value_block, block_start = inputs

        def first_live(state):
            row_dot, post_grad = state
            scores, normalized, grad_mix, grad_prob = recompute(key_block, value_block, block_start)
            row_dot = row_dot + jnp.sum(normalized * grad_prob, axis=-1)
            post_grad = post_grad + jnp.einsum(
                "gtk,ftk->gf", normalized, grad_mix, precision=HIGHEST
            )
            value_grad = jnp.zeros(piece_shape, jnp.float32)
            return ((row_dot, post_grad), value_grad)

        def first_dead(state):
            return (state, jnp.zeros(piece_shape, jnp.float32))

        return lax.cond(block_start <= last_query, first_live, first_dead, running)

    begin = (jnp.zeros((H, rows_here), jnp.float32), jnp.zeros((H, H), jnp.float32))
    (row_dot, post_grad), value_grads = lax.scan(
        first_pass, begin, (key_blocks, value_blocks, starts)
    )

    def second_pass(running, inputs):
        key_block, value_block, block_start = inputs

        def second_live(state):
            query_grad, pre_grad = state
            scores, normalized, grad_mix, grad_prob = recompute(key_block, value_block, block_start)
            grad_logit = normalized * (grad_prob - row_dot[..., None])
            grad_score = jnp.einsum("gtk,hg->htk", grad_logit, mixing_pre, precision=HIGHEST)
            pre_grad = pre_grad + jnp.einsum("htk,gtk->hg", scores, grad_logit, precision=HIGHEST)
            score_low = grad_score.astype(jnp.bfloat16)
            query_grad = query_grad + jnp.einsum(
                "htk,khd->thd", score_low, key_block, preferred_element_type=jnp.float32
            ) * E ** (-0.5)
            key_grad = jnp.zeros(piece_shape, jnp.float32)
            return ((query_grad, pre_grad), key_grad)

        def second_dead(state):
            return (state, jnp.zeros(piece_shape, jnp.float32))

        return lax.cond(block_start <= last_query, second_live, second_dead, running)

    begin = (jnp.zeros((rows_here, H, E), jnp.float32), jnp.zeros((H, H), jnp.float32))
    (query_grad, pre_grad), key_grads = lax.scan(
        second_pass, begin, (key_blocks, value_blocks, starts)
    )
    key_grads = None
    value_grads = None
    return (query_grad.reshape(rows_here, D), key_grads, value_grads, pre_grad, post_grad, row_dot)


def attend_keys(
    all_queries, all_grads, all_log, all_dot, own_keys, own_values, mixing_pre, mixing_post, key_pos
):
    length = all_queries.shape[0]
    own_rows = own_keys.shape[0]
    block_rows = min(512, length)
    block_count = length // block_rows
    query_blocks = all_queries.reshape(block_count, block_rows, H, E)
    grad_blocks = all_grads.reshape(block_count, block_rows, H, E)
    log_blocks = all_log.reshape(H, block_count, block_rows).transpose(1, 0, 2)
    dot_blocks = all_dot.reshape(H, block_count, block_rows).transpose(1, 0, 2)
    starts = jnp.arange(block_count, dtype=jnp.int32) * block_rows
    offsets = jnp.arange(block_rows, dtype=jnp.int32)
    first_key = key_pos[0]

    def key_pass(running, inputs):
        query_block, grad_block, log_block, dot_block, block_start = inputs

        def key_live(state):
            key_grad, value_grad = state
            query_pos = block_start + offsets
            unused_scores, logits = block_logits(
                query_block, own_keys, mixing_pre, query_pos, key_pos
            )
            normalized = jnp.exp(logits - log_block[..., None])
            grad_mix = jnp.einsum(
                "thd,khd->htk", grad_block, own_values, preferred_element_type=jnp.float32
            )
            grad_prob = jnp.einsum("ftk,gf->gtk", grad_mix, mixing_post, precision=HIGHEST)
            mixture = jnp.einsum("gtk,gf->ftk", normalized, mixing_post, precision=HIGHEST).astype(
                jnp.bfloat16
            )
            value_grad = value_grad + jnp.einsum(
                "ftk,tfd->kfd", mixture, grad_block, preferred_element_type=jnp.float32
            )
            grad_logit = normalized * (grad_prob - dot_block[..., None])
            grad_score = jnp.einsum(
                "gtk,hg->htk", grad_logit, mixing_pre, precision=HIGHEST
            ).astype(jnp.bfloat16)
            key_grad = key_grad + jnp.einsum(
                "htk,thd->khd", grad_score, query_block, preferred_element_type=jnp.float32
            ) * E ** (-0.5)
            return (key_grad, value_grad)

        return (
            lax.cond(
                block_start + block_rows - 1 >= first_key, key_live, lambda state: state, running
            ),
            None,
        )

    begin = (jnp.zeros((own_rows, H, E), jnp.float32), jnp.zeros((own_rows, H, E), jnp.float32))
    (key_grad, value_grad), ignored = lax.scan(
        key_pass, begin, (query_blocks, grad_blocks, log_blocks, dot_blocks, starts)
    )
    return (key_grad.reshape(own_rows, D), value_grad.reshape(own_rows, D))


def shards(
    token_ids,
    embedding,
    gain_attn,
    w_qkv,
    w_proj,
    gain_ffn,
    w_in,
    w_back,
    mix_pre,
    mix_post,
    cotangent,
):
    token_list = token_ids.reshape(-1)
    rows_here = token_list.shape[0]
    shard_rows = lax.all_gather(embedding, ("batch", "seq"), axis=0, tiled=True)
    columns = jnp.arange(shard_rows.shape[0], dtype=jnp.int32)
    selector = (token_list[:, None] == columns[None, :]).astype(jnp.bfloat16)
    stream = jnp.dot(selector, shard_rows, preferred_element_type=jnp.float32)
    position = lax.axis_index("seq") * rows_here + jnp.arange(rows_here, dtype=jnp.int32)
    gathered = []
    saved_state = []
    for layer_index in range(LAYERS):
        weights = fetch_layer(layer_index, gain_attn, w_qkv, w_proj, gain_ffn, w_in, w_back)
        gathered.append(weights)
        attn_gain, qkv_full, proj_full, ffn_gain, in_full, back_full = weights
        normed = rms_norm(stream, attn_gain.astype(jnp.float32)).astype(jnp.bfloat16)
        projected = jnp.dot(normed, qkv_full, preferred_element_type=jnp.float32)
        queries = projected[:, :D].astype(jnp.bfloat16)
        keys_local = projected[:, D : 2 * D].astype(jnp.bfloat16)
        values_local = projected[:, 2 * D :].astype(jnp.bfloat16)
        keys_full, values_full = (
            lax.all_gather(keys_local, "seq", axis=0, tiled=True),
            lax.all_gather(values_local, "seq", axis=0, tiled=True),
        )
        query_heads = queries.reshape(rows_here, H, E)
        key_heads = keys_full.reshape(-1, H, E)
        value_heads = values_full.reshape(-1, H, E)
        attended, log_total = attend_forward(
            query_heads,
            key_heads,
            value_heads,
            mix_pre[layer_index],
            mix_post[layer_index],
            position,
        )
        attended = attended.astype(jnp.bfloat16)
        middle = stream + jnp.dot(attended, proj_full, preferred_element_type=jnp.float32)
        normed_ffn = rms_norm(middle, ffn_gain.astype(jnp.float32)).astype(jnp.bfloat16)
        hidden_pre = jnp.dot(normed_ffn, in_full, preferred_element_type=jnp.float32)
        activated = jax.nn.gelu(hidden_pre, approximate=True).astype(jnp.bfloat16)
        saved_state.append(
            (
                stream,
                normed,
                query_heads,
                key_heads,
                value_heads,
                keys_local,
                values_local,
                log_total,
                attended,
                middle,
                normed_ffn,
                hidden_pre,
                activated,
            )
        )
        stream = middle + jnp.dot(activated, back_full, preferred_element_type=jnp.float32)
    output = stream.astype(jnp.bfloat16).reshape(token_ids.shape + (D,))
    grad_stream = cotangent.reshape(rows_here, D).astype(jnp.float32)
    layer_grads = [None] * LAYERS
    pre_list = [None] * LAYERS
    post_list = [None] * LAYERS
    for layer_index in reversed(range(LAYERS)):
        weights = fetch_layer(layer_index, gain_attn, w_qkv, w_proj, gain_ffn, w_in, w_back)
        attn_gain, qkv_full, proj_full, ffn_gain, in_full, back_full = weights
        (
            stream_in,
            normed,
            query_heads,
            key_heads,
            value_heads,
            keys_local,
            values_local,
            log_total,
            attended,
            middle,
            normed_ffn,
            hidden_pre,
            activated,
        ) = saved_state[layer_index]
        branch_grad = grad_stream.astype(jnp.bfloat16)
        back_weight_grad = jnp.einsum(
            "tf,td->fd", activated, branch_grad, preferred_element_type=jnp.float32
        )
        act_grad = jnp.einsum(
            "td,fd->tf", branch_grad, back_full, preferred_element_type=jnp.float32
        )
        ignored, gelu_pull = jax.vjp(
            lambda pre_values: jax.nn.gelu(pre_values, approximate=True), hidden_pre
        )
        hidden_grad = gelu_pull(act_grad)[0].astype(jnp.bfloat16)
        in_weight_grad = jnp.einsum(
            "td,tf->df", normed_ffn, hidden_grad, preferred_element_type=jnp.float32
        )
        normed_grad = jnp.einsum(
            "tf,df->td", hidden_grad, in_full, preferred_element_type=jnp.float32
        )
        ignored, norm_pull = jax.vjp(rms_norm, middle, ffn_gain.astype(jnp.float32))
        middle_grad, ffn_gain_grad = norm_pull(normed_grad)
        middle_grad = middle_grad + grad_stream
        attn_branch = middle_grad.astype(jnp.bfloat16)
        proj_weight_grad = jnp.einsum(
            "tc,td->cd", attended, attn_branch, preferred_element_type=jnp.float32
        )
        attended_grad = jnp.einsum(
            "td,cd->tc", attn_branch, proj_full, preferred_element_type=jnp.float32
        ).astype(jnp.bfloat16)
        grad_heads = attended_grad.reshape(rows_here, H, E)
        query_grad, unused_keys, unused_values, pre_grad, post_grad, row_dot = attend_backward(
            query_heads,
            key_heads,
            value_heads,
            mix_pre[layer_index],
            mix_post[layer_index],
            position,
            log_total,
            grad_heads,
        )
        all_queries, all_grads, all_log, all_dot = (
            lax.all_gather(query_heads, "seq", axis=0, tiled=True),
            lax.all_gather(grad_heads, "seq", axis=0, tiled=True),
            lax.all_gather(log_total.astype(jnp.bfloat16), "seq", axis=1, tiled=True).astype(
                log_total.dtype
            ),
            lax.all_gather(row_dot.astype(jnp.bfloat16), "seq", axis=1, tiled=True).astype(
                row_dot.dtype
            ),
        )
        key_sum, value_sum = attend_keys(
            all_queries,
            all_grads,
            all_log,
            all_dot,
            keys_local.reshape(rows_here, H, E),
            values_local.reshape(rows_here, H, E),
            mix_pre[layer_index],
            mix_post[layer_index],
            position,
        )
        qkv_grad = jnp.concatenate(
            [
                query_grad.astype(jnp.bfloat16),
                key_sum.astype(jnp.bfloat16),
                value_sum.astype(jnp.bfloat16),
            ],
            axis=1,
        )
        qkv_weight_grad = jnp.einsum(
            "td,tc->dc", normed, qkv_grad, preferred_element_type=jnp.float32
        )
        normed_attn_grad = jnp.einsum(
            "tc,dc->td", qkv_grad, qkv_full, preferred_element_type=jnp.float32
        )
        ignored, norm_pull = jax.vjp(rms_norm, stream_in, attn_gain.astype(jnp.float32))
        stream_grad, attn_gain_grad = norm_pull(normed_attn_grad)
        grad_stream = middle_grad + stream_grad
        layer_grads[layer_index] = (
            lax.psum_scatter(attn_gain_grad, ("batch", "seq"), scatter_dimension=0, tiled=True),
            lax.psum_scatter(qkv_weight_grad, ("batch", "seq"), scatter_dimension=0, tiled=True),
            lax.psum_scatter(proj_weight_grad, ("batch", "seq"), scatter_dimension=0, tiled=True),
            lax.psum_scatter(ffn_gain_grad, ("batch", "seq"), scatter_dimension=0, tiled=True),
            lax.psum_scatter(in_weight_grad, ("batch", "seq"), scatter_dimension=0, tiled=True),
            lax.psum_scatter(back_weight_grad, ("batch", "seq"), scatter_dimension=0, tiled=True),
        )
        pre_list[layer_index] = pre_grad
        post_list[layer_index] = post_grad
    final_grad = grad_stream.astype(jnp.bfloat16)
    vocab_rows = embedding.shape[0]
    all_tokens = lax.all_gather(token_list, ("batch", "seq"), axis=0, tiled=True)
    own_rows = lax.axis_index(("batch", "seq")) * vocab_rows + jnp.arange(
        vocab_rows, dtype=jnp.int32
    )
    selector = (own_rows[:, None] == all_tokens[None, :]).astype(jnp.bfloat16)
    embedding_grad = jnp.dot(
        selector,
        lax.all_gather(final_grad, ("batch", "seq"), axis=0, tiled=True),
        preferred_element_type=jnp.float32,
    )
    mix_pre_grad, mix_post_grad = lax.psum(
        (jnp.stack(pre_list), jnp.stack(post_list)), ("batch", "seq")
    )
    return (
        output,
        embedding_grad,
        jnp.stack([entry[0] for entry in layer_grads]),
        jnp.stack([entry[1] for entry in layer_grads]),
        jnp.stack([entry[2] for entry in layer_grads]),
        jnp.stack([entry[3] for entry in layer_grads]),
        jnp.stack([entry[4] for entry in layer_grads]),
        jnp.stack([entry[5] for entry in layer_grads]),
        mix_pre_grad,
        mix_post_grad,
    )


def solution(mesh):
    placed = (
        P("batch", "seq"),
        P(("batch", "seq"), None),
        P(None, ("batch", "seq")),
        P(None, ("batch", "seq"), None),
        P(None, ("batch", "seq"), None),
        P(None, ("batch", "seq")),
        P(None, ("batch", "seq"), None),
        P(None, ("batch", "seq"), None),
        P(),
        P(),
        P("batch", "seq", None),
    )
    return jax.shard_map(
        shards,
        mesh=mesh,
        in_specs=placed,
        out_specs=(
            P("batch", "seq", None),
            P(("batch", "seq"), None),
            P(None, ("batch", "seq")),
            P(None, ("batch", "seq"), None),
            P(None, ("batch", "seq"), None),
            P(None, ("batch", "seq")),
            P(None, ("batch", "seq"), None),
            P(None, ("batch", "seq"), None),
            P(),
            P(),
        ),
        check_vma=False,
    )
```

profile of v0, /device:TPU:0, one launch (start us, length us, event | category | flops | bytes accessed | tf_op | source)
XLA Modules:
  0.0 2471.4 jit_solution(15719747095557020487)
XLA Ops:
  12.0 44.2 %all-reduce.9 = (bf16[768]{0:T(1024)(128)(2,1)S(1)}, bf16[768]{0:T(1024)(128)(2,1)S(1)}, bf16[768]{0:T(1024)(128)(2,1)S(1)}, bf16[768]{0:T(1024)(128)(2,1)}) all-reduce(bf16[768]{0:T(1024)(128)(2,1)S(1)} %dynamic-update-slice, bf16[768]{0:T(1024)(128)(2,1)S(1)} %dynamic-update-slice.1, ...), channel_id=2, replica_groups=mesh['batch'=4,'seq'=8] {'batch','seq'}, use_global_device_ids=true, to_apply=%add | all-reduce | flops 3072 | bytes 12288
  56.3 230.2 %all-gather.67.cloned.1.call-done = bf16[32,1004,768]{2,1,0:T(8,128)(2,1)} async-done(((bf16[1,1004,768]{2,1,0:T(8,128)(2,1)}), bf16[32,1004,768]{2,1,0:T(8,128)(2,1)}) %all-gather.67.cloned.1.call-update) | async-done | bytes 49348624 | tf_op jit(solution)/shard_map/all_gather | solution.py:250
  286.4 38.4 %reshape.513 = bf16[32128,768]{1,0:T(8,128)(2,1)} reshape(bf16[32,1004,768]{2,1,0:T(8,128)(2,1)} %all-gather.67.cloned.1.call-done) | data formatting | bytes 98697216
  324.9 18.5 multiply_reduce_fusion.11
  360.0 34.7 %all-gather.33.cloned.1.call-done = bf16[1024,768]{1,0:T(8,128)(2,1)} async-done(((bf16[128,768]{1,0:T(8,128)(2,1)}), bf16[1024,768]{1,0:T(8,128)(2,1)}) %all-gather.33.cloned.1.call-update) | async-done | bytes 1572880 | tf_op jit(solution)/shard_map/all_gather | solution.py:267
  399.1 41.3 %all-gather.35.cloned.1.call-done = bf16[1024,768]{1,0:T(8,128)(2,1)} async-done(((bf16[128,768]{1,0:T(8,128)(2,1)}), bf16[1024,768]{1,0:T(8,128)(2,1)}) %all-gather.35.cloned.1.call-update) | async-done | bytes 1572880 | tf_op jit(solution)/shard_map/all_gather | solution.py:268
  444.8 19.3 while.140
  447.3 14.4 conditional.30
  465.5 24.6 while.141
  468.0 19.8 conditional.31
  498.0 64.1 %all-gather.55.cloned.1.call-done = bf16[1,768,3072]{2,1,0:T(8,128)(2,1)} async-done(((bf16[1,24,3072]{2,1,0:T(8,128)(2,1)}), bf16[1,768,3072]{2,1,0:T(8,128)(2,1)}) %all-gather.55.cloned.1.call-update) | async-done | bytes 4718608 | tf_op jit(solution)/shard_map/all_gather | solution.py:26
  565.4 62.7 %all-gather.57.cloned.1.call-done = bf16[1,3072,768]{2,1,0:T(8,128)(2,1)} async-done(((bf16[1,96,768]{2,1,0:T(8,128)(2,1)}), bf16[1,3072,768]{2,1,0:T(8,128)(2,1)}) %all-gather.57.cloned.1.call-update) | async-done | bytes 4718608 | tf_op jit(solution)/shard_map/all_gather | solution.py:27
  631.6 58.4 %all-gather.59.cloned.1.call-done = bf16[1,768,2304]{2,1,0:T(8,128)(2,1)} async-done(((bf16[1,24,2304]{2,1,0:T(8,128)(2,1)}), bf16[1,768,2304]{2,1,0:T(8,128)(2,1)}) %all-gather.59.cloned.1.call-update) | async-done | bytes 3538960 | tf_op jit(solution)/shard_map/all_gather | solution.py:23
  698.0 38.7 %all-gather.37.cloned.1.call-done = bf16[1024,768]{1,0:T(8,128)(2,1)} async-done(((bf16[128,768]{1,0:T(8,128)(2,1)}), bf16[1024,768]{1,0:T(8,128)(2,1)}) %all-gather.37.cloned.1.call-update) | async-done | bytes 1572880 | tf_op jit(solution)/shard_map/all_gather | solution.py:267
  741.3 18.9 while.142
  760.3 22.1 all-gather.39.cloned.1.call-done
  788.2 25.2 %while.143 = (s32[]{:T(128)}, f32[128,12,64]{0,2,1:T(8,128)}, s32[2]{0:T(128)}, s32[]{:T(128)}, bf16[2,512,12,64]{1,3,2,0:T(8,128)(2,1)}, /*index=5*/bf16[128,12...) while((s32[]{:T(128)}, f32[128,12,64]{0,2,1:T(8,128)}, ...), condition=%wide.region_22.23_spmd.clone, body=%wide.region_19.22_spmd.clone.sunk | while | flops 431129216 | bytes 31541160 | solution.py:99
  791.1 19.8 conditional.33
  814.4 23.9 all-gather.61.cloned.1.call-done
  840.2 63.5 %all-gather.63.cloned.1.call-done = bf16[1,768,3072]{2,1,0:T(8,128)(2,1)} async-done(((bf16[1,24,3072]{2,1,0:T(8,128)(2,1)}), bf16[1,768,3072]{2,1,0:T(8,128)(2,1)}) %all-gather.63.cloned.1.call-update) | async-done | bytes 4718608 | tf_op jit(solution)/shard_map/all_gather | solution.py:26
  906.9 62.7 %all-gather.65.cloned.1.call-done = bf16[1,3072,768]{2,1,0:T(8,128)(2,1)} async-done(((bf16[1,96,768]{2,1,0:T(8,128)(2,1)}), bf16[1,3072,768]{2,1,0:T(8,128)(2,1)}) %all-gather.65.cloned.1.call-update) | async-done | bytes 4718608 | tf_op jit(solution)/shard_map/all_gather | solution.py:27
  980.4 35.3 %all-gather.41.cloned.1.call-done = bf16[1024,12,64]{0,2,1:T(8,128)(2,1)} async-done(((bf16[128,12,64]{0,2,1:T(8,128)(2,1)}), bf16[1024,12,64]{0,2,1:T(8,128)(2,1)}) %all-gather.41.cloned.1.call-update) | async-done | bytes 1572880 | tf_op jit(solution)/shard_map/all_gather | solution.py:366
  1018.5 31.1 %all_gather.112 = bf16[12,1024]{0,1:T(8,128)(2,1)S(1)} all-gather(bf16[12,128]{0,1:T(8,128)(2,1)S(1)} %copy-done.108), channel_id=1, replica_groups=mesh['batch'=4,'seq'=8] {'seq'}, dimensions={1}, use_global_device_ids=true | all-gather | bytes 27648 | tf_op jit(solution)/shard_map/all_gather | solution.py:368
  1050.5 39.7 %while.144 = (s32[]{:T(128)}, f32[12,128]{0,1:T(8,128)S(1)}, f32[12,12]{1,0:T(8,128)S(1)}, s32[2]{0:T(128)}, s32[]{:T(128)}, /*index=5*/bf16[2,512,12,64]{1,3,2,...) while((s32[]{:T(128)}, f32[12,128]{0,1:T(8,128)S(1)}, ...), condition=%wide.region_29.30_spmd.clone, body=%wide.region_25.0_spmd.clone.sunk | while | flops 546636544 | bytes 72205504 | solution.py:143
  1053.1 34.6 %conditional.34 = ((f32[12,128]{0,1:T(8,128)S(1)}, f32[12,12]{1,0:T(8,128)S(1)})) conditional(s32[]{:T(128)} %convert_element_type.366, (f32[12,128]{0,1:T(8,128)S(1)}, f32[12,12]{1,0:T(8,128)S(1)}) %tuple.427, (s32[]{:T(128)}, s32[512]{0:T(512)S(1)}, s32[]{:T(128)}, bf16[2,512,12,64]{1,3,2,0:T(8,128)(2,1)}, s32[]{:T(128)}, ...), branch_computations={%region_26.26_spmd, %region_27.28_spmd} | conditional | flops 546636544 | bytes 72202648 | solution.py:140
  1090.2 64.6 %all_gather.114 = bf16[12,1024]{0,1:T(8,128)(2,1)} all-gather(bf16[12,128]{0,1:T(8,128)(2,1)S(1)} %convert_element_type.265), channel_id=1, replica_groups=mesh['batch'=4,'seq'=8] {'seq'}, dimensions={1}, use_global_device_ids=true | all-gather | bytes 27648 | tf_op jit(solution)/shard_map/all_gather | solution.py:371
  1155.6 58.6 %while.145 = (s32[]{:T(128)}, f32[128,12,64]{0,2,1:T(8,128)}, f32[12,12]{1,0:T(8,128)S(1)}, s32[2]{0:T(128)}, s32[]{:T(128)}, /*index=5*/bf16[2,512,12,64]{1,3,2...) while((s32[]{:T(128)}, f32[128,12,64]{0,2,1:T(8,128)}, ...), condition=%wide.region_33.34_spmd.clone, body=%wide.region_30.0_spmd.clone.sunk | while | flops 759956224 | bytes 77358864 | solution.py:169
  1170.8 40.6 %conditional.35 = ((f32[128,12,64]{0,2,1:T(8,128)}, f32[12,12]{1,0:T(8,128)S(1)})) conditional(s32[]{:T(128)} %convert_element_type.367, (f32[128,12,64]{0,2,1:T(8,128)}, f32[12,12]{1,0:T(8,128)S(1)}) %tuple.430, (s32[]{:T(128)}, s32[512]{0:T(512)S(1)}, s32[]{:T(128)}, bf16[2,512,12,64]{1,3,2,0:T(8,128)(2,1)}, s32[]{:T(128)}, ...), branch_computations={%region_31.31_spmd, %region_32.32_spmd} | conditional | flops 759956224 | bytes 77355992 | solution.py:166
  1220.3 68.2 %while.146 = (s32[]{:T(128)}, f32[128,12,64]{0,2,1:T(8,128)S(1)}, f32[128,12,64]{0,2,1:T(8,128)}, s32[2]{0:T(128)}, s32[]{:T(128)}, /*index=5*/bf16[2,512,12,64]...) while((s32[]{:T(128)}, f32[128,12,64]{0,2,1:T(8,128)S(1)}, ...), condition=%wide.region_37.38_spmd.clone, body=%wide.region_34.37_spmd.clone.sunk | while | flops 863076992 | bytes 45480768 | solution.py:229
  1223.7 30.6 %conditional.36 = ((f32[128,12,64]{0,2,1:T(8,128)S(1)}, f32[128,12,64]{0,2,1:T(8,128)})) conditional(s32[]{:T(128)} %convert_element_type.368, (f32[128,12,64]{0,2,1:T(8,128)S(1)}, f32[128,12,64]{0,2,1:T(8,128)}) %tuple.433, (s32[]{:T(128)}, s32[]{:T(128)}, s32[512]{0:T(512)}, bf16[2,512,12,64]{1,3,2,0:T(8,128)(2,1)S(1)}, s32[]{:T(128)}, ...), branch_computations={%region_35.35_spmd, %region_36.36_spmd} | conditional | flops 863076992 | bytes 45477880 | solution.py:222
  1257.8 30.6 %conditional.36 = ((f32[128,12,64]{0,2,1:T(8,128)S(1)}, f32[128,12,64]{0,2,1:T(8,128)})) conditional(s32[]{:T(128)} %convert_element_type.368, (f32[128,12,64]{0,2,1:T(8,128)S(1)}, f32[128,12,64]{0,2,1:T(8,128)}) %tuple.433, (s32[]{:T(128)}, s32[]{:T(128)}, s32[512]{0:T(512)}, bf16[2,512,12,64]{1,3,2,0:T(8,128)(2,1)S(1)}, s32[]{:T(128)}, ...), branch_computations={%region_35.35_spmd, %region_36.36_spmd} | conditional | flops 863076992 | bytes 45477880 | solution.py:222
  1316.1 41.1 %all_gather.116 = bf16[12,1024]{0,1:T(8,128)(2,1)S(1)} all-gather(bf16[12,128]{0,1:T(8,128)(2,1)S(1)} %copy-done.107), channel_id=1, replica_groups=mesh['batch'=4,'seq'=8] {'seq'}, dimensions={1}, use_global_device_ids=true | all-gather | bytes 27648 | tf_op jit(solution)/shard_map/all_gather | solution.py:368
  1358.1 39.8 %while.147 = (s32[]{:T(128)}, f32[12,128]{0,1:T(8,128)S(1)}, f32[12,12]{1,0:T(8,128)S(1)}, s32[2]{0:T(128)}, s32[]{:T(128)}, /*index=5*/bf16[2,512,12,64]{1,3,2,...) while((s32[]{:T(128)}, f32[12,128]{0,1:T(8,128)S(1)}, ...), condition=%wide.region_44.45_spmd.clone, body=%wide.region_40.44_spmd.clone.sunk | while | flops 546636544 | bytes 72205504 | solution.py:143
  1360.8 34.6 %conditional.37 = ((f32[12,128]{0,1:T(8,128)S(1)}, f32[12,12]{1,0:T(8,128)S(1)})) conditional(s32[]{:T(128)} %convert_element_type.369, (f32[12,128]{0,1:T(8,128)S(1)}, f32[12,12]{1,0:T(8,128)S(1)}) %tuple.436, (s32[]{:T(128)}, s32[512]{0:T(512)S(1)}, s32[]{:T(128)}, bf16[2,512,12,64]{1,3,2,0:T(8,128)(2,1)}, s32[]{:T(128)}, ...), branch_computations={%region_41.41_spmd, %region_42.43_spmd} | conditional | flops 546636544 | bytes 72202648 | solution.py:140
  1398.7 58.8 %while.148 = (s32[]{:T(128)}, f32[128,12,64]{0,2,1:T(8,128)}, f32[12,12]{1,0:T(8,128)S(1)}, s32[2]{0:T(128)}, s32[]{:T(128)}, /*index=5*/bf16[2,512,12,64]{1,3,2...) while((s32[]{:T(128)}, f32[128,12,64]{0,2,1:T(8,128)}, ...), condition=%wide.region_48.49_spmd.clone, body=%wide.region_45.48_spmd.clone.sunk | while | flops 759956224 | bytes 77358864 | solution.py:169
  1414.0 40.6 %conditional.38 = ((f32[128,12,64]{0,2,1:T(8,128)}, f32[12,12]{1,0:T(8,128)S(1)})) conditional(s32[]{:T(128)} %convert_element_type.370, (f32[128,12,64]{0,2,1:T(8,128)}, f32[12,12]{1,0:T(8,128)S(1)}) %tuple.439, (s32[]{:T(128)}, s32[512]{0:T(512)S(1)}, s32[]{:T(128)}, bf16[2,512,12,64]{1,3,2,0:T(8,128)(2,1)}, s32[]{:T(128)}, ...), branch_computations={%region_46.46_spmd, %region_47.47_spmd} | conditional | flops 759956224 | bytes 77355992 | solution.py:166
  1459.4 106.7 %all_gather.118 = bf16[12,1024]{0,1:T(8,128)(2,1)S(1)} all-gather(bf16[12,128]{0,1:T(8,128)(2,1)S(1)} %convert_element_type.277), channel_id=1, replica_groups=mesh['batch'=4,'seq'=8] {'seq'}, dimensions={1}, use_global_device_ids=true | all-gather | bytes 27648 | tf_op jit(solution)/shard_map/all_gather | solution.py:371
  1569.4 68.4 %while.149 = (s32[]{:T(128)}, f32[128,12,64]{0,2,1:T(8,128)S(1)}, f32[128,12,64]{0,2,1:T(8,128)}, s32[2]{0:T(128)}, s32[]{:T(128)}, /*index=5*/bf16[2,512,12,64]...) while((s32[]{:T(128)}, f32[128,12,64]{0,2,1:T(8,128)S(1)}, ...), condition=%wide.region_52.53_spmd.clone, body=%wide.region_49.52_spmd.clone.sunk | while | flops 863076992 | bytes 45480768 | solution.py:229
  1572.8 30.6 %conditional.39 = ((f32[128,12,64]{0,2,1:T(8,128)S(1)}, f32[128,12,64]{0,2,1:T(8,128)})) conditional(s32[]{:T(128)} %convert_element_type.371, (f32[128,12,64]{0,2,1:T(8,128)S(1)}, f32[128,12,64]{0,2,1:T(8,128)}) %tuple.442, (s32[]{:T(128)}, s32[]{:T(128)}, s32[512]{0:T(512)}, bf16[2,512,12,64]{1,3,2,0:T(8,128)(2,1)S(1)}, s32[]{:T(128)}, ...), branch_computations={%region_50.50_spmd, %region_51.51_spmd} | conditional | flops 863076992 | bytes 45477880 | solution.py:222
  1607.0 30.6 %conditional.39 = ((f32[128,12,64]{0,2,1:T(8,128)S(1)}, f32[128,12,64]{0,2,1:T(8,128)})) conditional(s32[]{:T(128)} %convert_element_type.371, (f32[128,12,64]{0,2,1:T(8,128)S(1)}, f32[128,12,64]{0,2,1:T(8,128)}) %tuple.442, (s32[]{:T(128)}, s32[]{:T(128)}, s32[512]{0:T(512)}, bf16[2,512,12,64]{1,3,2,0:T(8,128)(2,1)S(1)}, s32[]{:T(128)}, ...), branch_computations={%region_50.50_spmd, %region_51.51_spmd} | conditional | flops 863076992 | bytes 45477880 | solution.py:222
  1676.1 64.8 %all-gather.12 = s32[1,4096]{1,0:T(1,128)S(1)} all-gather(s32[1,128]{1,0:T(1,128)S(1)} %copy-done.136), channel_id=14, replica_groups=mesh['batch'=4,'seq'=8] {'batch','seq'}, dimensions={1}, use_global_device_ids=true | all-gather | bytes 16896 | tf_op jit(solution)/shard_map/all_gather | solution.py:415
  1745.1 39.7 %all-reduce.8 = (f32[768]{0:T(1024)S(1)}, f32[768]{0:T(1024)S(1)}, f32[768]{0:T(1024)S(1)}, f32[768]{0:T(1024)S(1)}, f32[2,12,12]{2,1,0:T(8,128)S(1)}, /*index=5*/f32[2,12,12]{2,1,0:T(8,128)S(1)}) all-reduce(f32[768]{0:T(1024)S(1)} %copy-done.131, ...), channel_id=16, replica_groups=mesh['batch'=4,'seq'=8] {'batch','seq'}, use_global_device_ids=true, to_apply=%region_57.58.clone | all-reduce | flops 3648 | bytes 29184
  1789.0 29.1 %reduce-scatter.9.cloned.1.call-done = f32[24,2304]{1,0:T(8,128)} async-done(((f32[768,2304]{1,0:T(8,128)}), f32[24,2304]{1,0:T(8,128)}) %reduce-scatter.9.cloned.1.call-update) | async-done | bytes 221200 | tf_op jit(solution)/shard_map/reduce_scatter | solution.py:405
  1819.9 138.9 %reduce-scatter.23.cloned.1.call-done = f32[96,768]{1,0:T(8,128)} async-done(((f32[3072,768]{1,0:T(8,128)}), f32[96,768]{1,0:T(8,128)}) %reduce-scatter.23.cloned.1.call-update) | async-done | bytes 294928 | tf_op jit(solution)/shard_map/reduce_scatter | solution.py:409
  1958.9 141.4 %reduce-scatter.21.cloned.1.call-done = f32[96,768]{1,0:T(8,128)} async-done(((f32[3072,768]{1,0:T(8,128)}), f32[96,768]{1,0:T(8,128)}) %reduce-scatter.21.cloned.1.call-update) | async-done | bytes 294928 | tf_op jit(solution)/shard_map/reduce_scatter | solution.py:409
  2102.2 138.6 %reduce-scatter.19.cloned.1.call-done = f32[24,3072]{1,0:T(8,128)} async-done(((f32[768,3072]{1,0:T(8,128)}), f32[24,3072]{1,0:T(8,128)}) %reduce-scatter.19.cloned.1.call-update) | async-done | bytes 294928 | tf_op jit(solution)/shard_map/reduce_scatter | solution.py:408
  2240.7 141.6 %reduce-scatter.17.cloned.1.call-done = f32[24,3072]{1,0:T(8,128)} async-done(((f32[768,3072]{1,0:T(8,128)}), f32[24,3072]{1,0:T(8,128)}) %reduce-scatter.17.cloned.1.call-update) | async-done | bytes 294928 | tf_op jit(solution)/shard_map/reduce_scatter | solution.py:408
  2384.2 69.3 %all-gather.49.cloned.1.call-done = bf16[4096,768]{1,0:T(8,128)(2,1)} async-done(((bf16[128,768]{1,0:T(8,128)(2,1)}), bf16[4096,768]{1,0:T(8,128)(2,1)}) %all-gather.49.cloned.1.call-update) | async-done | bytes 6291472 | tf_op jit(solution)/shard_map/all_gather | solution.py:422
  (720 shorter events, 570.9 us)
Async XLA Ops:
  7.2 279.3 %all-gather.67.cloned.1.call-start = ((), (), s32[]{:S(2)}) async-start(), calls=%async_computation.33 | async-start | bytes 51093504 | tf_op jit(solution)/shard_map/all_gather | solution.py:250
  7.9 340.4 %all-gather.51.cloned.1.call-start = ((), (), s32[]{:S(2)}) async-start(), calls=%async_computation.25 | async-start | bytes 3649536 | tf_op jit(solution)/shard_map/all_gather | solution.py:23
  9.6 385.1 %all-gather.33.cloned.1.call-start = ((), (), s32[]{:S(2)}) async-start(), calls=%async_computation.8 | async-start | bytes 1769472 | tf_op jit(solution)/shard_map/all_gather | solution.py:267
  56.3 292.1 %copy-start.103 = (f32[768]{0:T(1024)}, f32[768]{0:T(1024)S(1)}, u32[]{:S(2)}) copy-start(f32[768]{0:T(1024)S(1)} %convert_element_type.287) | copy-start | bytes 9220
  56.3 268.6 %copy-start.135 = (s32[1,128]{1,0:T(1,128)S(1)}, s32[1,128]{1,0:T(1,128)}, u32[]{:S(2)}) copy-start(s32[1,128]{1,0:T(1,128)} %param.51) | copy-start | bytes 1540
  351.9 88.5 %all-gather.35.cloned.1.call-start = ((), (), s32[]{:S(2)}) async-start(), calls=%async_computation.9 | async-start | bytes 1769472 | tf_op jit(solution)/shard_map/all_gather | solution.py:268
  352.5 143.7 %all-gather.53.cloned.1.call-start = ((), (), s32[]{:S(2)}) async-start(), calls=%async_computation.26 | async-start | bytes 1216512 | tf_op jit(solution)/shard_map/all_gather | solution.py:24
  353.2 208.9 %all-gather.55.cloned.1.call-start = ((), (), s32[]{:S(2)}) async-start(), calls=%async_computation.27 | async-start | bytes 4866048 | tf_op jit(solution)/shard_map/all_gather | solution.py:26
  354.0 274.1 %all-gather.57.cloned.1.call-start = ((), (), s32[]{:S(2)}) async-start(), calls=%async_computation.28 | async-start | bytes 4866048 | tf_op jit(solution)/shard_map/all_gather | solution.py:27
  354.8 335.2 %all-gather.59.cloned.1.call-start = ((), (), s32[]{:S(2)}) async-start(), calls=%async_computation.29 | async-start | bytes 3649536 | tf_op jit(solution)/shard_map/all_gather | solution.py:23
  355.6 381.1 %all-gather.37.cloned.1.call-start = ((), (), s32[]{:S(2)}) async-start(), calls=%async_computation.10 | async-start | bytes 1769472 | tf_op jit(solution)/shard_map/all_gather | solution.py:267
  465.5 96.6 %copy-start.96 = (f32[768]{0:T(1024)S(1)}, f32[768]{0:T(1024)}, u32[]{:S(2)}) copy-start(f32[768]{0:T(1024)} %convert_element_type.288) | copy-start | bytes 9220
  490.2 75.1 %copy-start.14 = (bf16[128,12,64]{0,2,1:T(8,128)(2,1)}, bf16[128,12,64]{0,2,1:T(8,128)(2,1)S(1)}, u32[]{:S(2)}) copy-start(bf16[128,12,64]{0,2,1:T(8,128)(2,1)S(1)} %get-tuple-element.4547) | copy-start | bytes 589828
  490.2 75.1 %copy-start.19 = (f32[12,128]{0,1:T(8,128)}, f32[12,128]{0,1:T(8,128)S(1)}, u32[]{:S(2)}) copy-start(f32[12,128]{0,1:T(8,128)S(1)} %get-tuple-element.4569) | copy-start | bytes 18436
  490.2 75.1 %copy-start.62 = (f32[12,12]{0,1:T(8,128)}, f32[12,12]{0,1:T(8,128)S(1)}, u32[]{:S(2)}) copy-start(f32[12,12]{0,1:T(8,128)S(1)} %get-tuple-element.4601) | copy-start | bytes 1732
  490.2 75.1 %copy-start.64 = (f32[12,12]{0,1:T(8,128)}, f32[12,12]{0,1:T(8,128)S(1)}, u32[]{:S(2)}) copy-start(f32[12,12]{0,1:T(8,128)S(1)} %get-tuple-element.4603) | copy-start | bytes 1732
  491.3 70.8 %copy-start.70 = (bf16[128,12,64]{0,2,1:T(8,128)(2,1)}, bf16[128,12,64]{0,2,1:T(8,128)(2,1)S(1)}, u32[]{:S(2)}) copy-start(bf16[128,12,64]{0,2,1:T(8,128)(2,1)S(1)} %convert_element_type.245) | copy-start | bytes 589828
  498.0 67.4 %copy-start.133 = (f32[128]{0:T(128)}, f32[128]{0:T(128)S(1)}, u32[]{:S(2)}) copy-start(f32[128]{0:T(128)S(1)} %get-tuple-element.3280) | copy-start | bytes 1540
  498.0 130.1 %copy-start.30 = (f32[128,768]{1,0:T(8,128)}, f32[128,768]{1,0:T(8,128)S(1)}, u32[]{:S(2)}) copy-start(f32[128,768]{1,0:T(8,128)S(1)} %get-tuple-element.3281) | copy-start | bytes 1179652
  498.0 67.3 %copy-start.120 = (f32[128]{0:T(128)}, f32[128]{0:T(128)S(1)}, u32[]{:S(2)}) copy-start(f32[128]{0:T(128)S(1)} %fusion.418) | copy-start | bytes 1540
  565.3 66.2 %copy-start.35 = (f32[128,3072]{1,0:T(8,128)}, f32[128,3072]{1,0:T(8,128)S(1)}, u32[]{:S(2)}) copy-start(f32[128,3072]{1,0:T(8,128)S(1)} %fusion.348) | copy-start | bytes 4718596
  565.3 124.7 %copy-start.105 = (f32[768]{0:T(1024)S(1)}, f32[768]{0:T(1024)}, u32[]{:S(2)}) copy-start(f32[768]{0:T(1024)} %convert_element_type.289) | copy-start | bytes 9220
  693.6 88.8 %all-gather.39.cloned.1.call-start = ((), (), s32[]{:S(2)}) async-start(), calls=%async_computation.11 | async-start | bytes 1769472 | tf_op jit(solution)/shard_map/all_gather | solution.py:268
  694.2 144.2 %all-gather.61.cloned.1.call-start = ((), (), s32[]{:S(2)}) async-start(), calls=%async_computation.30 | async-start | bytes 1216512 | tf_op jit(solution)/shard_map/all_gather | solution.py:24
  694.9 208.8 %all-gather.63.cloned.1.call-start = ((), (), s32[]{:S(2)}) async-start(), calls=%async_computation.31 | async-start | bytes 4866048 | tf_op jit(solution)/shard_map/all_gather | solution.py:26
  695.5 274.2 %all-gather.65.cloned.1.call-start = ((), (), s32[]{:S(2)}) async-start(), calls=%async_computation.32 | async-start | bytes 4866048 | tf_op jit(solution)/shard_map/all_gather | solution.py:27
  696.2 319.5 %all-gather.41.cloned.1.call-start = ((), (), s32[]{:S(2)}) async-start(), calls=%async_computation.12 | async-start | bytes 1769472 | tf_op jit(solution)/shard_map/all_gather | solution.py:366
  697.9 519.9 %all-gather.43.cloned.1.call-start = ((), (), s32[]{:S(2)}) async-start(), calls=%async_computation.13 | async-start | bytes 1769472 | tf_op jit(solution)/shard_map/all_gather | solution.py:367
  788.2 115.5 %copy-start.99 = (f32[768]{0:T(1024)S(1)}, f32[768]{0:T(1024)}, u32[]{:S(2)}) copy-start(f32[768]{0:T(1024)} %convert_element_type.290) | copy-start | bytes 9220
  813.4 93.6 %copy-start.66 = (f32[12,12]{0,1:T(8,128)}, f32[12,12]{0,1:T(8,128)S(1)}, u32[]{:S(2)}) copy-start(f32[12,12]{0,1:T(8,128)S(1)} %get-tuple-element.4604) | copy-start | bytes 1732
  814.4 89.3 %copy-start.72 = (bf16[128,12,64]{0,2,1:T(8,128)(2,1)}, bf16[128,12,64]{0,2,1:T(8,128)(2,1)S(1)}, u32[]{:S(2)}) copy-start(bf16[128,12,64]{0,2,1:T(8,128)(2,1)S(1)} %convert_element_type.252) | copy-start | bytes 589828
  840.1 136.3 %copy-start.33 = (f32[128,768]{1,0:T(8,128)}, f32[128,768]{1,0:T(8,128)S(1)}, u32[]{:S(2)}) copy-start(f32[128,768]{1,0:T(8,128)S(1)} %get-tuple-element.3285) | copy-start | bytes 1179652
  840.2 136.3 %copy-start.123 = (f32[128]{0:T(128)}, f32[128]{0:T(128)S(1)}, u32[]{:S(2)}) copy-start(f32[128]{0:T(128)S(1)} %fusion.420) | copy-start | bytes 1540
  906.9 67.1 %copy-start.38 = (f32[128,3072]{1,0:T(8,128)}, f32[128,3072]{1,0:T(8,128)S(1)}, u32[]{:S(2)}) copy-start(f32[128,3072]{1,0:T(8,128)S(1)} %fusion.340) | copy-start | bytes 4718596
  978.0 335.3 %all-gather.45.cloned.1.call-start = ((), (), s32[]{:S(2)}) async-start(), calls=%async_computation.14 | async-start | bytes 1769472 | tf_op jit(solution)/shard_map/all_gather | solution.py:366
  978.7 588.1 %all-gather.47.cloned.1.call-start = ((), (), s32[]{:S(2)}) async-start(), calls=%async_computation.15 | async-start | bytes 1769472 | tf_op jit(solution)/shard_map/all_gather | solution.py:367
  1302.6 484.8 %reduce-scatter.15.cloned.1.call-start = ((), (), s32[]{:S(2)}) async-start(), calls=%async_computation.20 | async-start | bytes 2433024 | tf_op jit(solution)/shard_map/reduce_scatter | solution.py:406
  1304.5 482.9 %reduce-scatter.13.cloned.1.call-start = ((), (), s32[]{:S(2)}) async-start(), calls=%async_computation.19 | async-start | bytes 2433024 | tf_op jit(solution)/shard_map/reduce_scatter | solution.py:406
  1306.5 482.5 %reduce-scatter.11.cloned.1.call-start = ((), (), s32[]{:S(2)}) async-start(), calls=%async_computation.18 | async-start | bytes 7299072 | tf_op jit(solution)/shard_map/reduce_scatter | solution.py:405
  1310.8 507.3 %reduce-scatter.9.cloned.1.call-start = ((), (), s32[]{:S(2)}) async-start(), calls=%async_computation.17 | async-start | bytes 7299072 | tf_op jit(solution)/shard_map/reduce_scatter | solution.py:405
  1457.5 111.0 %copy-start.92 = (f32[12,12]{1,0:T(8,128)}, f32[12,12]{1,0:T(8,128)S(1)}, u32[]{:S(2)}) copy-start(f32[12,12]{1,0:T(8,128)S(1)} %get-tuple-element.2156) | copy-start | bytes 1732
  1457.5 111.9 %copy-start.17 = (bf16[12,8,2,8,512]{4,3,1,0,2:T(8,128)(2,1)S(1)}, bf16[12,8,2,8,512]{4,3,1,0,2:T(8,128)(2,1)}, u32[]{:S(2)}) copy-start(bf16[12,8,2,8,512]{4,3,1,0,2:T(8,128)(2,1)} %copy.388) | copy-start | bytes 4718596
  1457.5 111.8 %copy-start.63 = (f32[12,12]{0,1:T(8,128)S(1)}, f32[12,12]{0,1:T(8,128)}, u32[]{:S(2)}) copy-start(f32[12,12]{0,1:T(8,128)} %copy-done.62) | copy-start | bytes 1732
  1644.7 314.2 %reduce-scatter.23.cloned.1.call-start = ((), (), s32[]{:S(2)}) async-start(), calls=%async_computation.24 | async-start | bytes 9732096 | tf_op jit(solution)/shard_map/reduce_scatter | solution.py:409
  1651.3 449.0 %reduce-scatter.21.cloned.1.call-start = ((), (), s32[]{:S(2)}) async-start(), calls=%async_computation.23 | async-start | bytes 9732096 | tf_op jit(solution)/shard_map/reduce_scatter | solution.py:409
  1657.9 582.8 %reduce-scatter.19.cloned.1.call-start = ((), (), s32[]{:S(2)}) async-start(), calls=%async_computation.22 | async-start | bytes 9732096 | tf_op jit(solution)/shard_map/reduce_scatter | solution.py:408
  1664.3 718.1 %reduce-scatter.17.cloned.1.call-start = ((), (), s32[]{:S(2)}) async-start(), calls=%async_computation.21 | async-start | bytes 9732096 | tf_op jit(solution)/shard_map/reduce_scatter | solution.py:408
  1670.6 782.9 %all-gather.49.cloned.1.call-start = ((), (), s32[]{:S(2)}) async-start(), calls=%async_computation.16 | async-start | bytes 6488064 | tf_op jit(solution)/shard_map/all_gather | solution.py:422
  (137 other events, 1164.3 us)
Sparse Core Ops, SparseCore 0:
  10.9 275.4 all-gather.66
  289.9 58.3 all-gather.50
  352.0 42.6 all-gather.32
  397.3 42.9 all-gather.34
  443.1 52.9 all-gather.52
  499.5 62.5 all-gather.54
  565.6 62.4 all-gather.56
  631.0 58.9 all-gather.58
  693.7 42.9 all-gather.36
  739.3 43.0 all-gather.38
  785.3 52.9 all-gather.60
  841.1 62.5 all-gather.62
  907.2 62.4 all-gather.64
  971.6 44.1 all-gather.40
  1017.6 43.9 all-gather.42
  1063.5 43.6 all-gather.44
  1302.7 58.0 all-gather.46
  1366.5 97.2 reduce-scatter.14
  1470.0 98.5 reduce-scatter.12
  1574.1 118.2 reduce-scatter.10
  1698.9 119.1 reduce-scatter.8
  1824.0 134.8 reduce-scatter.22
  1965.8 134.4 reduce-scatter.20
  2106.0 134.6 reduce-scatter.18
  2247.6 134.6 reduce-scatter.16
  2385.1 68.4 all-gather.48
where the time goes:
time: 2480 us; the launch traced here: 2470 us
  waiting for transfers between devices  1410 us (57%)
  blocking collectives  392 us (16%)
  matrix products  391 us (16%)
  local copies, waits for them, and re-layouts  169 us (7%)
  loops' own time  53.2 us (2%)
  other arithmetic  37.3 us (2%)
    reduce_scatter x2, waiting for transfers between devices, shards(): lax.psum_scatter(back_weight_grad, ('batch', 'seq'), scatter_dimension=0,...  280 us
    reduce_scatter x2, waiting for transfers between devices, shards(): lax.psum_scatter(in_weight_grad, ('batch', 'seq'), scatter_dimension=0, t...  280 us
    all_gather x1, waiting for transfers between devices, shards(): shard_rows = lax.all_gather(embedding, ('batch', 'seq'), axis=0, tiled=True)  230 us
    all_gather x2, blocking collectives, shards(): lax.all_gather(row_dot.astype(jnp.bfloat16), 'seq', axis=1, tiled=True)  171 us
    all_gather x2, waiting for transfers between devices, fetch_layer(): lax.all_gather(w_in[layer_index], ('batch', 'seq'), axis=0, tiled=True)  128 us
    all_gather x2, waiting for transfers between devices, fetch_layer(): lax.all_gather(w_back[layer_index], ('batch', 'seq'), axis=0, tiled=True)  125 us
    dot_general x12, matrix products, block_logits(): logits = jnp.einsum('htk,hg->gtk', scores, mixing_pre, precision=HIGHEST)  86 us
    unnamed x2, blocking collectives  83.9 us
  transfers between devices with their start and end apart: 26, of which 20 were waited for; matrix products, arithmetic and copies ran while one was open for 23% of the time, Pallas kernels for 0%

commit v1 on v0

v1 whole, which is shorter than its diff:
```python
import functools

import jax
import jax.numpy as jnp
from jax import lax
from jax.experimental import pallas as pl
from jax.experimental.pallas import tpu as pltpu
from jax.sharding import PartitionSpec as P

D = 768
H = 12
E = 64
LAYERS = 2
AXES = ("batch", "seq")
NEGATIVE = -1e30
CHUNK = 256
F32 = jnp.float32
BF16 = jnp.bfloat16


class Geometry:
    def __init__(self, mesh):
        self.b = mesh.shape["batch"]
        self.n = mesh.shape["seq"]
        self.r = self.n // self.b
        self.count = self.b * self.n
        self.core = self.n
        low = list(range(self.r))
        high = [k * self.n for k in range(0, self.b, 2)]
        self.plane = [h + l for h in high for l in low]
        self.zs = [k * self.r for k in range(self.b)]
        self.order = [c + p + z for c in (0, self.core) for p in self.plane for z in self.zs]

    def rank_mask(self, mask):
        return (mask // self.n) * self.r + mask % self.n

    def device(self, sequence, rank):
        return (rank // self.r) * self.n + sequence * self.r + rank % self.r


def swap(value, mask, count):
    return lax.ppermute(value, AXES, [(p, p ^ mask) for p in range(count)])


def dot(a, b, contract):
    return lax.dot_general(a, b, (contract, ((), ())), preferred_element_type=F32)


def load_keys(masks, half, rank, pieces, kv, sems):
    n = len(masks)
    copies = []
    for index, mask in enumerate(masks):
        owner = rank ^ mask
        for part, place in ((0, owner), (1, 2 * n - 1 - owner)):
            start = pl.multiple_of(place * half, half)
            copies.append(
                pltpu.make_async_copy(
                    pieces[index].at[pl.ds(part * half, half)],
                    kv.at[pl.ds(start, half)],
                    sems.at[2 * index + part],
                )
            )
    for copy in copies:
        copy.start()
    return copies


def mixed_rows(rows, weights):
    return jnp.concatenate([rows * weights[g : g + 1, :] for g in range(H)], axis=0)


def forward_kernel(masks, half, rank_ref, q_ref, pre_ref, post_ref, *rest):
    n = len(masks)
    pieces = rest[:n]
    o_ref, lse_ref, pv_ref = rest[n : n + 3]
    kv, qg, logits, top, total, acc, sems = rest[n + 3 :]
    rank = rank_ref[0]
    rows = H * half
    copies = load_keys(masks, half, rank, pieces, kv, sems)
    for copy in copies:
        copy.wait()
    for part in range(2):
        place = rank if part == 0 else 2 * n - 1 - rank
        live = (place * half + half + CHUNK - 1) // CHUNK
        q_part = q_ref[part * half : (part + 1) * half, :].astype(F32)
        qg[...] = mixed_rows(q_part, pre_ref[...]).astype(BF16)
        top[...] = jnp.full((rows, 128), NEGATIVE, F32)
        total[...] = jnp.zeros((rows, 128), F32)
        acc[...] = jnp.zeros((rows, D), F32)
        spot = place * half + lax.broadcasted_iota(jnp.int32, (rows, CHUNK), 0) % half
        lane = lax.broadcasted_iota(jnp.int32, (rows, CHUNK), 1)

        def score(c, carry):
            start = pl.multiple_of(c * CHUNK, CHUNK)
            found = dot(qg[...], kv[pl.ds(start, CHUNK), :D], ((1,), (1,)))
            found = jnp.where(start + lane <= spot, found, NEGATIVE)
            logits[c] = found
            best = found[:, :128]
            for k in range(1, CHUNK // 128):
                best = jnp.maximum(best, found[:, k * 128 : (k + 1) * 128])
            top[...] = jnp.maximum(top[...], best)
            return carry

        lax.fori_loop(0, live, score, 0)
        row_max = jnp.max(top[...], axis=1, keepdims=True)

        def weigh(c, carry):
            start = pl.multiple_of(c * CHUNK, CHUNK)
            prob = jnp.exp(logits[c] - row_max)
            part_sum = prob[:, :128]
            for k in range(1, CHUNK // 128):
                part_sum = part_sum + prob[:, k * 128 : (k + 1) * 128]
            total[...] += part_sum
            acc[...] += dot(prob.astype(BF16), kv[pl.ds(start, CHUNK), D:], ((1,), (0,)))
            return carry

        lax.fori_loop(0, live, weigh, 0)
        row_sum = jnp.sum(total[...], axis=1, keepdims=True)
        scale = 1.0 / row_sum
        lse = jnp.broadcast_to(row_max + jnp.log(row_sum), (rows, 128))
        lse_ref[part] = jnp.transpose(lse)[:8, :]
        out = jnp.zeros((half, D), F32)
        for g in range(H):
            normal = acc[g * half : (g + 1) * half, :] * scale[g * half : (g + 1) * half, :]
            pv_ref[part, g * half : (g + 1) * half, :] = normal.astype(BF16)
            out = out + normal * post_ref[g : g + 1, :]
        o_ref[part * half : (part + 1) * half, :] = out.astype(BF16)


def backward_kernel(masks, half, rank_ref, q_ref, go_ref, lse_ref, pv_ref, pre_ref, post_ref, *rest):
    n = len(masks)
    pieces = rest[:n]
    gq_ref, pre_grad_ref, post_grad_ref = rest[n : n + 3]
    grads = rest[n + 3 : 2 * n + 3]
    kv, qg, gg, gk, gv, acc, sems, out_sems = rest[2 * n + 3 :]
    rank = rank_ref[0]
    rows = H * half
    copies = load_keys(masks, half, rank, pieces, kv, sems)
    gk[...] = jnp.zeros(gk.shape, F32)
    gv[...] = jnp.zeros(gv.shape, F32)
    pre_grad_ref[...] = jnp.zeros(pre_grad_ref.shape, F32)
    post_grad_ref[...] = jnp.zeros(post_grad_ref.shape, F32)
    for copy in copies:
        copy.wait()
    for part in range(2):
        place = rank if part == 0 else 2 * n - 1 - rank
        live = (place * half + half + CHUNK - 1) // CHUNK
        q_part = q_ref[part * half : (part + 1) * half, :].astype(F32)
        go_part = go_ref[part * half : (part + 1) * half, :].astype(F32)
        row_dots = []
        for g in range(H):
            qg[g * half : (g + 1) * half, :] = (q_part * pre_ref[g : g + 1, :]).astype(BF16)
            mixed = go_part * post_ref[g : g + 1, :]
            gg[g * half : (g + 1) * half, :] = mixed.astype(BF16)
            normal = pv_ref[part, g * half : (g + 1) * half, :].astype(F32)
            row_dots.append(jnp.sum(mixed * normal, axis=1, keepdims=True))
            post_grad_ref[g : g + 1, :] += jnp.sum(go_part * normal, axis=0, keepdims=True)
        row_dot = jnp.broadcast_to(jnp.concatenate(row_dots, axis=0), (rows, 128))
        row_dot = jnp.transpose(row_dot)[:1, :]
        lse = lse_ref[part][:1, :]
        acc[...] = jnp.zeros((rows, D), F32)
        spot = place * half + lax.broadcasted_iota(jnp.int32, (CHUNK, rows), 1) % half
        line = lax.broadcasted_iota(jnp.int32, (CHUNK, rows), 0)

        def block(c, carry):
            start = pl.multiple_of(c * CHUNK, CHUNK)
            keys = kv[pl.ds(start, CHUNK), :D]
            values = kv[pl.ds(start, CHUNK), D:]
            found = dot(keys, qg[...], ((1,), (1,)))
            found = jnp.where(start + line <= spot, found, NEGATIVE)
            prob = jnp.exp(found - lse)
            grad_prob = dot(values, gg[...], ((1,), (1,)))
            grad_logit = (prob * (grad_prob - row_dot)).astype(BF16)
            gv[pl.ds(start, CHUNK), :] += dot(prob.astype(BF16), gg[...], ((1,), (0,)))
            gk[pl.ds(start, CHUNK), :] += dot(grad_logit, qg[...], ((1,), (0,)))
            acc[...] += dot(grad_logit, keys, ((0,), (0,)))
            return carry

        lax.fori_loop(0, live, block, 0)
        gq = jnp.zeros((half, D), F32)
        for g in range(H):
            found = acc[g * half : (g + 1) * half, :]
            gq = gq + found * pre_ref[g : g + 1, :]
            pre_grad_ref[g : g + 1, :] += jnp.sum(found * q_part, axis=0, keepdims=True)
        gq_ref[part * half : (part + 1) * half, :] = gq.astype(BF16)
    kv[:, :D] = gk[...].astype(BF16)
    kv[:, D:] = gv[...].astype(BF16)
    copies = []
    for index, mask in enumerate(masks):
        owner = rank ^ mask
        for part, place in ((0, owner), (1, 2 * n - 1 - owner)):
            start = pl.multiple_of(place * half, half)
            copies.append(
                pltpu.make_async_copy(
                    kv.at[pl.ds(start, half)],
                    grads[index].at[pl.ds(part * half, half)],
                    out_sems.at[2 * index + part],
                )
            )
    for copy in copies:
        copy.start()
    for copy in copies:
        copy.wait()


VMEM = pl.BlockSpec(memory_space=pltpu.VMEM)
SMEM = pl.BlockSpec(memory_space=pltpu.SMEM)
ANY = pl.BlockSpec(memory_space=pl.ANY)
LIMIT = pltpu.CompilerParams(vmem_limit_bytes=58 * 2**20)


def attend(masks, rank, queries, pieces, pre, post):
    n = len(masks)
    tokens = queries.shape[0]
    half = tokens // 2
    rows = H * half
    length = n * tokens
    return pl.pallas_call(
        functools.partial(forward_kernel, masks, half),
        out_shape=(
            jax.ShapeDtypeStruct((tokens, D), BF16),
            jax.ShapeDtypeStruct((2, 8, rows), F32),
            jax.ShapeDtypeStruct((2, rows, D), BF16),
        ),
        in_specs=[SMEM, VMEM, VMEM, VMEM] + [ANY] * n,
        out_specs=(VMEM, VMEM, VMEM),
        scratch_shapes=[
            pltpu.VMEM((length, 2 * D), BF16),
            pltpu.VMEM((rows, D), BF16),
            pltpu.VMEM((length // CHUNK, rows, CHUNK), F32),
            pltpu.VMEM((rows, 128), F32),
            pltpu.VMEM((rows, 128), F32),
            pltpu.VMEM((rows, D), F32),
            pltpu.SemaphoreType.DMA((2 * n,)),
        ],
        compiler_params=LIMIT,
        name="attend",
    )(rank, queries, pre, post, *pieces)


def attend_back(masks, rank, queries, grad_out, lse, pv, pieces, pre, post):
    n = len(masks)
    tokens = queries.shape[0]
    half = tokens // 2
    rows = H * half
    length = n * tokens
    outs = pl.pallas_call(
        functools.partial(backward_kernel, masks, half),
        out_shape=(
            jax.ShapeDtypeStruct((tokens, D), BF16),
            jax.ShapeDtypeStruct((H, D), F32),
            jax.ShapeDtypeStruct((H, D), F32),
        )
        + tuple(jax.ShapeDtypeStruct((tokens, 2 * D), BF16) for _ in masks),
        in_specs=[SMEM] + [VMEM] * 6 + [ANY] * n,
        out_specs=(VMEM, VMEM, VMEM) + (ANY,) * n,
        scratch_shapes=[
            pltpu.VMEM((length, 2 * D), BF16),
            pltpu.VMEM((rows, D), BF16),
            pltpu.VMEM((rows, D), BF16),
            pltpu.VMEM((length, D), F32),
            pltpu.VMEM((length, D), F32),
            pltpu.VMEM((rows, D), F32),
            pltpu.SemaphoreType.DMA((2 * n,)),
            pltpu.SemaphoreType.DMA((2 * n,)),
        ],
        compiler_params=LIMIT,
        name="attend_back",
    )(rank, queries, grad_out, lse, pv, pre, post, *pieces)
    return outs[0], outs[1], outs[2], outs[3:]


def mm(a, b):
    return jnp.dot(a, b, preferred_element_type=F32)


def mm_t(a, b):
    return lax.dot_general(a, b, (((1,), (1,)), ((), ())), preferred_element_type=F32)


def t_mm(a, b):
    return lax.dot_general(a, b, (((0,), (0,)), ((), ())), preferred_element_type=F32)


def norm_parts(x):
    return lax.rsqrt(jnp.mean(x * x, axis=-1, keepdims=True) + 1e-06)


def norm_back(x, gain, grad):
    r = norm_parts(x)
    gain_grad = jnp.sum(grad * x * r, axis=0)
    scaled = grad * gain
    x_grad = r * scaled - x * (r * r * r) * jnp.mean(scaled * x, axis=-1, keepdims=True)
    return x_grad, gain_grad


def shards(
    geo,
    token_ids,
    embedding,
    gain_attn,
    w_qkv,
    w_proj,
    gain_ffn,
    w_in,
    w_back,
    mix_pre,
    mix_post,
    cotangent,
):
    n, r, count, core = geo.n, geo.r, geo.count, geo.core
    tokens = token_ids.size
    half = tokens // 2
    i = lax.axis_index("batch")
    j = lax.axis_index("seq")
    me = i * n + j
    rank = i * r + j % r
    rank_arg = rank.reshape(1).astype(jnp.int32)
    share = w_qkv.shape[1]
    back_share = w_back.shape[1]
    folds = back_share // share
    ff = w_in.shape[2]
    sw = functools.partial(swap, count=count)

    columns = []
    for l in range(LAYERS):
        inward = w_in[l].reshape(share, count, folds, share).transpose(0, 2, 1, 3).reshape(share, ff)
        outward = w_back[l].reshape(folds, share, D).transpose(1, 0, 2).reshape(share, folds * D)
        columns += [w_qkv[l], w_proj[l], inward, outward]
    gains = jnp.stack([gain_attn[0], gain_ffn[0], gain_attn[1], gain_ffn[1]], axis=1)
    columns.append(jnp.pad(gains, ((0, 0), (0, 124))))
    weights = lax.all_gather(jnp.concatenate(columns, axis=1), AXES, axis=0, tiled=True)
    width = 4 * D + 2 * ff

    def layer_weights(l):
        w = weights[:, l * width : (l + 1) * width]
        outward = w[:, 4 * D + ff :].reshape(D, folds, D).transpose(1, 0, 2).reshape(ff, D)
        gain = weights[:, LAYERS * width + 2 * l : LAYERS * width + 2 * l + 2].astype(F32)
        return w[:, : 3 * D], w[:, 3 * D : 4 * D], w[:, 4 * D : 4 * D + ff], outward, gain[:, 0], gain[:, 1]

    ids = token_ids.reshape(1, tokens)
    ids = jnp.concatenate([ids] + [sw(ids, m) for m in range(1, n)], axis=0)
    ids = jnp.concatenate([ids] + [sw(ids, m * n) for m in range(1, geo.b)], axis=0)
    target = me ^ jnp.array(geo.order, jnp.int32)
    t_seq = (target % n) // r
    t_rank = (target // n) * r + target % r
    halves = jnp.stack([t_rank, 2 * n - 1 - t_rank], axis=1)
    source = (t_seq[:, None] * n + halves // 2) ^ me
    ids = jnp.take(ids.reshape(2 * count, half), (source * 2 + halves % 2).reshape(-1), axis=0).reshape(-1)

    vocab = embedding.shape[0]
    table = jnp.concatenate([embedding, sw(embedding, core)], axis=0)
    line = jnp.arange(vocab, dtype=jnp.int32)
    names = jnp.concatenate([me * vocab + line, (me ^ core) * vocab + line])
    near = ids[: ids.shape[0] // 2]
    picked = mm((near[:, None] == names[None, :]).astype(BF16), table).astype(BF16)
    picked = picked.reshape(len(geo.plane), -1, D)
    row = picked[0]
    for k in range(1, len(geo.plane)):
        row = row + sw(picked[k], geo.plane[k])
    row = row.reshape(len(geo.zs), tokens, D)
    stream = row[0]
    for k in range(1, len(geo.zs)):
        stream = stream + sw(row[k], geo.zs[k])
    stream = stream.astype(F32)

    def half_moves(parity):
        moves = []
        for b in range(geo.b):
            for block in range(n):
                h = 2 * block + parity
                to = geo.device(b, h if h < n else 2 * n - 1 - h)
                moves.append((b * n + block, to))
        return moves

    flat = cotangent.reshape(tokens, D)
    evens = lax.ppermute(flat[:half], AXES, half_moves(0))
    odds = lax.ppermute(flat[half:], AXES, half_moves(1))
    even_rank = rank % 2 == 0
    grad_stream = jnp.where(
        even_rank, jnp.concatenate([evens, odds], axis=0), jnp.concatenate([odds, evens], axis=0)
    ).astype(F32)

    near_masks = list(geo.plane)
    masks = [geo.rank_mask(m) for m in near_masks] + [geo.rank_mask(m ^ core) for m in near_masks]
    spread_pre = [jnp.repeat(mix_pre[l].T, E, axis=1) * E ** (-0.5) for l in range(LAYERS)]
    spread_post = [jnp.repeat(mix_post[l], E, axis=1) for l in range(LAYERS)]

    saved = []
    for l in range(LAYERS):
        qkv, proj, inward, outward, gain_a, gain_f = layer_weights(l)
        n1 = (stream * norm_parts(stream) * gain_a).astype(BF16)
        projected = mm(n1, qkv).astype(BF16)
        queries = projected[:, :D]
        own = projected[:, D:]
        pieces = [own] + [sw(own, m) for m in near_masks[1:]]
        pieces = pieces + [sw(piece, core) for piece in pieces]
        attended, lse, pv = attend(masks, rank_arg, queries, pieces, spread_pre[l], spread_post[l])
        middle = stream + mm(attended, proj)
        n2 = (middle * norm_parts(middle) * gain_f).astype(BF16)
        hidden = mm(n2, inward)
        active = jax.nn.gelu(hidden, approximate=True).astype(BF16)
        saved.append((stream, n1, queries, pieces, attended, lse, pv, middle, n2, hidden, active))
        stream = middle + mm(active, outward)

    final = stream.astype(BF16)
    back_even = [(b, a) for a, b in half_moves(0)]
    back_odd = [(b, a) for a, b in half_moves(1)]
    first = jnp.where(even_rank, final[:half], final[half:])
    second = jnp.where(even_rank, final[half:], final[:half])
    output = jnp.concatenate(
        [lax.ppermute(first, AXES, back_even), lax.ppermute(second, AXES, back_odd)], axis=0
    ).reshape(cotangent.shape)

    shares = [None] * LAYERS
    mixes = [None] * LAYERS
    for l in reversed(range(LAYERS)):
        qkv, proj, inward, outward, gain_a, gain_f = layer_weights(l)
        stream_in, n1, queries, pieces, attended, lse, pv, middle, n2, hidden, active = saved[l]
        gf = grad_stream.astype(BF16)
        back_grad = t_mm(active, gf)
        pull = jax.vjp(lambda z: jax.nn.gelu(z, approximate=True), hidden)[1]
        gz = pull(mm_t(gf, outward))[0].astype(BF16)
        in_grad = t_mm(n2, gz)
        delta, gain_f_grad = norm_back(middle, gain_f, mm_t(gz, inward))
        middle_grad = grad_stream + delta
        gy = middle_grad.astype(BF16)
        proj_grad = t_mm(attended, gy)
        go = mm_t(gy, proj).astype(BF16)
        gq, pre_grad, post_grad, parts = attend_back(
            masks, rank_arg, queries, go, lse, pv, pieces, spread_pre[l], spread_post[l]
        )
        mixes[l] = (pre_grad, post_grad)
        size = len(near_masks)
        sums = [parts[k].astype(F32) + sw(parts[size + k], core).astype(F32) for k in range(size)]
        kv_grad = sums[0]
        for k in range(1, size):
            kv_grad = kv_grad + sw(sums[k].astype(BF16), near_masks[k]).astype(F32)
        joint = jnp.concatenate([gq, kv_grad.astype(BF16)], axis=1)
        qkv_grad = t_mm(n1, joint)
        delta, gain_a_grad = norm_back(stream_in, gain_a, mm_t(joint, qkv))
        grad_stream = middle_grad + delta
        back_cols = back_grad.reshape(folds, D, D)
        gain_cols = jnp.pad(jnp.stack([gain_a_grad, gain_f_grad], axis=1), ((0, 0), (0, 126)))
        packed = jnp.concatenate(
            [qkv_grad.astype(BF16), proj_grad.astype(BF16), in_grad.astype(BF16)]
            + [back_cols[a].astype(BF16) for a in range(folds)]
            + [gain_cols.astype(BF16)],
            axis=1,
        )
        shares[l] = lax.psum_scatter(packed, AXES, scatter_dimension=0, tiled=True).astype(F32)

    g0 = grad_stream.astype(BF16)
    rows = jnp.concatenate([g0] + [sw(g0, m) for m in geo.zs[1:]], axis=0)
    blocks = [rows] + [sw(rows, m) for m in geo.plane[1:]]
    blocks = blocks + [sw(block, core) for block in blocks]
    own_names = me * vocab + line
    embedding_grad = mm(
        (own_names[:, None] == ids[None, :]).astype(BF16), jnp.concatenate(blocks, axis=0)
    )

    pre_sum = jnp.stack([mixes[l][0] for l in range(LAYERS)]).reshape(LAYERS, H, H, E).sum(-1)
    post_sum = jnp.stack([mixes[l][1] for l in range(LAYERS)]).reshape(LAYERS, H, H, E).sum(-1)
    mix = jnp.stack([pre_sum.transpose(0, 2, 1) * E ** (-0.5), post_sum])
    bit = 1
    while bit < count:
        mix = mix + sw(mix, bit)
        bit *= 2

    def in_order(packed):
        part = packed[:, 4 * D : 4 * D + ff]
        return part.reshape(share, folds, count, share).transpose(0, 2, 1, 3).reshape(share, ff)

    def back_order(packed):
        part = packed[:, 4 * D + ff : width]
        return part.reshape(share, folds, D).transpose(1, 0, 2).reshape(back_share, D)

    return (
        output,
        embedding_grad,
        jnp.stack([s[:, width] for s in shares]),
        jnp.stack([s[:, : 3 * D] for s in shares]),
        jnp.stack([s[:, 3 * D : 4 * D] for s in shares]),
        jnp.stack([s[:, width + 1] for s in shares]),
        jnp.stack([in_order(s) for s in shares]),
        jnp.stack([back_order(s) for s in shares]),
        mix[0],
        mix[1],
    )


def solution(mesh):
    everywhere = ("batch", "seq")
    weight = P(None, everywhere, None)
    vector = P(None, everywhere)
    return jax.shard_map(
        functools.partial(shards, Geometry(mesh)),
        mesh=mesh,
        in_specs=(
            P("batch", "seq"),
            P(everywhere, None),
            vector,
            weight,
            weight,
            vector,
            weight,
            weight,
            P(),
            P(),
            P("batch", "seq", None),
        ),
        out_specs=(
            P("batch", "seq", None),
            P(everywhere, None),
            vector,
            weight,
            weight,
            vector,
            weight,
            weight,
            P(),
            P(),
        ),
        check_vma=False,
    )
```

time: 2480 us -> 820 us (0.33)
  waiting for transfers between devices: 1410 us -> 450 us
  blocking collectives: 392 us -> 0 us
  matrix products: 391 us -> 97.8 us
  local copies, waits for them, and re-layouts: 169 us -> 92.6 us
  starting transfers between devices: 1.58 us -> 64.9 us
  Pallas kernels: 0 us -> 60.9 us
  loops' own time: 53.2 us -> 0 us
    all_gather x18 -> x1, waiting for transfers between devices: 817 us -> 74.1 us  [shards(): lax.all_gather(jnp.concatenate(columns, axis=1), AXES, axis=0, tiled=True)]
    reduce_scatter x8 -> x0, waiting for transfers between devices: 590 us -> none  [the longest x2 280 us: shards(): lax.psum_scatter(back_weight_grad, ('batch', 'seq'), scatter_dimension=0,...]
    all_gather x5 -> x0, blocking collectives: 308 us -> none  [the longest x2 171 us: shards(): lax.all_gather(row_dot.astype(jnp.bfloat16), 'seq', axis=1, tiled=True)]
    dot_general x94 -> x26, matrix products: 391 us -> 97.8 us  [the longest x10 41.3 us: mm(): return jnp.dot(a, b, preferred_element_type=F32)]
    ppermute x0 -> x64, waiting for transfers between devices: none -> 204 us  [the longest x60 178 us: swap(): return lax.ppermute(value, AXES, [(p, p ^ mask) for p in range(count)])]
    unnamed x26 -> x5, waiting for transfers between devices: 4.64 us -> 172 us
    unnamed x2 -> x0, blocking collectives: 83.9 us -> none
    ppermute x0 -> x64, starting transfers between devices: none -> 64.1 us  [the longest x60 55.9 us: swap(): return lax.ppermute(value, AXES, [(p, p ^ mask) for p in range(count)])]
  transfers between devices with their start and end apart: 26 -> 67, of which waited for: 20 -> 28; matrix products, arithmetic and copies ran while one was open for 23% -> 18% of each run, Pallas kernels for 0% -> 4%
where the time goes in v1:
time: 820 us; the launch traced here: 814 us
  waiting for transfers between devices  450 us (55%)
  matrix products  97.8 us (12%)
  local copies, waits for them, and re-layouts  92.6 us (11%)
  starting transfers between devices  64.9 us (8%)
  Pallas kernels  60.9 us (7%)
  other arithmetic  31.5 us (4%)
  between operations  15.4 us (2%)
    ppermute x60, waiting for transfers between devices, swap(): return lax.ppermute(value, AXES, [(p, p ^ mask) for p in range(count)])  178 us
    unnamed x5, waiting for transfers between devices  172 us
    all_gather x1, waiting for transfers between devices, shards(): lax.all_gather(jnp.concatenate(columns, axis=1), AXES, axis=0, tiled=True)  74.1 us
    ppermute x60, starting transfers between devices, swap(): return lax.ppermute(value, AXES, [(p, p ^ mask) for p in range(count)])  55.9 us
    dot_general x10, matrix products, mm(): return jnp.dot(a, b, preferred_element_type=F32)  41.3 us
    pallas_call x2, Pallas kernels, attend_back(): pl.pallas_call(functools.partial(backward_kernel, masks, half), out_shape...  37.3 us
    dot_general x8, matrix products, mm_t(): lax.dot_general(a, b, (((1,), (1,)), ((), ())), preferred_element_type=F32)  30.1 us
    unnamed x197, local copies, waits for them, and re-layouts  30 us
  transfers between devices with their start and end apart: 67, of which 28 were waited for; matrix products, arithmetic and copies ran while one was open for 18% of the time, Pallas kernels for 4%

profile of v1, /device:TPU:0, one launch (start us, length us, event | category | flops | bytes accessed | tf_op | source)
XLA Modules:
  0.0 813.5 jit_solution(8196800097510603537)
XLA Ops:
  17.3 6.1 collective-permute-start.6
  39.3 9.3 %fusion.20 = bf16[2048,768]{1,0:T(8,128)(2,1)S(1)} fusion(s32[2008]{0:T(1024)S(1)} %pad_add_fusion, s32[2048]{0:T(1024)S(1)} %eq.40, bf16[1004,768]{1,0:T(8,128)(2,1)} %collective-permute-done.10, bf16[1004,768]{1,0:T(8,128)(2,1)} %param.13), kind=kOutput, calls=%fused_computation.31 | convolution fusion | flops 6328475648 | bytes 6246240 | tf_op jit(solution)/shard_map/dot_general | solution.py:274
  53.6 46.4 %collective-permute-done.11 = bf16[512,768]{1,0:T(8,128)(2,1)} collective-permute-done((bf16[512,768]{1,0:T(8,128)(2,1)}, bf16[512,768]{1,0:T(8,128)(2,1)}, u32[]{:S(2)}, u32[]{:S(2)}) %collective-permute-start.11) | collective-permute-done | bytes 786464 | tf_op jit(solution)/shard_map/ppermute | solution.py:42
  100.0 14.0 %collective-permute-done.12 = bf16[512,768]{1,0:T(8,128)(2,1)} collective-permute-done((bf16[512,768]{1,0:T(8,128)(2,1)}, bf16[512,768]{1,0:T(8,128)(2,1)}, u32[]{:S(2)}, u32[]{:S(2)}) %collective-permute-start.12) | collective-permute-done | bytes 786464 | tf_op jit(solution)/shard_map/ppermute | solution.py:42
  121.8 8.2 %collective-permute-done.14 = bf16[128,768]{1,0:T(8,128)(2,1)S(1)} collective-permute-done((bf16[128,768]{1,0:T(8,128)(2,1)S(1)}, bf16[128,768]{1,0:T(8,128)(2,1)S(1)}, u32[]{:S(2)}, u32[]{:S(2)}) %collective-permute-start.14) | collective-permute-done | bytes 196640 | tf_op jit(solution)/shard_map/ppermute | solution.py:42
  129.9 6.2 collective-permute-done.16
  136.1 12.2 %collective-permute-done.15 = bf16[128,768]{1,0:T(8,128)(2,1)S(1)} collective-permute-done((bf16[128,768]{1,0:T(8,128)(2,1)S(1)}, bf16[128,768]{1,0:T(8,128)(2,1)S(1)}, u32[]{:S(2)}, u32[]{:S(2)}) %collective-permute-start.15) | collective-permute-done | bytes 196640 | tf_op jit(solution)/shard_map/ppermute | solution.py:42
  150.1 74.1 %all-gather.2.cloned.1.call-done = bf16[768,18560]{1,0:T(8,128)(2,1)} async-done(((bf16[24,18560]{1,0:T(8,128)(2,1)}), bf16[768,18560]{1,0:T(8,128)(2,1)}) %all-gather.2.cloned.1.call-update) | async-done | bytes 28508176 | tf_op jit(solution)/shard_map/all_gather | solution.py:332
  225.7 2.7 convolution_convert_fusion.7
  233.5 8.0 collective-permute-done.19.rest_3_
  241.5 7.8 collective-permute-done.18.rest_2_
  249.7 6.7 fusion.93
  261.2 11.8 %attend.2 = (bf16[128,768]{1,0:T(8,128)(2,1)}, f32[2,8,768]{2,1,0:T(8,128)}, bf16[2,768,768]{2,1,0:T(8,128)(2,1)}) custom-call(s32[1]{0:T(128)} %bitcast.3.rank_ref, bf16[128,768]{1,0:T(8,128)(2,1)} %slice.351.q_ref, f32[12,768]{1,0:T(8,128)} %mul.480.pre_ref, f32[12,768]{1,0:T(8,128)} %reshape.374.post_ref, bf16[128,1536]{1,0:T(8,128)(2,1)} %copy-done.11, ...), custom_call_target="tpu_custom_call" | custom-call | tf_op jit(solution)/shard_map/attend/pallas_call | solution.py:218
  275.5 3.3 fusion.18
  287.3 9.4 %collective-permute-done.26.rest_3_ = bf16[128,1536]{1,0:T(8,128)(2,1)S(1)} collective-permute-done((bf16[128,1536]{1,0:T(8,128)(2,1)S(1)}, bf16[128,1536]{1,0:T(8,128)(2,1)S(1)}, u32[]{:S(2)}, u32[]{:S(2)}) %collective-permute-start.26) | collective-permute-done | bytes 393248 | tf_op jit(solution)/shard_map/ppermute | solution.py:42
  296.8 7.4 collective-permute-done.25.rest_2_
  314.3 4.8 copy.113
  322.3 11.8 %attend.3 = (bf16[128,768]{1,0:T(8,128)(2,1)}, f32[2,8,768]{2,1,0:T(8,128)}, bf16[2,768,768]{2,1,0:T(8,128)(2,1)}) custom-call(s32[1]{0:T(128)} %bitcast.3.rank_ref, bf16[128,768]{1,0:T(8,128)(2,1)} %slice.360.q_ref, f32[12,768]{1,0:T(8,128)} %mul.500.pre_ref, f32[12,768]{1,0:T(8,128)} %reshape.377.post_ref, bf16[128,1536]{1,0:T(8,128)(2,1)} %copy-done.12, ...), custom_call_target="tpu_custom_call" | custom-call | tf_op jit(solution)/shard_map/attend/pallas_call | solution.py:218
  336.0 3.3 fusion.14
  339.7 2.8 fusion.45
  342.6 4.4 multiply_reduce_fusion
  350.8 18.4 %attend_back.2 = (bf16[128,768]{1,0:T(8,128)(2,1)}, f32[12,768]{1,0:T(8,128)}, f32[12,768]{1,0:T(8,128)}, bf16[128,1536]{1,0:T(8,128)(2,1)}, bf16[128,1536]{1,0:...) custom-call(s32[1]{0:T(128)} %bitcast.3.rank_ref, ...), custom_call_target="tpu_custom_call" | custom-call | tf_op jit(solution)/shard_map/attend_back/pallas_call | solution.py:247
  385.8 5.0 convolution_convert_fusion
  390.7 7.3 collective-permute-done.41
  399.7 3.0 fusion.9
  402.7 4.6 multiply_reduce_fusion.1
  412.0 4.9 fusion.8
  424.6 4.7 fusion.38
  429.3 4.8 multiply_reduce_fusion.2
  434.3 2.8 convolution_convert_fusion.10.go_ref
  437.1 18.9 %attend_back.3 = (bf16[128,768]{1,0:T(8,128)(2,1)}, f32[12,768]{1,0:T(8,128)}, f32[12,768]{1,0:T(8,128)}, bf16[128,1536]{1,0:T(8,128)(2,1)}, bf16[128,1536]{1,0:...) custom-call(s32[1]{0:T(128)} %bitcast.3.rank_ref, ...), custom_call_target="tpu_custom_call" | custom-call | tf_op jit(solution)/shard_map/attend_back/pallas_call | solution.py:247
  468.6 3.8 convolution_convert_fusion.3
  473.5 2.9 collective-permute-done.46
  476.5 17.2 %collective-permute-done.48 = bf16[128,1536]{1,0:T(8,128)(2,1)S(1)} collective-permute-done((bf16[128,1536]{1,0:T(8,128)(2,1)S(1)}, bf16[128,1536]{1,0:T(8,128)(2,1)S(1)}, u32[]{:S(2)}, u32[]{:S(2)}) %collective-permute-start.48) | collective-permute-done | bytes 393248 | tf_op jit(solution)/shard_map/ppermute | solution.py:42
  495.0 3.4 fusion.62
  498.8 3.0 fusion.11
  502.9 3.7 fusion.10
  512.9 4.1 fusion.46
  520.2 3.7 collective-permute-start.49
  523.9 5.2 collective-permute-done.51
  529.1 6.7 collective-permute-done.50
  539.1 4.0 collective-permute-start.32
  544.3 10.6 %collective-permute-done.61 = f32[2,2,12,12]{2,3,1,0:T(8,128)S(1)} collective-permute-done((f32[2,2,12,12]{2,3,1,0:T(8,128)S(1)}, f32[2,2,12,12]{2,3,1,0:T(8,128)S(1)}, u32[]{:S(2)}, u32[]{:S(2)}) %collective-permute-start.61) | collective-permute-done | bytes 2336 | tf_op jit(solution)/shard_map/ppermute | solution.py:42
  556.2 4.3 collective-permute-start.63
  560.5 26.1 %collective-permute-done.32 = bf16[64,768]{1,0:T(8,128)(2,1)S(1)} collective-permute-done((bf16[64,768]{1,0:T(8,128)(2,1)S(1)}, bf16[64,768]{1,0:T(8,128)(2,1)S(1)}, u32[]{:S(2)}, u32[]{:S(2)}) %collective-permute-start.32) | collective-permute-done | bytes 98336 | tf_op jit(solution)/shard_map/ppermute | solution.py:412
  600.9 11.0 %fusion.2 = f32[1004,768]{1,0:T(8,128)} fusion(bf16[4096,768]{1,0:T(8,128)(2,1)} %constant_dynamic-update-slice_fusion.7, s32[4096]{0:T(1024)S(1)} %select_n.127, s32[1004]{0:T(1024)S(1)} %copy-done.59), kind=kOutput, calls=%fused_computation.3 | convolution fusion | flops 6320734208 | bytes 9396144 | tf_op jit(solution)/shard_map/dot_general | solution.py:274
  612.0 10.2 %reduce-scatter.9.cloned.1.call-done = bf16[24,9344]{1,0:T(8,128)(2,1)} async-done(((bf16[768,9344]{1,0:T(8,128)(2,1)}), bf16[24,9344]{1,0:T(8,128)(2,1)}) %reduce-scatter.9.cloned.1.call-update) | async-done | bytes 448528
  630.3 161.9 %reduce-scatter.7.cloned.1.call-done = bf16[24,9344]{1,0:T(8,128)(2,1)} async-done(((bf16[768,9344]{1,0:T(8,128)(2,1)}), bf16[24,9344]{1,0:T(8,128)(2,1)}) %reduce-scatter.7.cloned.1.call-update) | async-done | bytes 448528
  (460 shorter events, 181.1 us)
Async XLA Ops:
  7.2 217.0 %all-gather.2.cloned.1.call-start = ((), (), s32[]{:S(2)}) async-start(), calls=%async_computation.2 | async-start | bytes 29399040 | tf_op jit(solution)/shard_map/all_gather | solution.py:332
  16.8 605.4 %reduce-scatter.9.cloned.1.call-start = ((), (), s32[]{:S(2)}) async-start(), calls=%async_computation.4 | async-start | bytes 14800896
  17.3 9.8 %collective-permute-start.6 = (s32[1,128]{1,0:T(1,128)S(1)}, s32[1,128]{1,0:T(1,128)S(1)}, u32[]{:S(2)}, u32[]{:S(2)}) collective-permute-start(s32[1,128]{1,0:T(1,128)S(1)} %copy-done.65), channel_id=1, source_target_pairs={{0,7},{1,6},{2,5},{3,4},{4,3},{5,2},{6,1},{7,0},{8,15},{9,14},{10,... | collective-permute-start | bytes 1544 | tf_op jit(solution)/shard_map/ppermute | solution.py:42
  26.4 12.9 %collective-permute-start.10 = (bf16[1004,768]{1,0:T(8,128)(2,1)}, bf16[1004,768]{1,0:T(8,128)(2,1)}, u32[]{:S(2)}, u32[]{:S(2)}) collective-permute-start(bf16[1004,768]{1,0:T(8,128)(2,1)} %param.13), channel_id=1, source_target_pairs={{0,8},{1,9},{2,10},{3,11},{4,12},{5,13},{6,14},{7,15},{8,0},{9,1},... | collective-permute-start | bytes 4626440 | tf_op jit(solution)/shard_map/ppermute | solution.py:42
  50.1 49.9 %collective-permute-start.11 = (bf16[512,768]{1,0:T(8,128)(2,1)}, bf16[512,768]{1,0:T(8,128)(2,1)}, u32[]{:S(2)}, u32[]{:S(2)}) collective-permute-start(bf16[512,768]{1,0:T(8,128)(2,1)} %get-tuple-element.103), channel_id=1, source_target_pairs={{0,1},{1,0},{2,3},{3,2},{4,5},{5,4},{6,7},{7,6},{8,9},{9,8},{10,11... | collective-permute-start | bytes 2359304 | tf_op jit(solution)/shard_map/ppermute | solution.py:42
  50.6 49.3 %collective-permute-start.13 = (bf16[512,768]{1,0:T(8,128)(2,1)}, bf16[512,768]{1,0:T(8,128)(2,1)}, u32[]{:S(2)}, u32[]{:S(2)}) collective-permute-start(bf16[512,768]{1,0:T(8,128)(2,1)} %get-tuple-element.104), channel_id=1, source_target_pairs={{0,17},{1,16},{2,19},{3,18},{4,21},{5,20},{6,23},{7,22},{8,25},{9,... | collective-permute-start | bytes 2359304 | tf_op jit(solution)/shard_map/ppermute | solution.py:42
  52.8 61.1 %collective-permute-start.12 = (bf16[512,768]{1,0:T(8,128)(2,1)}, bf16[512,768]{1,0:T(8,128)(2,1)}, u32[]{:S(2)}, u32[]{:S(2)}) collective-permute-start(bf16[512,768]{1,0:T(8,128)(2,1)} %get-tuple-element.105), channel_id=1, source_target_pairs={{0,16},{1,17},{2,18},{3,19},{4,20},{5,21},{6,22},{7,23},{8,24},{9,... | collective-permute-start | bytes 2359304 | tf_op jit(solution)/shard_map/ppermute | solution.py:42
  116.6 13.3 %collective-permute-start.14 = (bf16[128,768]{1,0:T(8,128)(2,1)S(1)}, bf16[128,768]{1,0:T(8,128)(2,1)S(1)}, u32[]{:S(2)}, u32[]{:S(2)}) collective-permute-start(bf16[128,768]{1,0:T(8,128)(2,1)S(1)} %get-tuple-element.106), channel_id=1, source_target_pairs={{0,2},{1,3},{2,0},{3,1},{4,6},{5,7},{6,4},{7,5},{8,10},{9,11},{10,... | collective-permute-start | bytes 589832 | tf_op jit(solution)/shard_map/ppermute | solution.py:42
  118.0 18.2 %collective-permute-start.16 = (bf16[128,768]{1,0:T(8,128)(2,1)S(1)}, bf16[128,768]{1,0:T(8,128)(2,1)S(1)}, u32[]{:S(2)}, u32[]{:S(2)}) collective-permute-start(bf16[128,768]{1,0:T(8,128)(2,1)S(1)} %get-tuple-element.107), channel_id=1, source_target_pairs={{0,6},{1,7},{2,4},{3,5},{4,2},{5,3},{6,0},{7,1},{8,14},{9,15},{10,... | collective-permute-start | bytes 589832 | tf_op jit(solution)/shard_map/ppermute | solution.py:42
  120.4 28.0 %collective-permute-start.15 = (bf16[128,768]{1,0:T(8,128)(2,1)S(1)}, bf16[128,768]{1,0:T(8,128)(2,1)S(1)}, u32[]{:S(2)}, u32[]{:S(2)}) collective-permute-start(bf16[128,768]{1,0:T(8,128)(2,1)S(1)} %get-tuple-element.108), channel_id=1, source_target_pairs={{0,4},{1,5},{2,6},{3,7},{4,0},{5,1},{6,2},{7,3},{8,12},{9,13},{10,... | collective-permute-start | bytes 589832 | tf_op jit(solution)/shard_map/ppermute | solution.py:42
  228.5 13.0 %collective-permute-start.19 = (bf16[128,1536]{1,0:T(8,128)(2,1)S(1)}, bf16[128,1536]{1,0:T(8,128)(2,1)S(1)}, u32[]{:S(2)}, u32[]{:S(2)}) collective-permute-start(bf16[128,1536]{1,0:T(8,128)(2,1)S(1)} %slice.352.rest_0_), channel_id=1, source_target_pairs={{0,17},{1,16},{2,19},{3,18},{4,21},{5,20},{6,23},{7,22},{8,25},{9,... | collective-permute-start | bytes 1179656 | tf_op jit(solution)/shard_map/ppermute | solution.py:42
  230.0 19.2 %collective-permute-start.18 = (bf16[128,1536]{1,0:T(8,128)(2,1)S(1)}, bf16[128,1536]{1,0:T(8,128)(2,1)S(1)}, u32[]{:S(2)}, u32[]{:S(2)}) collective-permute-start(bf16[128,1536]{1,0:T(8,128)(2,1)S(1)} %slice.352.rest_0_), channel_id=1, source_target_pairs={{0,16},{1,17},{2,18},{3,19},{4,20},{5,21},{6,22},{7,23},{8,24},{9,... | collective-permute-start | bytes 1179656 | tf_op jit(solution)/shard_map/ppermute | solution.py:42
  231.5 17.7 %collective-permute-start.17 = (bf16[128,1536]{1,0:T(8,128)(2,1)S(1)}, bf16[128,1536]{1,0:T(8,128)(2,1)S(1)}, u32[]{:S(2)}, u32[]{:S(2)}) collective-permute-start(bf16[128,1536]{1,0:T(8,128)(2,1)S(1)} %slice.352.rest_0_), channel_id=1, source_target_pairs={{0,1},{1,0},{2,3},{3,2},{4,5},{5,4},{6,7},{7,6},{8,9},{9,8},{10,11... | collective-permute-start | bytes 1179656 | tf_op jit(solution)/shard_map/ppermute | solution.py:42
  233.5 26.6 %collective-permute-start.20 = (bf16[128,1536]{1,0:T(8,128)(2,1)S(1)}, bf16[128,1536]{1,0:T(8,128)(2,1)S(1)}, u32[]{:S(2)}, u32[]{:S(2)}) collective-permute-start(bf16[128,1536]{1,0:T(8,128)(2,1)S(1)} %slice.352.rest_0_), channel_id=1, source_target_pairs={{0,8},{1,9},{2,10},{3,11},{4,12},{5,13},{6,14},{7,15},{8,0},{9,1},... | collective-permute-start | bytes 1179656 | tf_op jit(solution)/shard_map/ppermute | solution.py:42
  241.4 18.7 %collective-permute-start.23 = (bf16[128,1536]{1,0:T(8,128)(2,1)S(1)}, bf16[128,1536]{1,0:T(8,128)(2,1)S(1)}, u32[]{:S(2)}, u32[]{:S(2)}) collective-permute-start(bf16[128,1536]{1,0:T(8,128)(2,1)S(1)} %collective-permute-done.19.rest_3_), channel_id=1, source_target_pairs={{0,8},{1,9},{2,10},{3,11},{4,12},{5,13},{6,14},{7,15},{8,0},{9,1},... | collective-permute-start | bytes 1179656 | tf_op jit(solution)/shard_map/ppermute | solution.py:42
  249.2 10.9 %collective-permute-start.22 = (bf16[128,1536]{1,0:T(8,128)(2,1)S(1)}, bf16[128,1536]{1,0:T(8,128)(2,1)S(1)}, u32[]{:S(2)}, u32[]{:S(2)}) collective-permute-start(bf16[128,1536]{1,0:T(8,128)(2,1)S(1)} %collective-permute-done.18.rest_2_), channel_id=1, source_target_pairs={{0,8},{1,9},{2,10},{3,11},{4,12},{5,13},{6,14},{7,15},{8,0},{9,1},... | collective-permute-start | bytes 1179656 | tf_op jit(solution)/shard_map/ppermute | solution.py:42
  249.2 10.9 %collective-permute-start.21 = (bf16[128,1536]{1,0:T(8,128)(2,1)S(1)}, bf16[128,1536]{1,0:T(8,128)(2,1)S(1)}, u32[]{:S(2)}, u32[]{:S(2)}) collective-permute-start(bf16[128,1536]{1,0:T(8,128)(2,1)S(1)} %collective-permute-done.17.rest_1_), channel_id=1, source_target_pairs={{0,8},{1,9},{2,10},{3,11},{4,12},{5,13},{6,14},{7,15},{8,0},{9,1},... | collective-permute-start | bytes 1179656 | tf_op jit(solution)/shard_map/ppermute | solution.py:42
  283.8 13.0 %collective-permute-start.26 = (bf16[128,1536]{1,0:T(8,128)(2,1)S(1)}, bf16[128,1536]{1,0:T(8,128)(2,1)S(1)}, u32[]{:S(2)}, u32[]{:S(2)}) collective-permute-start(bf16[128,1536]{1,0:T(8,128)(2,1)S(1)} %slice.361.rest_0_), channel_id=1, source_target_pairs={{0,17},{1,16},{2,19},{3,18},{4,21},{5,20},{6,23},{7,22},{8,25},{9,... | collective-permute-start | bytes 1179656 | tf_op jit(solution)/shard_map/ppermute | solution.py:42
  285.3 18.9 %collective-permute-start.25 = (bf16[128,1536]{1,0:T(8,128)(2,1)S(1)}, bf16[128,1536]{1,0:T(8,128)(2,1)S(1)}, u32[]{:S(2)}, u32[]{:S(2)}) collective-permute-start(bf16[128,1536]{1,0:T(8,128)(2,1)S(1)} %slice.361.rest_0_), channel_id=1, source_target_pairs={{0,16},{1,17},{2,18},{3,19},{4,20},{5,21},{6,22},{7,23},{8,24},{9,... | collective-permute-start | bytes 1179656 | tf_op jit(solution)/shard_map/ppermute | solution.py:42
  286.4 17.9 %collective-permute-start.24 = (bf16[128,1536]{1,0:T(8,128)(2,1)S(1)}, bf16[128,1536]{1,0:T(8,128)(2,1)S(1)}, u32[]{:S(2)}, u32[]{:S(2)}) collective-permute-start(bf16[128,1536]{1,0:T(8,128)(2,1)S(1)} %slice.361.rest_0_), channel_id=1, source_target_pairs={{0,1},{1,0},{2,3},{3,2},{4,5},{5,4},{6,7},{7,6},{8,9},{9,8},{10,11... | collective-permute-start | bytes 1179656 | tf_op jit(solution)/shard_map/ppermute | solution.py:42
  287.3 33.5 %collective-permute-start.27 = (bf16[128,1536]{1,0:T(8,128)(2,1)S(1)}, bf16[128,1536]{1,0:T(8,128)(2,1)}, u32[]{:S(2)}, u32[]{:S(2)}) collective-permute-start(bf16[128,1536]{1,0:T(8,128)(2,1)S(1)} %slice.361.rest_0_), channel_id=1, source_target_pairs={{0,8},{1,9},{2,10},{3,11},{4,12},{5,13},{6,14},{7,15},{8,0},{9,1},... | collective-permute-start | bytes 1179656 | tf_op jit(solution)/shard_map/ppermute | solution.py:42
  296.8 25.5 %collective-permute-start.30 = (bf16[128,1536]{1,0:T(8,128)(2,1)S(1)}, bf16[128,1536]{1,0:T(8,128)(2,1)}, u32[]{:S(2)}, u32[]{:S(2)}) collective-permute-start(bf16[128,1536]{1,0:T(8,128)(2,1)S(1)} %collective-permute-done.26.rest_3_), channel_id=1, source_target_pairs={{0,8},{1,9},{2,10},{3,11},{4,12},{5,13},{6,14},{7,15},{8,0},{9,1},... | collective-permute-start | bytes 1179656 | tf_op jit(solution)/shard_map/ppermute | solution.py:42
  304.2 18.1 %collective-permute-start.29 = (bf16[128,1536]{1,0:T(8,128)(2,1)S(1)}, bf16[128,1536]{1,0:T(8,128)(2,1)}, u32[]{:S(2)}, u32[]{:S(2)}) collective-permute-start(bf16[128,1536]{1,0:T(8,128)(2,1)S(1)} %collective-permute-done.25.rest_2_), channel_id=1, source_target_pairs={{0,8},{1,9},{2,10},{3,11},{4,12},{5,13},{6,14},{7,15},{8,0},{9,1},... | collective-permute-start | bytes 1179656 | tf_op jit(solution)/shard_map/ppermute | solution.py:42
  304.3 18.0 %collective-permute-start.28 = (bf16[128,1536]{1,0:T(8,128)(2,1)S(1)}, bf16[128,1536]{1,0:T(8,128)(2,1)}, u32[]{:S(2)}, u32[]{:S(2)}) collective-permute-start(bf16[128,1536]{1,0:T(8,128)(2,1)S(1)} %collective-permute-done.24.rest_1_), channel_id=1, source_target_pairs={{0,8},{1,9},{2,10},{3,11},{4,12},{5,13},{6,14},{7,15},{8,0},{9,1},... | collective-permute-start | bytes 1179656 | tf_op jit(solution)/shard_map/ppermute | solution.py:42
  305.5 33.8 %collective-permute-start.33 = (bf16[64,768]{1,0:T(8,128)(2,1)}, bf16[64,768]{1,0:T(8,128)(2,1)}, u32[]{:S(2)}, u32[]{:S(2)}) collective-permute-start(bf16[64,768]{1,0:T(8,128)(2,1)} %get-tuple-element.117), channel_id=1, source_target_pairs={{0,0},{1,8},{2,16},{3,24},{4,25},{5,17},{6,9},{7,1},{8,2},{9,10},{... | collective-permute-start | bytes 294920 | tf_op jit(solution)/shard_map/ppermute | solution.py:377
  320.8 18.5 %collective-permute-start.34 = (bf16[64,768]{1,0:T(8,128)(2,1)S(1)}, bf16[64,768]{1,0:T(8,128)(2,1)S(1)}, u32[]{:S(2)}, u32[]{:S(2)}) collective-permute-start(bf16[64,768]{1,0:T(8,128)(2,1)S(1)} %copy-done.48), channel_id=1, source_target_pairs={{0,1},{1,9},{2,17},{3,25},{4,24},{5,16},{6,8},{7,0},{8,3},{9,11},{... | collective-permute-start | bytes 294920 | tf_op jit(solution)/shard_map/ppermute | solution.py:378
  370.9 19.8 %collective-permute-start.35 = (bf16[128,1536]{1,0:T(8,128)(2,1)}, bf16[128,1536]{1,0:T(8,128)(2,1)}, u32[]{:S(2)}, u32[]{:S(2)}) collective-permute-start(bf16[128,1536]{1,0:T(8,128)(2,1)} %get-tuple-element.44), channel_id=1, source_target_pairs={{0,8},{1,9},{2,10},{3,11},{4,12},{5,13},{6,14},{7,15},{8,0},{9,1},... | collective-permute-start | bytes 1179656 | tf_op jit(solution)/shard_map/ppermute | solution.py:42
  374.3 16.4 %collective-permute-start.37 = (bf16[128,1536]{1,0:T(8,128)(2,1)}, bf16[128,1536]{1,0:T(8,128)(2,1)}, u32[]{:S(2)}, u32[]{:S(2)}) collective-permute-start(bf16[128,1536]{1,0:T(8,128)(2,1)} %add_convert_fusion.7), channel_id=1, source_target_pairs={{0,1},{1,0},{2,3},{3,2},{4,5},{5,4},{6,7},{7,6},{8,9},{9,8},{10,11... | collective-permute-start | bytes 1179656 | tf_op jit(solution)/shard_map/ppermute | solution.py:42
  376.1 14.6 %collective-permute-start.39 = (bf16[128,1536]{1,0:T(8,128)(2,1)}, bf16[128,1536]{1,0:T(8,128)(2,1)}, u32[]{:S(2)}, u32[]{:S(2)}) collective-permute-start(bf16[128,1536]{1,0:T(8,128)(2,1)} %add_convert_fusion.6), channel_id=1, source_target_pairs={{0,16},{1,17},{2,18},{3,19},{4,20},{5,21},{6,22},{7,23},{8,24},{9,... | collective-permute-start | bytes 1179656 | tf_op jit(solution)/shard_map/ppermute | solution.py:42
  380.4 17.7 %collective-permute-start.41 = (bf16[128,1536]{1,0:T(8,128)(2,1)}, bf16[128,1536]{1,0:T(8,128)(2,1)}, u32[]{:S(2)}, u32[]{:S(2)}) collective-permute-start(bf16[128,1536]{1,0:T(8,128)(2,1)} %add_convert_fusion.5), channel_id=1, source_target_pairs={{0,17},{1,16},{2,19},{3,18},{4,21},{5,20},{6,23},{7,22},{8,25},{9,... | collective-permute-start | bytes 1179656 | tf_op jit(solution)/shard_map/ppermute | solution.py:42
  422.3 369.9 %reduce-scatter.7.cloned.1.call-start = ((), (), s32[]{:S(2)}) async-start(), calls=%async_computation.3 | async-start | bytes 14800896
  456.1 16.3 %collective-permute-start.42 = (bf16[128,1536]{1,0:T(8,128)(2,1)}, bf16[128,1536]{1,0:T(8,128)(2,1)}, u32[]{:S(2)}, u32[]{:S(2)}) collective-permute-start(bf16[128,1536]{1,0:T(8,128)(2,1)} %get-tuple-element.55), channel_id=1, source_target_pairs={{0,8},{1,9},{2,10},{3,11},{4,12},{5,13},{6,14},{7,15},{8,0},{9,1},... | collective-permute-start | bytes 1179656 | tf_op jit(solution)/shard_map/ppermute | solution.py:42
  462.4 11.2 %collective-permute-start.44 = (bf16[128,1536]{1,0:T(8,128)(2,1)S(1)}, bf16[128,1536]{1,0:T(8,128)(2,1)S(1)}, u32[]{:S(2)}, u32[]{:S(2)}) collective-permute-start(bf16[128,1536]{1,0:T(8,128)(2,1)S(1)} %add_convert_fusion.3), channel_id=1, source_target_pairs={{0,1},{1,0},{2,3},{3,2},{4,5},{5,4},{6,7},{7,6},{8,9},{9,8},{10,11... | collective-permute-start | bytes 1179656 | tf_op jit(solution)/shard_map/ppermute | solution.py:42
  463.7 12.8 %collective-permute-start.46 = (bf16[128,1536]{1,0:T(8,128)(2,1)S(1)}, bf16[128,1536]{1,0:T(8,128)(2,1)S(1)}, u32[]{:S(2)}, u32[]{:S(2)}) collective-permute-start(bf16[128,1536]{1,0:T(8,128)(2,1)S(1)} %add_convert_fusion.2), channel_id=1, source_target_pairs={{0,16},{1,17},{2,18},{3,19},{4,20},{5,21},{6,22},{7,23},{8,24},{9,... | collective-permute-start | bytes 1179656 | tf_op jit(solution)/shard_map/ppermute | solution.py:42
  466.7 27.0 %collective-permute-start.48 = (bf16[128,1536]{1,0:T(8,128)(2,1)S(1)}, bf16[128,1536]{1,0:T(8,128)(2,1)S(1)}, u32[]{:S(2)}, u32[]{:S(2)}) collective-permute-start(bf16[128,1536]{1,0:T(8,128)(2,1)S(1)} %add_convert_fusion.1), channel_id=1, source_target_pairs={{0,17},{1,16},{2,19},{3,18},{4,21},{5,20},{6,23},{7,22},{8,25},{9,... | collective-permute-start | bytes 1179656 | tf_op jit(solution)/shard_map/ppermute | solution.py:42
  519.5 9.6 %collective-permute-start.51 = (bf16[128,768]{1,0:T(8,128)(2,1)S(1)}, bf16[128,768]{1,0:T(8,128)(2,1)S(1)}, u32[]{:S(2)}, u32[]{:S(2)}) collective-permute-start(bf16[128,768]{1,0:T(8,128)(2,1)S(1)} %get-tuple-element.93), channel_id=1, source_target_pairs={{0,6},{1,7},{2,4},{3,5},{4,2},{5,3},{6,0},{7,1},{8,14},{9,15},{10,... | collective-permute-start | bytes 589832 | tf_op jit(solution)/shard_map/ppermute | solution.py:42
  519.5 16.4 %collective-permute-start.50 = (bf16[128,768]{1,0:T(8,128)(2,1)S(1)}, bf16[128,768]{1,0:T(8,128)(2,1)S(1)}, u32[]{:S(2)}, u32[]{:S(2)}) collective-permute-start(bf16[128,768]{1,0:T(8,128)(2,1)S(1)} %get-tuple-element.93), channel_id=1, source_target_pairs={{0,4},{1,5},{2,6},{3,7},{4,0},{5,1},{6,2},{7,3},{8,12},{9,13},{10,... | collective-permute-start | bytes 589832 | tf_op jit(solution)/shard_map/ppermute | solution.py:42
  520.2 15.7 %collective-permute-start.49 = (bf16[128,768]{1,0:T(8,128)(2,1)S(1)}, bf16[128,768]{1,0:T(8,128)(2,1)S(1)}, u32[]{:S(2)}, u32[]{:S(2)}) collective-permute-start(bf16[128,768]{1,0:T(8,128)(2,1)S(1)} %get-tuple-element.93), channel_id=1, source_target_pairs={{0,2},{1,3},{2,0},{3,1},{4,6},{5,7},{6,4},{7,5},{8,10},{9,11},{10,... | collective-permute-start | bytes 589832 | tf_op jit(solution)/shard_map/ppermute | solution.py:42
  523.9 19.2 %collective-permute-start.60 = (f32[2,2,12,12]{2,3,1,0:T(8,128)S(1)}, f32[2,2,12,12]{2,3,1,0:T(8,128)S(1)}, u32[]{:S(2)}, u32[]{:S(2)}) collective-permute-start(f32[2,2,12,12]{2,3,1,0:T(8,128)S(1)} %fusion.88), channel_id=1, source_target_pairs={{0,2},{1,3},{2,0},{3,1},{4,6},{5,7},{6,4},{7,5},{8,10},{9,11},{10,... | collective-permute-start | bytes 6920 | tf_op jit(solution)/shard_map/ppermute | solution.py:42
  535.9 54.1 %collective-permute-start.53 = (bf16[512,768]{1,0:T(8,128)(2,1)S(1)}, bf16[512,768]{1,0:T(8,128)(2,1)S(1)}, u32[]{:S(2)}, u32[]{:S(2)}) collective-permute-start(bf16[512,768]{1,0:T(8,128)(2,1)S(1)} %pad_maximum_fusion), channel_id=1, source_target_pairs={{0,16},{1,17},{2,18},{3,19},{4,20},{5,21},{6,22},{7,23},{8,24},{9,... | collective-permute-start | bytes 2359304 | tf_op jit(solution)/shard_map/ppermute | solution.py:42
  537.1 51.7 %collective-permute-start.52 = (bf16[512,768]{1,0:T(8,128)(2,1)S(1)}, bf16[512,768]{1,0:T(8,128)(2,1)S(1)}, u32[]{:S(2)}, u32[]{:S(2)}) collective-permute-start(bf16[512,768]{1,0:T(8,128)(2,1)S(1)} %pad_maximum_fusion), channel_id=1, source_target_pairs={{0,1},{1,0},{2,3},{3,2},{4,5},{5,4},{6,7},{7,6},{8,9},{9,8},{10,11... | collective-permute-start | bytes 2359304 | tf_op jit(solution)/shard_map/ppermute | solution.py:42
  538.5 17.7 %collective-permute-start.31 = (bf16[64,768]{1,0:T(8,128)(2,1)S(1)}, bf16[64,768]{1,0:T(8,128)(2,1)S(1)}, u32[]{:S(2)}, u32[]{:S(2)}) collective-permute-start(bf16[64,768]{1,0:T(8,128)(2,1)S(1)} %get-tuple-element.119), channel_id=1, source_target_pairs={{0,0},{8,1},{16,2},{24,3},{25,4},{17,5},{9,6},{1,7},{2,8},{10,9},{... | collective-permute-start | bytes 294920 | tf_op jit(solution)/shard_map/ppermute | solution.py:412
  539.1 47.5 %collective-permute-start.32 = (bf16[64,768]{1,0:T(8,128)(2,1)S(1)}, bf16[64,768]{1,0:T(8,128)(2,1)S(1)}, u32[]{:S(2)}, u32[]{:S(2)}) collective-permute-start(bf16[64,768]{1,0:T(8,128)(2,1)S(1)} %get-tuple-element.120), channel_id=1, source_target_pairs={{1,0},{9,1},{17,2},{25,3},{24,4},{16,5},{8,6},{0,7},{3,8},{11,9},{... | collective-permute-start | bytes 294920 | tf_op jit(solution)/shard_map/ppermute | solution.py:412
  543.1 11.8 %collective-permute-start.61 = (f32[2,2,12,12]{2,3,1,0:T(8,128)S(1)}, f32[2,2,12,12]{2,3,1,0:T(8,128)S(1)}, u32[]{:S(2)}, u32[]{:S(2)}) collective-permute-start(f32[2,2,12,12]{2,3,1,0:T(8,128)S(1)} %fusion.115), channel_id=1, source_target_pairs={{0,4},{1,5},{2,6},{3,7},{4,0},{5,1},{6,2},{7,3},{8,12},{9,13},{10,... | collective-permute-start | bytes 6920 | tf_op jit(solution)/shard_map/ppermute | solution.py:42
  556.1 35.4 %collective-permute-start.54 = (bf16[512,768]{1,0:T(8,128)(2,1)S(1)}, bf16[512,768]{1,0:T(8,128)(2,1)}, u32[]{:S(2)}, u32[]{:S(2)}) collective-permute-start(bf16[512,768]{1,0:T(8,128)(2,1)S(1)} %pad_maximum_fusion), channel_id=1, source_target_pairs={{0,17},{1,16},{2,19},{3,18},{4,21},{5,20},{6,23},{7,22},{8,25},{9,... | collective-permute-start | bytes 2359304 | tf_op jit(solution)/shard_map/ppermute | solution.py:42
  556.2 31.2 %collective-permute-start.63 = (f32[2,2,12,12]{2,3,1,0:T(8,128)S(1)}, f32[2,2,12,12]{2,3,1,0:T(8,128)S(1)}, u32[]{:S(2)}, u32[]{:S(2)}) collective-permute-start(f32[2,2,12,12]{2,3,1,0:T(8,128)S(1)} %add.373), channel_id=1, source_target_pairs={{0,16},{1,17},{2,18},{3,19},{4,20},{5,21},{6,22},{7,23},{8,24},{9,... | collective-permute-start | bytes 6920 | tf_op jit(solution)/shard_map/ppermute | solution.py:42
  588.8 9.3 %collective-permute-start.56 = (bf16[512,768]{1,0:T(8,128)(2,1)S(1)}, bf16[512,768]{1,0:T(8,128)(2,1)S(1)}, u32[]{:S(2)}, u32[]{:S(2)}) collective-permute-start(bf16[512,768]{1,0:T(8,128)(2,1)S(1)} %collective-permute-done.52), channel_id=1, source_target_pairs={{0,8},{1,9},{2,10},{3,11},{4,12},{5,13},{6,14},{7,15},{8,0},{9,1},... | collective-permute-start | bytes 2359304 | tf_op jit(solution)/shard_map/ppermute | solution.py:42
  590.0 9.0 %collective-permute-start.57 = (bf16[512,768]{1,0:T(8,128)(2,1)S(1)}, bf16[512,768]{1,0:T(8,128)(2,1)S(1)}, u32[]{:S(2)}, u32[]{:S(2)}) collective-permute-start(bf16[512,768]{1,0:T(8,128)(2,1)S(1)} %collective-permute-done.53), channel_id=1, source_target_pairs={{0,8},{1,9},{2,10},{3,11},{4,12},{5,13},{6,14},{7,15},{8,0},{9,1},... | collective-permute-start | bytes 2359304 | tf_op jit(solution)/shard_map/ppermute | solution.py:42
  (102 other events, 1173.8 us)
Sparse Core Ops, SparseCore 0:
  16.9 207.2 all-gather.1
  422.4 199.7 reduce-scatter.8
  629.4 162.7 reduce-scatter.6

commit v2 on v1

--- a/solution.py
+++ b/solution.py
@@ -26,10 +26,16 @@
         self.count = self.b * self.n
         self.core = self.n
         low = list(range(self.r))
-        high = [k * self.n for k in range(0, self.b, 2)]
-        self.plane = [h + l for h in high for l in low]
+        self.high = [k * self.n for k in range(0, self.b, 2)]
+        self.low = low
+        self.plane = [h + l for h in self.high for l in low]
         self.zs = [k * self.r for k in range(self.b)]
-        self.order = [c + p + z for c in (0, self.core) for p in self.plane for z in self.zs]
+        self.order = [c + h + l + z for c in (0, self.core) for h in self.high for l in low for z in self.zs]
+        z_bits = bits(self.r, self.n)[::-1]
+        x_bits = [bit for bit in bits(self.n, self.count) if bit != self.core]
+        y_bits = bits(1, self.r)
+        self.x_last = z_bits + y_bits + x_bits + [self.core]
+        self.y_last = z_bits + x_bits + y_bits + [self.core]
 
     def rank_mask(self, mask):
         return (mask // self.n) * self.r + mask % self.n
@@ -38,6 +44,21 @@
         return (rank // self.r) * self.n + sequence * self.r + rank % self.r
 
 
+def bits(first, end):
+    found = []
+    while first < end:
+        found.append(first)
+        first *= 2
+    return found
+
+
+def reached(masks):
+    order = [0]
+    for mask in masks:
+        order = order + [o ^ mask for o in order]
+    return order
+
+
 def swap(value, mask, count):
     return lax.ppermute(value, AXES, [(p, p ^ mask) for p in range(count)])
 
@@ -46,20 +67,18 @@
     return lax.dot_general(a, b, (contract, ((), ())), preferred_element_type=F32)
 
 
-def load_keys(masks, half, rank, pieces, kv, sems):
-    n = len(masks)
+def load_keys(sources, n, half, rank, pieces, kv, sems):
     copies = []
-    for index, mask in enumerate(masks):
+    for k, (index, row, mask, part) in enumerate(sources):
         owner = rank ^ mask
-        for part, place in ((0, owner), (1, 2 * n - 1 - owner)):
-            start = pl.multiple_of(place * half, half)
-            copies.append(
-                pltpu.make_async_copy(
-                    pieces[index].at[pl.ds(part * half, half)],
-                    kv.at[pl.ds(start, half)],
-                    sems.at[2 * index + part],
-                )
+        place = owner if part == 0 else 2 * n - 1 - owner
+        copies.append(
+            pltpu.make_async_copy(
+                pieces[index].at[pl.ds(row, half)],
+                kv.at[pl.ds(pl.multiple_of(place * half, half), half)],
+                sems.at[k],
             )
+        )
     for copy in copies:
         copy.start()
     return copies
@@ -69,14 +88,13 @@
     return jnp.concatenate([rows * weights[g : g + 1, :] for g in range(H)], axis=0)
 
 
-def forward_kernel(masks, half, rank_ref, q_ref, pre_ref, post_ref, *rest):
-    n = len(masks)
-    pieces = rest[:n]
-    o_ref, lse_ref, pv_ref = rest[n : n + 3]
-    kv, qg, logits, top, total, acc, sems = rest[n + 3 :]
+def forward_kernel(n, sources, count, half, rank_ref, q_ref, pre_ref, post_ref, *rest):
+    pieces = rest[:count]
+    o_ref, lse_ref, pv_ref = rest[count : count + 3]
+    kv, qg, logits, top, total, acc, sems = rest[count + 3 :]
     rank = rank_ref[0]
     rows = H * half
-    copies = load_keys(masks, half, rank, pieces, kv, sems)
+    copies = load_keys(sources, n, half, rank, pieces, kv, sems)
     for copy in copies:
         copy.wait()
     for part in range(2):
@@ -127,15 +145,14 @@
         o_ref[part * half : (part + 1) * half, :] = out.astype(BF16)
 
 
-def backward_kernel(masks, half, rank_ref, q_ref, go_ref, lse_ref, pv_ref, pre_ref, post_ref, *rest):
-    n = len(masks)
-    pieces = rest[:n]
-    gq_ref, pre_grad_ref, post_grad_ref = rest[n : n + 3]
-    grads = rest[n + 3 : 2 * n + 3]
-    kv, qg, gg, gk, gv, acc, sems, out_sems = rest[2 * n + 3 :]
+def backward_kernel(n, sources, count, masks, half, rank_ref, q_ref, go_ref, lse_ref, pv_ref, pre_ref, post_ref, *rest):
+    pieces = rest[:count]
+    gq_ref, pre_grad_ref, post_grad_ref = rest[count : count + 3]
+    grads = rest[count + 3 : count + 3 + n]
+    kv, qg, gg, gk, gv, acc, sems, out_sems = rest[count + 3 + n :]
     rank = rank_ref[0]
     rows = H * half
-    copies = load_keys(masks, half, rank, pieces, kv, sems)
+    copies = load_keys(sources, n, half, rank, pieces, kv, sems)
     gk[...] = jnp.zeros(gk.shape, F32)
     gv[...] = jnp.zeros(gv.shape, F32)
     pre_grad_ref[...] = jnp.zeros(pre_grad_ref.shape, F32)
@@ -209,20 +226,20 @@
 LIMIT = pltpu.CompilerParams(vmem_limit_bytes=58 * 2**20)
 
 
-def attend(masks, rank, queries, pieces, pre, post):
-    n = len(masks)
+def attend(n, sources, rank, queries, pieces, pre, post):
+    count = len(pieces)
     tokens = queries.shape[0]
     half = tokens // 2
     rows = H * half
     length = n * tokens
     return pl.pallas_call(
-        functools.partial(forward_kernel, masks, half),
+        functools.partial(forward_kernel, n, sources, count, half),
         out_shape=(
             jax.ShapeDtypeStruct((tokens, D), BF16),
             jax.ShapeDtypeStruct((2, 8, rows), F32),
             jax.ShapeDtypeStruct((2, rows, D), BF16),
         ),
-        in_specs=[SMEM, VMEM, VMEM, VMEM] + [ANY] * n,
+        in_specs=[SMEM, VMEM, VMEM, VMEM] + [ANY] * count,
         out_specs=(VMEM, VMEM, VMEM),
         scratch_shapes=[
             pltpu.VMEM((length, 2 * D), BF16),
@@ -234,25 +251,27 @@
             pltpu.SemaphoreType.DMA((2 * n,)),
         ],
         compiler_params=LIMIT,
+        cost_estimate=pl.CostEstimate(flops=10**10, bytes_accessed=8 * 2**20, transcendentals=2**20),
         name="attend",
     )(rank, queries, pre, post, *pieces)
 
 
-def attend_back(masks, rank, queries, grad_out, lse, pv, pieces, pre, post):
+def attend_back(sources, masks, rank, queries, grad_out, lse, pv, pieces, pre, post):
     n = len(masks)
+    count = len(pieces)
     tokens = queries.shape[0]
     half = tokens // 2
     rows = H * half
     length = n * tokens
     outs = pl.pallas_call(
-        functools.partial(backward_kernel, masks, half),
+        functools.partial(backward_kernel, n, sources, count, masks, half),
         out_shape=(
             jax.ShapeDtypeStruct((tokens, D), BF16),
             jax.ShapeDtypeStruct((H, D), F32),
             jax.ShapeDtypeStruct((H, D), F32),
         )
         + tuple(jax.ShapeDtypeStruct((tokens, 2 * D), BF16) for _ in masks),
-        in_specs=[SMEM] + [VMEM] * 6 + [ANY] * n,
+        in_specs=[SMEM] + [VMEM] * 6 + [ANY] * count,
         out_specs=(VMEM, VMEM, VMEM) + (ANY,) * n,
         scratch_shapes=[
             pltpu.VMEM((length, 2 * D), BF16),
@@ -265,6 +284,7 @@
             pltpu.SemaphoreType.DMA((2 * n,)),
         ],
         compiler_params=LIMIT,
+        cost_estimate=pl.CostEstimate(flops=16 * 10**9, bytes_accessed=12 * 2**20, transcendentals=2**20),
         name="attend_back",
     )(rank, queries, grad_out, lse, pv, pre, post, *pieces)
     return outs[0], outs[1], outs[2], outs[3:]
@@ -322,25 +342,63 @@
     ff = w_in.shape[2]
     sw = functools.partial(swap, count=count)
 
-    columns = []
-    for l in range(LAYERS):
-        inward = w_in[l].reshape(share, count, folds, share).transpose(0, 2, 1, 3).reshape(share, ff)
-        outward = w_back[l].reshape(folds, share, D).transpose(1, 0, 2).reshape(share, folds * D)
-        columns += [w_qkv[l], w_proj[l], inward, outward]
+    def packed_in(l):
+        return w_in[l].reshape(share, count, folds, share).transpose(0, 2, 1, 3).reshape(share, ff)
+
+    def packed_back(l):
+        return jnp.concatenate([w_back[l, a * share : (a + 1) * share] for a in range(folds)], axis=1)
+
     gains = jnp.stack([gain_attn[0], gain_ffn[0], gain_attn[1], gain_ffn[1]], axis=1)
-    columns.append(jnp.pad(gains, ((0, 0), (0, 124))))
-    weights = lax.all_gather(jnp.concatenate(columns, axis=1), AXES, axis=0, tiled=True)
-    width = 4 * D + 2 * ff
-
-    def layer_weights(l):
-        w = weights[:, l * width : (l + 1) * width]
-        outward = w[:, 4 * D + ff :].reshape(D, folds, D).transpose(1, 0, 2).reshape(ff, D)
-        gain = weights[:, LAYERS * width + 2 * l : LAYERS * width + 2 * l + 2].astype(F32)
-        return w[:, : 3 * D], w[:, 3 * D : 4 * D], w[:, 4 * D : 4 * D + ff], outward, gain[:, 0], gain[:, 1]
+    gains = jnp.pad(gains, ((0, 0), (0, 124)))
+    wide = [w_qkv[0], w_proj[0], gains]
+    pairs = [
+        jnp.concatenate(wide + [packed_in(0), packed_back(0)][:1], axis=1),
+        jnp.concatenate([packed_back(0), w_qkv[1], w_proj[1]], axis=1),
+        jnp.concatenate([packed_in(1), packed_back(1)], axis=1),
+    ]
+    borders = [4 * D + gains.shape[1], folds * D, ff]
+    routes = [geo.x_last, geo.y_last]
+    shared = len(geo.zs).bit_length() - 1
+    stages = len(geo.x_last) - 1
+    timed = stages == 4
+    split = [None] * len(pairs)
+    last_round = [None]
+
+    def begin_round(number, after, late=None):
+        pending = []
+        for p in range(len(pairs)):
+            k = number - 2 * p
+            if 0 <= k < shared:
+                pending.append((p, None, geo.x_last[k], pairs[p]))
+            elif shared <= k < stages:
+                if k == shared:
+                    split[p] = [pairs[p][:, : borders[p]], pairs[p][:, borders[p] :]]
+                pending += [(p, side, routes[side][k], split[p][side]) for side in range(2)]
+        values = [entry[3] for entry in pending]
+        if timed:
+            values = list(lax.optimization_barrier((values, after, last_round[0]))[0])
+            if late is not None:
+                values[late[0]], _ = lax.optimization_barrier((values[late[0]], late[1]))
+        arrived = [sw(value, entry[2]) for value, entry in zip(values, pending)]
+        last_round[0] = arrived
+        return pending, values, arrived
+
+    def end_round(state, hold):
+        pending, values, arrived = state
+        if timed and hold is not None:
+            arrived = lax.optimization_barrier((arrived, hold))[0]
+            last_round[0] = arrived
+        for value, there, (p, side, _, _) in zip(values, arrived, pending):
+            joined = jnp.concatenate([value, there], axis=0)
+            if side is None:
+                pairs[p] = joined
+            else:
+                split[p][side] = joined
 
     ids = token_ids.reshape(1, tokens)
-    ids = jnp.concatenate([ids] + [sw(ids, m) for m in range(1, n)], axis=0)
     ids = jnp.concatenate([ids] + [sw(ids, m * n) for m in range(1, geo.b)], axis=0)
+    first_ids = ids
+    ids = jnp.stack([ids] + [sw(ids, m) for m in range(1, n)], axis=1)
     target = me ^ jnp.array(geo.order, jnp.int32)
     t_seq = (target % n) // r
     t_rank = (target // n) * r + target % r
@@ -349,20 +407,147 @@
     ids = jnp.take(ids.reshape(2 * count, half), (source * 2 + halves % 2).reshape(-1), axis=0).reshape(-1)
 
     vocab = embedding.shape[0]
-    table = jnp.concatenate([embedding, sw(embedding, core)], axis=0)
     line = jnp.arange(vocab, dtype=jnp.int32)
-    names = jnp.concatenate([me * vocab + line, (me ^ core) * vocab + line])
-    near = ids[: ids.shape[0] // 2]
-    picked = mm((near[:, None] == names[None, :]).astype(BF16), table).astype(BF16)
-    picked = picked.reshape(len(geo.plane), -1, D)
-    row = picked[0]
-    for k in range(1, len(geo.plane)):
-        row = row + sw(picked[k], geo.plane[k])
+    table, first_ids = lax.optimization_barrier((embedding, first_ids))
+    tables = [table] + [sw(table, m) for m in geo.high[1:]]
+    tables = tables + [sw(part, core) for part in tables]
+    owners = geo.high + [m ^ core for m in geo.high]
+    end_round(begin_round(0, first_ids), None)
+    end_round(begin_round(1, first_ids), None)
+    third = begin_round(2, first_ids)
+    near = ids[: len(geo.low) * len(geo.zs) * tokens]
+    picked = jnp.zeros((near.shape[0], D), F32)
+    for m, part in zip(owners, tables):
+        picked = picked + mm((near[:, None] == ((me ^ m) * vocab + line)[None, :]).astype(BF16), part)
+    picked = picked.astype(BF16)
+    end_round(third, picked)
+    flat = picked.reshape(len(geo.low), -1, D)
+    row = flat[0]
+    for k in range(1, len(geo.low)):
+        row = row + sw(flat[k], geo.low[k])
+    fourth = begin_round(3, picked, (1, row))
     row = row.reshape(len(geo.zs), tokens, D)
     stream = row[0]
     for k in range(1, len(geo.zs)):
         stream = stream + sw(row[k], geo.zs[k])
     stream = stream.astype(F32)
+    end_round(fourth, stream)
+    fifth = begin_round(4, stream)
+    if not timed:
+        end_round(fifth, None)
+        for number in range(5, stages + 2 * len(pairs) - 2):
+            end_round(begin_round(number, None), None)
+
+    side = D // 2
+    feature = jnp.arange(D, dtype=jnp.int32)
+
+    def turner(route):
+        order = jnp.repeat(jnp.array(reached(route), jnp.int32), share)
+        origin = (me ^ order) * share + feature % share
+        return (feature[:, None] == origin[None, :]).astype(BF16)
+
+    turn_x, turn_y = turner(geo.x_last), turner(geo.y_last)
+
+    def relative(value, turn):
+        turned = mm(value, turn).astype(BF16)
+        return turned[:, :side], turned[:, side:]
+
+    def times(value, pair, start, width):
+        near, far = pair
+        return mm(value[0], near[:, start : start + width]) + mm(value[1], far[:, start : start + width])
+
+    def back_times(value, pair, start, width, turn):
+        near, far = pair
+        near, far = (mm_t(value, side[:, start : start + width]).astype(BF16) for side in (near, far))
+        return mm_t(jnp.concatenate([near, far], axis=1), turn)
+
+    def finish(p):
+        return [(value, sw(value, core)) for value in split[p]]
+
+    turns = [turn_x, turn_y]
+    attns, inwards, outwards = [None] * LAYERS, [None] * LAYERS, [None] * LAYERS
+    attns[0], inwards[0] = finish(0)
+    gain_all = jnp.concatenate([side[:, 4 * D : 4 * D + 8] for side in attns[0]], axis=0)
+    gain_all = mm(turn_x, gain_all).T
+
+    class Sum:
+        def __init__(self, value, route):
+            self.value = value
+            self.masks = list(route[:-2])
+
+        def outgoing(self):
+            if not self.masks:
+                return []
+            return [(self.value[self.value.shape[0] // 2 :], self.masks.pop())]
+
+        def incoming(self, arrived):
+            for there in arrived:
+                rows = self.value.shape[0] // 2
+                self.value = self.value[:rows].astype(F32) + there.astype(F32)
+                if self.masks:
+                    self.value = self.value.astype(BF16)
+
+        def step(self):
+            self.incoming([sw(value, mask) for value, mask in self.outgoing()])
+
+        def result(self):
+            while self.masks:
+                self.step()
+            return self.value
+
+    def exchange(after, sums, others=()):
+        entries = list(others)
+        spans = []
+        for one in sums:
+            out = one.outgoing()
+            spans.append(len(out))
+            entries += out
+        values = lax.optimization_barrier(([value for value, _ in entries], after))[0]
+        arrived = [sw(value, mask) for value, (_, mask) in zip(values, entries)]
+        arrived = list(lax.optimization_barrier(arrived))
+        place = len(others)
+        for one, span in zip(sums, spans):
+            one.incoming(arrived[place : place + span])
+            place += span
+        return arrived[: len(others)]
+
+    def tie(value, sums):
+        value, held_sums = lax.optimization_barrier((value, [one.value for one in sums]))
+        for one, held_sum in zip(sums, held_sums):
+            one.value = held_sum
+        return value
+
+    x_mask = geo.x_last[-2]
+    quarter = D // 4
+    quarters = [turn_x[:, k * quarter : (k + 1) * quarter] for k in range(4)]
+
+    rows_of = [
+        (i ^ (m // n)) * quarter + jnp.arange(quarter, dtype=jnp.int32) for m in (0, x_mask, core, x_mask ^ core)
+    ]
+    straight = [(feature[:, None] == rows[None, :]).astype(BF16) for rows in rows_of]
+
+    def four_rows(values, quarters):
+        tall = jnp.concatenate(values, axis=0)
+        stay, to_x, to_core, to_both = (mm(tall, q).astype(BF16) for q in quarters)
+        size = tall.shape[0]
+        from_x = sw(jnp.concatenate([to_x, to_both], axis=0), x_mask)
+        rest = sw(jnp.concatenate([to_core, from_x[size:]], axis=0), core)
+        spots = [slice(k * tokens, (k + 1) * tokens) for k in range(len(values))]
+        return [
+            jnp.concatenate([stay[s], from_x[:size][s], rest[:size][s], rest[size:][s]], axis=0) for s in spots
+        ]
+
+    def two_tokens(value):
+        return jnp.concatenate([value, sw(value, x_mask)], axis=0)
+
+    def four_tokens(value):
+        return jnp.concatenate([value, sw(value, core)], axis=0)
+
+    def side_by_side(parts):
+        return jnp.concatenate([part.astype(BF16) for part in parts], axis=1)
+
+    def fold(value, a):
+        return tuple(side[a * tokens : (a + 1) * tokens] for side in value)
 
     def half_moves(parity):
         moves = []
@@ -383,25 +568,59 @@
 
     near_masks = list(geo.plane)
     masks = [geo.rank_mask(m) for m in near_masks] + [geo.rank_mask(m ^ core) for m in near_masks]
+    if len(near_masks) == 4:
+        near_sources = [(k, part * half, m, part) for k, m in enumerate(masks[:3]) for part in range(2)]
+        near_sources += [(3, 0, masks[3], 0), (4, 0, masks[3], 1)]
+    else:
+        near_sources = [(k, part * half, m, part) for k, m in enumerate(masks[:n // 2]) for part in range(2)]
+    piece_count = near_sources[-1][0] + 1
+    sources = near_sources + [
+        (k + piece_count, row, m ^ geo.rank_mask(core), part) for k, row, m, part in near_sources
+    ]
+
     spread_pre = [jnp.repeat(mix_pre[l].T, E, axis=1) * E ** (-0.5) for l in range(LAYERS)]
     spread_post = [jnp.repeat(mix_post[l], E, axis=1) for l in range(LAYERS)]
 
+    def spread_keys(own):
+        if len(near_masks) == 4:
+            y, x = near_masks[1], near_masks[2]
+            by_y, by_x = sw(own, y), sw(own, x)
+            return [own, by_y, by_x, sw(by_x[:half], y), sw(by_y[half:], x)]
+        return [own] + [sw(own, m) for m in near_masks[1:]]
+
     saved = []
     for l in range(LAYERS):
-        qkv, proj, inward, outward, gain_a, gain_f = layer_weights(l)
+        gain_a, gain_f = gain_all[2 * l], gain_all[2 * l + 1]
+        turn = turns[l]
         n1 = (stream * norm_parts(stream) * gain_a).astype(BF16)
-        projected = mm(n1, qkv).astype(BF16)
+        projected = times(relative(n1, turn), attns[l], 0, 3 * D).astype(BF16)
         queries = projected[:, :D]
-        own = projected[:, D:]
-        pieces = [own] + [sw(own, m) for m in near_masks[1:]]
+        if timed and l == 0:
+            end_round(fifth, projected)
+            sixth = begin_round(5, projected)
+        pieces = spread_keys(projected[:, D:])
         pieces = pieces + [sw(piece, core) for piece in pieces]
-        attended, lse, pv = attend(masks, rank_arg, queries, pieces, spread_pre[l], spread_post[l])
-        middle = stream + mm(attended, proj)
+        attended, lse, pv = attend(n, sources, rank_arg, queries, pieces, spread_pre[l], spread_post[l])
+        if timed:
+            end_round(sixth if l == 0 else eighth, attended)
+        if l == 0:
+            if timed:
+                seventh = begin_round(6, attended)
+            outwards[0], attns[1] = finish(1)
+        else:
+            inwards[1], outwards[1] = finish(2)
+        middle = stream + times(relative(attended, turn), attns[l], 3 * D, D)
         n2 = (middle * norm_parts(middle) * gain_f).astype(BF16)
-        hidden = mm(n2, inward)
+        hidden = times(relative(n2, turns[1 - l]), inwards[l], 0, ff)
         active = jax.nn.gelu(hidden, approximate=True).astype(BF16)
-        saved.append((stream, n1, queries, pieces, attended, lse, pv, middle, n2, hidden, active))
-        stream = middle + mm(active, outward)
+        wide = relative(jnp.concatenate([active[:, a * D : (a + 1) * D] for a in range(folds)], axis=0), turns[l])
+        stream_in, stream = stream, middle
+        for a in range(folds):
+            stream = stream + times(fold(wide, a), outwards[l], a * D, D)
+        if timed and l == 0:
+            end_round(seventh, stream)
+            eighth = begin_round(7, stream)
+        saved.append((stream_in, n1, queries, pieces, attended, lse, pv, middle, n2, hidden, active, wide))
 
     final = stream.astype(BF16)
     back_even = [(b, a) for a, b in half_moves(0)]
@@ -414,76 +633,126 @@
 
     shares = [None] * LAYERS
     mixes = [None] * LAYERS
+    gain_grads = [None] * LAYERS
     for l in reversed(range(LAYERS)):
-        qkv, proj, inward, outward, gain_a, gain_f = layer_weights(l)
-        stream_in, n1, queries, pieces, attended, lse, pv, middle, n2, hidden, active = saved[l]
+        gain_a, gain_f = gain_all[2 * l], gain_all[2 * l + 1]
+        stream_in, n1, queries, pieces, attended, lse, pv, middle, n2, hidden, active, wide = saved[l]
         gf = grad_stream.astype(BF16)
-        back_grad = t_mm(active, gf)
         pull = jax.vjp(lambda z: jax.nn.gelu(z, approximate=True), hidden)[1]
-        gz = pull(mm_t(gf, outward))[0].astype(BF16)
-        in_grad = t_mm(n2, gz)
-        delta, gain_f_grad = norm_back(middle, gain_f, mm_t(gz, inward))
+        active_grad = [back_times(gf, outwards[l], a * D, D, turns[l]) for a in range(folds)]
+        gz = pull(jnp.concatenate(active_grad, axis=1))[0].astype(BF16)
+        normed_grad = back_times(gz, inwards[l], 0, ff, turns[1 - l])
+        gf_four = four_tokens(two_tokens(gf))
+        tall = four_rows([active[:, a * D : (a + 1) * D] for a in range(folds)] + [n2, attended], straight)
+        back_grad = [t_mm(part, gf_four) for part in tall[:folds]]
+        if l == 0:
+            (tall_n1,) = four_rows([n1], quarters)
+        else:
+            gz_two = two_tokens(gz)
+        delta, gain_f_grad = norm_back(middle, gain_f, normed_grad)
         middle_grad = grad_stream + delta
         gy = middle_grad.astype(BF16)
-        proj_grad = t_mm(attended, gy)
-        go = mm_t(gy, proj).astype(BF16)
+        go = back_times(gy, attns[l], 3 * D, D, turns[l]).astype(BF16)
+        if l == 0:
+            gz_two = two_tokens(jnp.concatenate([gz, gy], axis=1))
+            go, attn_grad, back_grad = lax.optimization_barrier((go, attn_grad, back_grad))
         gq, pre_grad, post_grad, parts = attend_back(
-            masks, rank_arg, queries, go, lse, pv, pieces, spread_pre[l], spread_post[l]
+            sources, masks, rank_arg, queries, go, lse, pv, pieces, spread_pre[l], spread_post[l]
         )
         mixes[l] = (pre_grad, post_grad)
         size = len(near_masks)
         sums = [parts[k].astype(F32) + sw(parts[size + k], core).astype(F32) for k in range(size)]
+        others = [(sums[k].astype(BF16), near_masks[k]) for k in range(1, size)]
+        arrived = [sw(value, mask) for value, mask in others]
+        gz_two, _ = lax.optimization_barrier((gz_two, sums))
+        gz_four = four_tokens(gz_two)
+        if l == 0:
+            pack = attn_grad + back_grad + [t_mm(tall[folds], gz_four[:, :ff]), t_mm(tall[folds + 1], gz_four[:, ff:])]
+        else:
+            pack = back_grad + [t_mm(tall[folds], gz_four)]
+        pack = side_by_side(pack)
+        pack, arrived = lax.optimization_barrier((pack, arrived))
+        shares[l] = lax.psum_scatter(pack, "seq", scatter_dimension=0, tiled=True)
+        if l == 0:
+            shares[1], arrived = lax.optimization_barrier((shares[1], arrived))
         kv_grad = sums[0]
-        for k in range(1, size):
-            kv_grad = kv_grad + sw(sums[k].astype(BF16), near_masks[k]).astype(F32)
+        for there in arrived:
+            kv_grad = kv_grad + there.astype(F32)
         joint = jnp.concatenate([gq, kv_grad.astype(BF16)], axis=1)
-        qkv_grad = t_mm(n1, joint)
-        delta, gain_a_grad = norm_back(stream_in, gain_a, mm_t(joint, qkv))
+        normed_grad = back_times(joint, attns[l], 0, 3 * D, turns[l])
+        if l == 0:
+            joint_zero = joint
+        else:
+            both = four_tokens(two_tokens(jnp.concatenate([joint, gy], axis=1)))
+            (tall_n1,) = four_rows([n1], straight)
+            attn_grad = [t_mm(tall_n1, both[:, : 3 * D]), t_mm(tall[folds + 1], both[:, 3 * D :])]
+        delta, gain_a_grad = norm_back(stream_in, gain_a, normed_grad)
         grad_stream = middle_grad + delta
-        back_cols = back_grad.reshape(folds, D, D)
-        gain_cols = jnp.pad(jnp.stack([gain_a_grad, gain_f_grad], axis=1), ((0, 0), (0, 126)))
-        packed = jnp.concatenate(
-            [qkv_grad.astype(BF16), proj_grad.astype(BF16), in_grad.astype(BF16)]
-            + [back_cols[a].astype(BF16) for a in range(folds)]
-            + [gain_cols.astype(BF16)],
-            axis=1,
-        )
-        shares[l] = lax.psum_scatter(packed, AXES, scatter_dimension=0, tiled=True).astype(F32)
+        gain_grads[l] = (gain_a_grad, gain_f_grad)
+
+    pre_sum = jnp.stack([mixes[l][0] for l in range(LAYERS)]).reshape(LAYERS, H, H, E).sum(-1)
+    post_sum = jnp.stack([mixes[l][1] for l in range(LAYERS)]).reshape(LAYERS, H, H, E).sum(-1)
+    small = jnp.concatenate(
+        [(pre_sum.transpose(0, 2, 1) * E ** (-0.5)).reshape(-1), post_sum.reshape(-1)]
+        + [gain_grads[l][k] for k in range(2) for l in range(LAYERS)]
+    )
+    size = small.shape[0]
+    small = jnp.pad(small, (0, -size % 1024)).reshape(-1, 128)
+    small_masks = bits(1, count)
 
     g0 = grad_stream.astype(BF16)
-    rows = jnp.concatenate([g0] + [sw(g0, m) for m in geo.zs[1:]], axis=0)
-    blocks = [rows] + [sw(rows, m) for m in geo.plane[1:]]
+    arrived = exchange(g0, [], [(joint_zero, x_mask)] + [(g0, m) for m in geo.zs[1:]])
+    joint_four = four_tokens(jnp.concatenate([joint_zero, arrived[0]], axis=0))
+    qkv_sum = Sum(t_mm(tall_n1, joint_four).astype(BF16), geo.x_last)
+    rows = jnp.concatenate([g0] + arrived[1:], axis=0)
+    if len(geo.plane) == 4:
+        cut = rows.shape[0] // 2
+        y, x = geo.plane[1], geo.plane[2]
+        by_y, by_x = exchange(rows, [], [(rows, y), (rows, x)])
+        both = exchange(by_x, [qkv_sum], [(by_x[:cut], y), (by_y[cut:], x)])
+        blocks = [rows, by_y, by_x] + both
+    else:
+        blocks = [rows] + exchange(rows, [], [(rows, m) for m in geo.plane[1:]])
+        exchange(blocks[-1], [qkv_sum])
     blocks = blocks + [sw(block, core) for block in blocks]
+
+    def share_small(after, sums):
+        nonlocal small
+        (there,) = exchange(after, sums, [(small, small_masks.pop())])
+        small = small + there
+
+    share_small(blocks, [qkv_sum])
     own_names = me * vocab + line
     embedding_grad = mm(
         (own_names[:, None] == ids[None, :]).astype(BF16), jnp.concatenate(blocks, axis=0)
     )
-
-    pre_sum = jnp.stack([mixes[l][0] for l in range(LAYERS)]).reshape(LAYERS, H, H, E).sum(-1)
-    post_sum = jnp.stack([mixes[l][1] for l in range(LAYERS)]).reshape(LAYERS, H, H, E).sum(-1)
-    mix = jnp.stack([pre_sum.transpose(0, 2, 1) * E ** (-0.5), post_sum])
-    bit = 1
-    while bit < count:
-        mix = mix + sw(mix, bit)
-        bit *= 2
-
-    def in_order(packed):
-        part = packed[:, 4 * D : 4 * D + ff]
+    share_small(qkv_sum.value, [qkv_sum])
+    while small_masks:
+        share_small(qkv_sum.value, [])
+    small = small.reshape(-1)[:size]
+    mix = small[: 2 * LAYERS * H * H].reshape(2, LAYERS, H, H)
+    gain_sum = small[2 * LAYERS * H * H :].reshape(2, LAYERS, D)
+    gain_sum = lax.dynamic_slice(gain_sum, (0, 0, me * share), (2, LAYERS, share))
+
+    def in_order(part):
         return part.reshape(share, folds, count, share).transpose(0, 2, 1, 3).reshape(share, ff)
 
-    def back_order(packed):
-        part = packed[:, 4 * D + ff : width]
-        return part.reshape(share, folds, D).transpose(1, 0, 2).reshape(back_share, D)
-
+    def back_order(part):
+        return jnp.concatenate([part[:, a * D : (a + 1) * D] for a in range(folds)], axis=0)
+
+    qkv_share = qkv_sum.result()
+    one, zero = shares[1].astype(F32), shares[0].astype(F32)
+    attn_share, zero = zero[:, : 4 * D], zero[:, 4 * D :]
+    width = folds * D
     return (
         output,
         embedding_grad,
-        jnp.stack([s[:, width] for s in shares]),
-        jnp.stack([s[:, : 3 * D] for s in shares]),
-        jnp.stack([s[:, 3 * D : 4 * D] for s in shares]),
-        jnp.stack([s[:, width + 1] for s in shares]),
-        jnp.stack([in_order(s) for s in shares]),
-        jnp.stack([back_order(s) for s in shares]),
+        gain_sum[0],
+        jnp.stack([qkv_share, attn_share[:, : 3 * D]]),
+        jnp.stack([zero[:, width + ff :], attn_share[:, 3 * D :]]),
+        gain_sum[1],
+        jnp.stack([in_order(zero[:, width : width + ff]), in_order(one[:, width:])]),
+        jnp.stack([back_order(zero[:, :width]), back_order(one[:, :width])]),
         mix[0],
         mix[1],
     )

time: 820 us -> 676 us (0.82)
  waiting for transfers between devices: 450 us -> 211 us
  matrix products: 97.8 us -> 134 us
  starting transfers between devices: 64.9 us -> 92.9 us
  other arithmetic: 31.5 us -> 54.4 us
    unnamed x5 -> x2, waiting for transfers between devices: 172 us -> 0.04 us
    all_gather x1 -> x0, waiting for transfers between devices: 74.1 us -> none  [shards(): lax.all_gather(jnp.concatenate(columns, axis=1), AXES, axis=0, tiled=True)]
    ppermute x60 -> x113, waiting for transfers between devices: 178 us -> 211 us  [swap(): return lax.ppermute(value, AXES, [(p, p ^ mask) for p in range(count)])]
    ppermute x60 -> x113, starting transfers between devices: 55.9 us -> 87.4 us  [swap(): return lax.ppermute(value, AXES, [(p, p ^ mask) for p in range(count)])]
    dot_general x10 -> x58, matrix products: 41.3 us -> 68.6 us  [mm(): return jnp.dot(a, b, preferred_element_type=F32)]
    ppermute x1, waiting for transfers between devices: 26.1 us -> 0.01 us  [shards(): lax.ppermute(second, AXES, back_odd)]
    concatenate x2 -> x30, other arithmetic: 0.13 us -> 26 us  [the longest x9 8.69 us: end_round(): joined = jnp.concatenate([value, there], axis=0)]
    concatenate x5 -> x15, local copies, waits for them, and re-layouts: 1.54 us -> 15.1 us  [the longest x9 14.2 us: end_round(): joined = jnp.concatenate([value, there], axis=0)]
  transfers between devices with their start and end apart: 67 -> 119, of which waited for: 28 -> 41; matrix products, arithmetic and copies ran while one was open for 18% -> 38% of each run, Pallas kernels for 4% -> 9%
where the time goes in v2:
time: 676 us; the launch traced here: 664 us
  waiting for transfers between devices  211 us (31%)
  matrix products  134 us (20%)
  local copies, waits for them, and re-layouts  94.5 us (14%)
  starting transfers between devices  92.9 us (14%)
  Pallas kernels  60.1 us (9%)
  other arithmetic  54.4 us (8%)
  between operations  17.6 us (3%)
    ppermute x113, waiting for transfers between devices, swap(): return lax.ppermute(value, AXES, [(p, p ^ mask) for p in range(count)])  211 us
    ppermute x113, starting transfers between devices, swap(): return lax.ppermute(value, AXES, [(p, p ^ mask) for p in range(count)])  87.4 us
    dot_general x58, matrix products, mm(): return jnp.dot(a, b, preferred_element_type=F32)  68.6 us
    dot_general x42, matrix products, mm_t(): lax.dot_general(a, b, (((1,), (1,)), ((), ())), preferred_element_type=F32)  38.4 us
    unnamed x405, local copies, waits for them, and re-layouts  36.7 us
    pallas_call x2, Pallas kernels, attend_back(): pl.pallas_call(functools.partial(backward_kernel, n, sources, count, mask...  36.6 us
    dot_general x14, matrix products, t_mm(): lax.dot_general(a, b, (((0,), (0,)), ((), ())), preferred_element_type=F32)  26.7 us
    pallas_call x2, Pallas kernels, attend(): pl.pallas_call(functools.partial(forward_kernel, n, sources, count, half)...  23.4 us
  transfers between devices with their start and end apart: 119, of which 41 were waited for; matrix products, arithmetic and copies ran while one was open for 38% of the time, Pallas kernels for 9%

profile of v2, /device:TPU:0, one launch (start us, length us, event | category | flops | bytes accessed | tf_op | source)
XLA Modules:
  0.0 664.0 jit_solution(9377306515446047917)
XLA Ops:
  7.7 2.6 collective-permute-start.1
  12.0 3.1 collective-permute-start.62
  36.2 4.6 collective-permute-start.4
  40.9 2.9 collective-permute-start.6
  46.9 2.4 collective-permute-start.9
  50.7 2.5 collective-permute-done.9
  54.0 3.3 fusion.10
  58.8 7.9 %collective-permute-done.17 = bf16[24,6272]{1,0:T(8,128)(2,1)S(1)} collective-permute-done((bf16[24,6272]{1,0:T(8,128)(2,1)S(1)}, bf16[24,6272]{1,0:T(8,128)(2,1)S(1)}, u32[]{:S(2)}, u32[]{:S(2)}) %collective-permute-start.17) | collective-permute-done | bytes 301088 | tf_op jit(solution)/shard_map/ppermute | solution.py:63
  66.8 18.4 %collective-permute-done.10 = bf16[1004,768]{1,0:T(8,128)(2,1)} collective-permute-done((bf16[1004,768]{1,0:T(8,128)(2,1)}, bf16[1004,768]{1,0:T(8,128)(2,1)}, u32[]{:S(2)}, u32[]{:S(2)}) %collective-permute-start.10) | collective-permute-done | bytes 1542176 | tf_op jit(solution)/shard_map/ppermute | solution.py:63
  87.6 3.3 fusion.8
  91.2 3.7 fusion.6
  98.9 7.1 %collective-permute-done.21 = bf16[24,6144]{1,0:T(8,128)(2,1)S(1)} collective-permute-done((bf16[24,6144]{1,0:T(8,128)(2,1)S(1)}, bf16[24,6144]{1,0:T(8,128)(2,1)S(1)}, u32[]{:S(2)}, u32[]{:S(2)}) %collective-permute-start.21) | collective-permute-done | bytes 294944 | tf_op jit(solution)/shard_map/ppermute | solution.py:63
  107.9 10.7 %collective-permute-done.13 = bf16[512,768]{1,0:T(8,128)(2,1)S(1)} collective-permute-done((bf16[512,768]{1,0:T(8,128)(2,1)S(1)}, bf16[512,768]{1,0:T(8,128)(2,1)S(1)}, u32[]{:S(2)}, u32[]{:S(2)}) %collective-permute-start.13) | collective-permute-done | bytes 786464 | tf_op jit(solution)/shard_map/ppermute | solution.py:63
  130.8 12.6 %collective-permute-done.15 = bf16[128,768]{1,0:T(8,128)(2,1)S(1)} collective-permute-done((bf16[128,768]{1,0:T(8,128)(2,1)}, bf16[128,768]{1,0:T(8,128)(2,1)S(1)}, u32[]{:S(2)}, u32[]{:S(2)}) %collective-permute-start.15) | collective-permute-done | bytes 196640 | tf_op jit(solution)/shard_map/ppermute | solution.py:63
  143.4 4.6 collective-permute-done.16
  149.7 2.6 constant_dynamic-update-slice_fusion.16
  173.7 3.6 collective-permute-done.38
  182.7 2.4 constant_dynamic-update-slice_fusion.30
  185.1 2.5 constant_dynamic-update-slice_fusion.28
  196.6 2.4 collective-permute-done.28.rest_3_
  204.8 11.9 %attend.2 = (bf16[128,768]{1,0:T(8,128)(2,1)}, f32[2,8,768]{2,1,0:T(8,128)}, bf16[2,768,768]{2,1,0:T(8,128)(2,1)}) custom-call(s32[1]{0:T(128)} %bitcast.11.rank_ref, bf16[128,768]{1,0:T(8,128)(2,1)} %slice.1008.q_ref, f32[12,768]{1,0:T(8,128)} %mul.527.pre_ref, f32[12,768]{1,0:T(8,128)} %reshape.407.post_ref, bf16[128,1536]{1,0:T(8,128)(2,1)} %copy-done.67, ...), custom_call_target="tpu_custom_call" | custom-call | flops 10000000000 | bytes 8388608 | tf_op jit(solution)/shard_map/attend/pallas_call | solution.py:235
  223.7 2.2 multiply_convert_fusion.1
  238.9 4.3 collective-permute-done.80
  254.5 5.1 collective-permute-done.53
  263.9 2.4 constant_dynamic-update-slice_fusion.36
  272.0 2.3 collective-permute-done.46.rest_3_
  280.8 11.6 %attend.3 = (bf16[128,768]{1,0:T(8,128)(2,1)}, f32[2,8,768]{2,1,0:T(8,128)}, bf16[2,768,768]{2,1,0:T(8,128)(2,1)}) custom-call(s32[1]{0:T(128)} %bitcast.11.rank_ref, bf16[128,768]{1,0:T(8,128)(2,1)} %slice.1046.q_ref, f32[12,768]{1,0:T(8,128)} %mul.549.pre_ref, f32[12,768]{1,0:T(8,128)} %reshape.409.post_ref, bf16[128,1536]{1,0:T(8,128)(2,1)} %copy-done.68, ...), custom_call_target="tpu_custom_call" | custom-call | flops 10000000000 | bytes 8388608 | tf_op jit(solution)/shard_map/attend/pallas_call | solution.py:235
  292.4 12.3 %collective-permute-done.55 = bf16[192,3072]{1,0:T(8,128)(2,1)} collective-permute-done((bf16[192,3072]{1,0:T(8,128)(2,1)}, bf16[192,3072]{1,0:T(8,128)(2,1)}, u32[]{:S(2)}, u32[]{:S(2)}) %collective-permute-start.55) | collective-permute-done | bytes 1179680 | tf_op jit(solution)/shard_map/ppermute | solution.py:63
  305.6 2.4 constant_dynamic-update-slice_fusion.35
  337.2 18.1 %attend_back.2 = (bf16[128,768]{1,0:T(8,128)(2,1)}, f32[12,768]{1,0:T(8,128)}, f32[12,768]{1,0:T(8,128)}, bf16[128,1536]{1,0:T(8,128)(2,1)}, bf16[128,1536]{1,0:...) custom-call(s32[1]{0:T(128)} %bitcast.11.rank_ref, ...), custom_call_target="tpu_custom_call" | custom-call | flops 16000000000 | bytes 12582912 | tf_op jit(solution)/shard_map/attend_back/pallas_call | solution.py:266
  367.6 12.7 %collective-permute-done.64 = bf16[1536,192]{0,1:T(8,128)(2,1)S(1)} collective-permute-done((bf16[1536,192]{0,1:T(8,128)(2,1)S(1)}, bf16[1536,192]{0,1:T(8,128)(2,1)S(1)}, u32[]{:S(2)}, u32[]{:S(2)}) %collective-permute-start.64) | collective-permute-done | bytes 589856 | tf_op jit(solution)/shard_map/ppermute | solution.py:63
  446.1 8.4 %collective-permute-done.85 = bf16[128,3840]{1,0:T(8,128)(2,1)} collective-permute-done((bf16[128,3840]{1,0:T(8,128)(2,1)S(1)}, bf16[128,3840]{1,0:T(8,128)(2,1)}, u32[]{:S(2)}, u32[]{:S(2)}) %collective-permute-start.85) | collective-permute-done | bytes 983072 | tf_op jit(solution)/shard_map/ppermute | solution.py:63
  457.4 4.8 pad_maximum_fusion
  465.2 18.5 %attend_back.3 = (bf16[128,768]{1,0:T(8,128)(2,1)}, f32[12,768]{1,0:T(8,128)}, f32[12,768]{1,0:T(8,128)}, bf16[128,1536]{1,0:T(8,128)(2,1)}, bf16[128,1536]{1,0:...) custom-call(s32[1]{0:T(128)} %bitcast.11.rank_ref, ...), custom_call_target="tpu_custom_call" | custom-call | flops 16000000000 | bytes 12582912 | tf_op jit(solution)/shard_map/attend_back/pallas_call | solution.py:266
  499.1 4.6 collective-permute-done.92
  503.7 7.7 %collective-permute-done.91 = bf16[128,1536]{1,0:T(8,128)(2,1)S(1)} collective-permute-done((bf16[128,1536]{1,0:T(8,128)(2,1)}, bf16[128,1536]{1,0:T(8,128)(2,1)S(1)}, u32[]{:S(2)}, u32[]{:S(2)}) %collective-permute-start.91) | collective-permute-done | bytes 393248 | tf_op jit(solution)/shard_map/ppermute | solution.py:63
  525.6 2.5 collective-permute-start.96
  528.8 5.6 collective-permute-done.94
  535.4 8.5 %collective-permute-done.95 = bf16[128,768]{1,0:T(8,128)(2,1)S(1)} collective-permute-done((bf16[128,768]{1,0:T(8,128)(2,1)S(1)}, bf16[128,768]{1,0:T(8,128)(2,1)S(1)}, u32[]{:S(2)}, u32[]{:S(2)}) %collective-permute-start.95) | collective-permute-done | bytes 196640 | tf_op jit(solution)/shard_map/ppermute | solution.py:63
  549.6 3.2 collective-permute-start.98
  556.2 2.6 stack_reshape.7
  559.7 13.8 %collective-permute-done.97 = bf16[512,768]{1,0:T(8,128)(2,1)} collective-permute-done((bf16[512,768]{1,0:T(8,128)(2,1)}, bf16[512,768]{1,0:T(8,128)(2,1)}, u32[]{:S(2)}, u32[]{:S(2)}) %collective-permute-start.97) | collective-permute-done | bytes 786464 | tf_op jit(solution)/shard_map/ppermute | solution.py:63
  583.7 24.6 %collective-permute-done.102 = bf16[256,768]{1,0:T(8,128)(2,1)S(1)} collective-permute-done((bf16[256,768]{1,0:T(8,128)(2,1)S(1)}, bf16[256,768]{1,0:T(8,128)(2,1)S(1)}, u32[]{:S(2)}, u32[]{:S(2)}) %collective-permute-start.102) | collective-permute-done | bytes 393248 | tf_op jit(solution)/shard_map/ppermute | solution.py:63
  613.1 3.3 collective-permute-done.110
  616.4 2.7 collective-permute-done.111
  622.0 4.8 collective-permute-done.113
  626.9 5.3 collective-permute-done.114
  632.3 8.5 %fusion = f32[1004,768]{1,0:T(8,128)} fusion(bf16[4096,768]{1,0:T(8,128)(2,1)S(1)} %constant_dynamic-update-slice_fusion.51, s32[4096]{0:T(1024)S(1)} %copy-done.130, s32[1004]{0:T(1024)S(1)} %copy-done.138), kind=kOutput, calls=%fused_computation.1 | convolution fusion | flops 6320734208 | bytes 9396144 | tf_op jit(solution)/shard_map/dot_general | solution.py:294
  (932 shorter events, 328.6 us)
Async XLA Ops:
  7.2 504.5 %reduce-scatter.3.cloned.1.call-start = ((), (), s32[]{:S(2)}) async-start(), calls=%async_computation.2 | async-start | bytes 2654208 | tf_op jit(solution)/shard_map/reduce_scatter | solution.py:675
  7.2 27.3 %collective-permute-start = (s32[1,128]{1,0:T(1,128)}, s32[1,128]{1,0:T(1,128)S(1)}, u32[]{:S(2)}, u32[]{:S(2)}) collective-permute-start(s32[1,128]{1,0:T(1,128)} %param.14), channel_id=1, source_target_pairs={{0,8},{1,9},{2,10},{3,11},{4,12},{5,13},{6,14},{7,15},{8,0},{9,1},... | collective-permute-start | bytes 1544 | tf_op jit(solution)/shard_map/ppermute | solution.py:63
  7.7 26.8 %collective-permute-start.1 = (s32[1,128]{1,0:T(1,128)}, s32[1,128]{1,0:T(1,128)S(1)}, u32[]{:S(2)}, u32[]{:S(2)}) collective-permute-start(s32[1,128]{1,0:T(1,128)} %param.14), channel_id=1, source_target_pairs={{0,16},{1,17},{2,18},{3,19},{4,20},{5,21},{6,22},{7,23},{8,24},{9,... | collective-permute-start | bytes 1544 | tf_op jit(solution)/shard_map/ppermute | solution.py:63
  10.3 24.2 %collective-permute-start.2 = (s32[1,128]{1,0:T(1,128)}, s32[1,128]{1,0:T(1,128)S(1)}, u32[]{:S(2)}, u32[]{:S(2)}) collective-permute-start(s32[1,128]{1,0:T(1,128)} %param.14), channel_id=1, source_target_pairs={{0,24},{1,25},{2,26},{3,27},{4,28},{5,29},{6,30},{7,31},{8,16},{9,... | collective-permute-start | bytes 1544 | tf_op jit(solution)/shard_map/ppermute | solution.py:63
  11.3 46.0 %collective-permute-start.61 = (bf16[64,768]{1,0:T(8,128)(2,1)S(1)}, bf16[64,768]{1,0:T(8,128)(2,1)S(1)}, u32[]{:S(2)}, u32[]{:S(2)}) collective-permute-start(bf16[64,768]{1,0:T(8,128)(2,1)S(1)} %get-tuple-element.372), channel_id=1, source_target_pairs={{0,0},{1,8},{2,16},{3,24},{4,25},{5,17},{6,9},{7,1},{8,2},{9,10},{... | collective-permute-start | bytes 294920 | tf_op jit(solution)/shard_map/ppermute | solution.py:562
  12.0 45.3 %collective-permute-start.62 = (bf16[64,768]{1,0:T(8,128)(2,1)S(1)}, bf16[64,768]{1,0:T(8,128)(2,1)S(1)}, u32[]{:S(2)}, u32[]{:S(2)}) collective-permute-start(bf16[64,768]{1,0:T(8,128)(2,1)S(1)} %get-tuple-element.373), channel_id=1, source_target_pairs={{0,1},{1,9},{2,17},{3,25},{4,24},{5,16},{6,8},{7,0},{8,3},{9,11},{... | collective-permute-start | bytes 294920 | tf_op jit(solution)/shard_map/ppermute | solution.py:563
  49.3 35.9 %collective-permute-start.10 = (bf16[1004,768]{1,0:T(8,128)(2,1)}, bf16[1004,768]{1,0:T(8,128)(2,1)}, u32[]{:S(2)}, u32[]{:S(2)}) collective-permute-start(bf16[1004,768]{1,0:T(8,128)(2,1)} %param.15), channel_id=1, source_target_pairs={{0,16},{1,17},{2,18},{3,19},{4,20},{5,21},{6,22},{7,23},{8,24},{9,... | collective-permute-start | bytes 4626440 | tf_op jit(solution)/shard_map/ppermute | solution.py:63
  50.7 40.2 %collective-permute-start.11 = (bf16[1004,768]{1,0:T(8,128)(2,1)}, bf16[1004,768]{1,0:T(8,128)(2,1)}, u32[]{:S(2)}, u32[]{:S(2)}) collective-permute-start(bf16[1004,768]{1,0:T(8,128)(2,1)} %param.15), channel_id=1, source_target_pairs={{0,8},{1,9},{2,10},{3,11},{4,12},{5,13},{6,14},{7,15},{8,0},{9,1},... | collective-permute-start | bytes 4626440 | tf_op jit(solution)/shard_map/ppermute | solution.py:63
  57.4 64.0 %collective-permute-start.66 = (bf16[128,768]{1,0:T(8,128)(2,1)S(1)}, bf16[128,768]{1,0:T(8,128)(2,1)}, u32[]{:S(2)}, u32[]{:S(2)}) collective-permute-start(bf16[128,768]{1,0:T(8,128)(2,1)S(1)} %maximum_select_fusion), channel_id=1, source_target_pairs={{0,16},{1,17},{2,18},{3,19},{4,20},{5,21},{6,22},{7,23},{8,24},{9,... | collective-permute-start | bytes 589832 | tf_op jit(solution)/shard_map/ppermute | solution.py:63
  85.4 20.6 %collective-permute-start.19 = (bf16[96,3200]{1,0:T(8,128)(2,1)S(1)}, bf16[96,3200]{1,0:T(8,128)(2,1)S(1)}, u32[]{:S(2)}, u32[]{:S(2)}) collective-permute-start(bf16[96,3200]{1,0:T(8,128)(2,1)S(1)} %slice.999), channel_id=1, source_target_pairs={{0,1},{1,0},{2,3},{3,2},{4,5},{5,4},{6,7},{7,6},{8,9},{9,8},{10,11... | collective-permute-start | bytes 1843208 | tf_op jit(solution)/shard_map/ppermute | solution.py:63
  86.0 20.0 %collective-permute-start.20 = (bf16[96,3072]{1,0:T(8,128)(2,1)S(1)}, bf16[96,3072]{1,0:T(8,128)(2,1)S(1)}, u32[]{:S(2)}, u32[]{:S(2)}) collective-permute-start(bf16[96,3072]{1,0:T(8,128)(2,1)S(1)} %slice.1000), channel_id=1, source_target_pairs={{0,16},{1,17},{2,18},{3,19},{4,20},{5,21},{6,22},{7,23},{8,24},{9,... | collective-permute-start | bytes 1769480 | tf_op jit(solution)/shard_map/ppermute | solution.py:63
  97.2 21.3 %collective-permute-start.13 = (bf16[512,768]{1,0:T(8,128)(2,1)S(1)}, bf16[512,768]{1,0:T(8,128)(2,1)S(1)}, u32[]{:S(2)}, u32[]{:S(2)}) collective-permute-start(bf16[512,768]{1,0:T(8,128)(2,1)S(1)} %slice.994), channel_id=1, source_target_pairs={{0,1},{1,0},{2,3},{3,2},{4,5},{5,4},{6,7},{7,6},{8,9},{9,8},{10,11... | collective-permute-start | bytes 2359304 | tf_op jit(solution)/shard_map/ppermute | solution.py:63
  107.0 42.7 %collective-permute-start.22 = (bf16[192,3200]{1,0:T(8,128)(2,1)S(1)}, bf16[192,3200]{1,0:T(8,128)(2,1)}, u32[]{:S(2)}, u32[]{:S(2)}) collective-permute-start(bf16[192,3200]{1,0:T(8,128)(2,1)S(1)} %pad_maximum_fusion.6), channel_id=1, source_target_pairs={{0,16},{1,17},{2,18},{3,19},{4,20},{5,21},{6,22},{7,23},{8,24},{9,... | collective-permute-start | bytes 3686408 | tf_op jit(solution)/shard_map/ppermute | solution.py:63
  118.6 31.1 %collective-permute-start.23 = (bf16[192,3072]{1,0:T(8,128)(2,1)S(1)}, bf16[192,3072]{1,0:T(8,128)(2,1)}, u32[]{:S(2)}, u32[]{:S(2)}) collective-permute-start(bf16[192,3072]{1,0:T(8,128)(2,1)S(1)} %pad_maximum_fusion.7), channel_id=1, source_target_pairs={{0,1},{1,0},{2,3},{3,2},{4,5},{5,4},{6,7},{7,6},{8,9},{9,8},{10,11... | collective-permute-start | bytes 3538952 | tf_op jit(solution)/shard_map/ppermute | solution.py:63
  123.1 26.6 %collective-permute-start.24 = (bf16[48,6144]{1,0:T(8,128)(2,1)}, bf16[48,6144]{1,0:T(8,128)(2,1)S(1)}, u32[]{:S(2)}, u32[]{:S(2)}) collective-permute-start(bf16[48,6144]{1,0:T(8,128)(2,1)} %pad_maximum_fusion.19), channel_id=1, source_target_pairs={{0,2},{1,3},{2,0},{3,1},{4,6},{5,7},{6,4},{7,5},{8,10},{9,11},{10,... | collective-permute-start | bytes 1769480 | tf_op jit(solution)/shard_map/ppermute | solution.py:63
  128.0 20.0 %collective-permute-start.16 = (bf16[128,768]{1,0:T(8,128)(2,1)}, bf16[128,768]{1,0:T(8,128)(2,1)S(1)}, u32[]{:S(2)}, u32[]{:S(2)}) collective-permute-start(bf16[128,768]{1,0:T(8,128)(2,1)} %get-tuple-element.304), channel_id=1, source_target_pairs={{0,6},{1,7},{2,4},{3,5},{4,2},{5,3},{6,0},{7,1},{8,14},{9,15},{10,... | collective-permute-start | bytes 589832 | tf_op jit(solution)/shard_map/ppermute | solution.py:63
  172.4 19.4 %collective-permute-start.27 = (bf16[128,1536]{1,0:T(8,128)(2,1)S(1)}, bf16[128,1536]{1,0:T(8,128)(2,1)S(1)}, u32[]{:S(2)}, u32[]{:S(2)}) collective-permute-start(bf16[128,1536]{1,0:T(8,128)(2,1)S(1)} %slice.1009.rest_0_), channel_id=1, source_target_pairs={{0,16},{1,17},{2,18},{3,19},{4,20},{5,21},{6,22},{7,23},{8,24},{9,... | collective-permute-start | bytes 1179656 | tf_op jit(solution)/shard_map/ppermute | solution.py:63
  172.9 19.6 %collective-permute-start.26 = (bf16[128,1536]{1,0:T(8,128)(2,1)S(1)}, bf16[128,1536]{1,0:T(8,128)(2,1)S(1)}, u32[]{:S(2)}, u32[]{:S(2)}) collective-permute-start(bf16[128,1536]{1,0:T(8,128)(2,1)S(1)} %slice.1009.rest_0_), channel_id=1, source_target_pairs={{0,1},{1,0},{2,3},{3,2},{4,5},{5,4},{6,7},{7,6},{8,9},{9,8},{10,11... | collective-permute-start | bytes 1179656 | tf_op jit(solution)/shard_map/ppermute | solution.py:63
  196.1 26.1 %collective-permute-start.35 = (bf16[384,3072]{1,0:T(8,128)(2,1)S(1)}, bf16[384,3072]{1,0:T(8,128)(2,1)S(1)}, u32[]{:S(2)}, u32[]{:S(2)}) collective-permute-start(bf16[384,3072]{1,0:T(8,128)(2,1)S(1)} %constant_dynamic-update-slice_fusion.18), channel_id=1, source_target_pairs={{0,8},{1,9},{2,10},{3,11},{4,12},{5,13},{6,14},{7,15},{8,0},{9,1},... | collective-permute-start | bytes 7077896 | tf_op jit(solution)/shard_map/ppermute | solution.py:63
  201.0 30.7 %collective-permute-start.39 = (bf16[192,3072]{1,0:T(8,128)(2,1)}, bf16[192,3072]{1,0:T(8,128)(2,1)}, u32[]{:S(2)}, u32[]{:S(2)}) collective-permute-start(bf16[192,3072]{1,0:T(8,128)(2,1)} %pad_maximum_fusion.8), channel_id=1, source_target_pairs={{0,16},{1,17},{2,18},{3,19},{4,20},{5,21},{6,22},{7,23},{8,24},{9,... | collective-permute-start | bytes 3538952 | tf_op jit(solution)/shard_map/ppermute | solution.py:63
  202.1 29.6 %collective-permute-start.40 = (bf16[192,3072]{1,0:T(8,128)(2,1)}, bf16[192,3072]{1,0:T(8,128)(2,1)}, u32[]{:S(2)}, u32[]{:S(2)}) collective-permute-start(bf16[192,3072]{1,0:T(8,128)(2,1)} %pad_maximum_fusion.9), channel_id=1, source_target_pairs={{0,1},{1,0},{2,3},{3,2},{4,5},{5,4},{6,7},{7,6},{8,9},{9,8},{10,11... | collective-permute-start | bytes 3538952 | tf_op jit(solution)/shard_map/ppermute | solution.py:63
  203.2 28.5 %collective-permute-start.41 = (bf16[48,6144]{1,0:T(8,128)(2,1)S(1)}, bf16[48,6144]{1,0:T(8,128)(2,1)}, u32[]{:S(2)}, u32[]{:S(2)}) collective-permute-start(bf16[48,6144]{1,0:T(8,128)(2,1)S(1)} %pad_maximum_fusion.20), channel_id=1, source_target_pairs={{0,2},{1,3},{2,0},{3,1},{4,6},{5,7},{6,4},{7,5},{8,10},{9,11},{10,... | collective-permute-start | bytes 1769480 | tf_op jit(solution)/shard_map/ppermute | solution.py:63
  254.5 21.5 %collective-permute-start.48 = (bf16[128,1536]{1,0:T(8,128)(2,1)S(1)}, bf16[128,1536]{1,0:T(8,128)(2,1)S(1)}, u32[]{:S(2)}, u32[]{:S(2)}) collective-permute-start(bf16[128,1536]{1,0:T(8,128)(2,1)S(1)} %slice.1047.rest_0_), channel_id=1, source_target_pairs={{0,8},{1,9},{2,10},{3,11},{4,12},{5,13},{6,14},{7,15},{8,0},{9,1},... | collective-permute-start | bytes 1179656 | tf_op jit(solution)/shard_map/ppermute | solution.py:63
  276.0 28.7 %collective-permute-start.55 = (bf16[192,3072]{1,0:T(8,128)(2,1)}, bf16[192,3072]{1,0:T(8,128)(2,1)}, u32[]{:S(2)}, u32[]{:S(2)}) collective-permute-start(bf16[192,3072]{1,0:T(8,128)(2,1)} %pad_maximum_fusion.10), channel_id=1, source_target_pairs={{0,16},{1,17},{2,18},{3,19},{4,20},{5,21},{6,22},{7,23},{8,24},{9,... | collective-permute-start | bytes 3538952 | tf_op jit(solution)/shard_map/ppermute | solution.py:63
  277.2 28.4 %collective-permute-start.56 = (bf16[192,3072]{1,0:T(8,128)(2,1)}, bf16[192,3072]{1,0:T(8,128)(2,1)}, u32[]{:S(2)}, u32[]{:S(2)}) collective-permute-start(bf16[192,3072]{1,0:T(8,128)(2,1)} %pad_maximum_fusion.11), channel_id=1, source_target_pairs={{0,1},{1,0},{2,3},{3,2},{4,5},{5,4},{6,7},{7,6},{8,9},{9,8},{10,11... | collective-permute-start | bytes 3538952 | tf_op jit(solution)/shard_map/ppermute | solution.py:63
  279.6 109.9 %collective-permute-start.67 = (bf16[256,768]{1,0:T(8,128)(2,1)}, bf16[256,768]{1,0:T(8,128)(2,1)}, u32[]{:S(2)}, u32[]{:S(2)}) collective-permute-start(bf16[256,768]{1,0:T(8,128)(2,1)} %pad_maximum_fusion.30), channel_id=1, source_target_pairs={{0,8},{1,9},{2,10},{3,11},{4,12},{5,13},{6,14},{7,15},{8,0},{9,1},... | collective-permute-start | bytes 1179656 | tf_op jit(solution)/shard_map/ppermute | solution.py:63
  323.3 58.5 %collective-permute-start.68 = (bf16[128,3072]{1,0:T(8,128)(2,1)S(1)}, bf16[128,3072]{1,0:T(8,128)(2,1)}, u32[]{:S(2)}, u32[]{:S(2)}) collective-permute-start(bf16[128,3072]{1,0:T(8,128)(2,1)S(1)} %get-tuple-element.285), channel_id=1, source_target_pairs={{0,16},{1,17},{2,18},{3,19},{4,20},{5,21},{6,22},{7,23},{8,24},{9,... | collective-permute-start | bytes 2359304 | tf_op jit(solution)/shard_map/ppermute | solution.py:63
  355.9 27.3 %collective-permute-start.69 = (bf16[128,1536]{1,0:T(8,128)(2,1)}, bf16[128,1536]{1,0:T(8,128)(2,1)S(1)}, u32[]{:S(2)}, u32[]{:S(2)}) collective-permute-start(bf16[128,1536]{1,0:T(8,128)(2,1)} %get-tuple-element.170), channel_id=1, source_target_pairs={{0,8},{1,9},{2,10},{3,11},{4,12},{5,13},{6,14},{7,15},{8,0},{9,1},... | collective-permute-start | bytes 1179656 | tf_op jit(solution)/shard_map/ppermute | solution.py:63
  366.6 34.5 %collective-permute-start.63 = (bf16[128,1536]{1,0:T(8,128)(2,1)}, bf16[128,1536]{1,0:T(8,128)(2,1)}, u32[]{:S(2)}, u32[]{:S(2)}) collective-permute-start(bf16[128,1536]{1,0:T(8,128)(2,1)} %get-tuple-element.168), channel_id=1, source_target_pairs={{0,8},{1,9},{2,10},{3,11},{4,12},{5,13},{6,14},{7,15},{8,0},{9,1},... | collective-permute-start | bytes 1179656 | tf_op jit(solution)/shard_map/ppermute | solution.py:63
  380.2 20.3 %collective-permute-start.75 = (bf16[128,1536]{1,0:T(8,128)(2,1)}, bf16[128,1536]{1,0:T(8,128)(2,1)}, u32[]{:S(2)}, u32[]{:S(2)}) collective-permute-start(bf16[128,1536]{1,0:T(8,128)(2,1)} %fusion.480), channel_id=1, source_target_pairs={{0,17},{1,16},{2,19},{3,18},{4,21},{5,20},{6,23},{7,22},{8,25},{9,... | collective-permute-start | bytes 1179656 | tf_op jit(solution)/shard_map/ppermute | solution.py:63
  398.7 64.9 %collective-permute-start.77 = (bf16[256,192]{0,1:T(8,128)(2,1)}, bf16[256,192]{0,1:T(8,128)(2,1)}, u32[]{:S(2)}, u32[]{:S(2)}) collective-permute-start(bf16[256,192]{0,1:T(8,128)(2,1)} %pad_maximum_fusion.36), channel_id=1, source_target_pairs={{0,8},{1,9},{2,10},{3,11},{4,12},{5,13},{6,14},{7,15},{8,0},{9,1},... | collective-permute-start | bytes 294920 | tf_op jit(solution)/shard_map/ppermute | solution.py:63
  407.7 24.8 %collective-permute-start.82 = (bf16[128,768]{1,0:T(8,128)(2,1)}, bf16[128,768]{1,0:T(8,128)(2,1)}, u32[]{:S(2)}, u32[]{:S(2)}) collective-permute-start(bf16[128,768]{1,0:T(8,128)(2,1)} %get-tuple-element.276), channel_id=1, source_target_pairs={{0,16},{1,17},{2,18},{3,19},{4,20},{5,21},{6,22},{7,23},{8,24},{9,... | collective-permute-start | bytes 589832 | tf_op jit(solution)/shard_map/ppermute | solution.py:63
  413.8 20.8 %collective-permute-start.78 = (bf16[128,3072]{1,0:T(8,128)(2,1)}, bf16[128,3072]{1,0:T(8,128)(2,1)}, u32[]{:S(2)}, u32[]{:S(2)}) collective-permute-start(bf16[128,3072]{1,0:T(8,128)(2,1)} %pad_maximum_fusion.15), channel_id=1, source_target_pairs={{0,16},{1,17},{2,18},{3,19},{4,20},{5,21},{6,22},{7,23},{8,24},{9,... | collective-permute-start | bytes 2359304 | tf_op jit(solution)/shard_map/ppermute | solution.py:63
  428.4 26.1 %collective-permute-start.85 = (bf16[128,3840]{1,0:T(8,128)(2,1)S(1)}, bf16[128,3840]{1,0:T(8,128)(2,1)}, u32[]{:S(2)}, u32[]{:S(2)}) collective-permute-start(bf16[128,3840]{1,0:T(8,128)(2,1)S(1)} %pad_maximum_fusion.13), channel_id=1, source_target_pairs={{0,16},{1,17},{2,18},{3,19},{4,20},{5,21},{6,22},{7,23},{8,24},{9,... | collective-permute-start | bytes 2949128 | tf_op jit(solution)/shard_map/ppermute | solution.py:63
  429.6 217.2 %reduce-scatter.5.cloned.1.call-start = ((), (), s32[]{:S(2)}) async-start(), calls=%async_computation.3 | async-start | bytes 4313088 | tf_op jit(solution)/shard_map/reduce_scatter | solution.py:675
  436.0 21.4 %collective-permute-start.79 = (bf16[256,3072]{1,0:T(8,128)(2,1)S(1)}, bf16[256,3072]{1,0:T(8,128)(2,1)S(1)}, u32[]{:S(2)}, u32[]{:S(2)}) collective-permute-start(bf16[256,3072]{1,0:T(8,128)(2,1)S(1)} %pad_maximum_fusion.5), channel_id=1, source_target_pairs={{0,8},{1,9},{2,10},{3,11},{4,12},{5,13},{6,14},{7,15},{8,0},{9,1},... | collective-permute-start | bytes 4718600 | tf_op jit(solution)/shard_map/ppermute | solution.py:63
  455.8 40.0 %collective-permute-start.89 = (bf16[256,3840]{1,0:T(8,128)(2,1)S(1)}, bf16[256,3840]{1,0:T(8,128)(2,1)S(1)}, u32[]{:S(2)}, u32[]{:S(2)}) collective-permute-start(bf16[256,3840]{1,0:T(8,128)(2,1)S(1)} %pad_maximum_fusion.1), channel_id=1, source_target_pairs={{0,8},{1,9},{2,10},{3,11},{4,12},{5,13},{6,14},{7,15},{8,0},{9,1},... | collective-permute-start | bytes 5898248 | tf_op jit(solution)/shard_map/ppermute | solution.py:63
  484.8 26.9 %collective-permute-start.84 = (bf16[128,1536]{1,0:T(8,128)(2,1)}, bf16[128,1536]{1,0:T(8,128)(2,1)S(1)}, u32[]{:S(2)}, u32[]{:S(2)}) collective-permute-start(bf16[128,1536]{1,0:T(8,128)(2,1)} %get-tuple-element.184), channel_id=1, source_target_pairs={{0,8},{1,9},{2,10},{3,11},{4,12},{5,13},{6,14},{7,15},{8,0},{9,1},... | collective-permute-start | bytes 1179656 | tf_op jit(solution)/shard_map/ppermute | solution.py:63
  519.6 24.2 %collective-permute-start.93 = (bf16[128,2304]{1,0:T(8,128)(2,1)S(1)}, bf16[128,2304]{1,0:T(8,128)(2,1)S(1)}, u32[]{:S(2)}, u32[]{:S(2)}) collective-permute-start(bf16[128,2304]{1,0:T(8,128)(2,1)S(1)} %pad_maximum_fusion.26), channel_id=1, source_target_pairs={{0,16},{1,17},{2,18},{3,19},{4,20},{5,21},{6,22},{7,23},{8,24},{9,... | collective-permute-start | bytes 1769480 | tf_op jit(solution)/shard_map/ppermute | solution.py:63
  545.0 30.9 %collective-permute-start.101 = (bf16[256,2304]{1,0:T(8,128)(2,1)}, bf16[256,2304]{1,0:T(8,128)(2,1)}, u32[]{:S(2)}, u32[]{:S(2)}) collective-permute-start(bf16[256,2304]{1,0:T(8,128)(2,1)} %pad_maximum_fusion.12), channel_id=1, source_target_pairs={{0,8},{1,9},{2,10},{3,11},{4,12},{5,13},{6,14},{7,15},{8,0},{9,1},... | collective-permute-start | bytes 3538952 | tf_op jit(solution)/shard_map/ppermute | solution.py:63
  545.7 30.3 %collective-permute-start.100 = (bf16[256,192]{0,1:T(8,128)(2,1)}, bf16[256,192]{0,1:T(8,128)(2,1)}, u32[]{:S(2)}, u32[]{:S(2)}) collective-permute-start(bf16[256,192]{0,1:T(8,128)(2,1)} %pad_maximum_fusion.38), channel_id=1, source_target_pairs={{0,8},{1,9},{2,10},{3,11},{4,12},{5,13},{6,14},{7,15},{8,0},{9,1},... | collective-permute-start | bytes 294920 | tf_op jit(solution)/shard_map/ppermute | solution.py:63
  548.6 24.9 %collective-permute-start.97 = (bf16[512,768]{1,0:T(8,128)(2,1)}, bf16[512,768]{1,0:T(8,128)(2,1)}, u32[]{:S(2)}, u32[]{:S(2)}) collective-permute-start(bf16[512,768]{1,0:T(8,128)(2,1)} %pad_maximum_fusion.17), channel_id=1, source_target_pairs={{0,1},{1,0},{2,3},{3,2},{4,5},{5,4},{6,7},{7,6},{8,9},{9,8},{10,11... | collective-permute-start | bytes 2359304 | tf_op jit(solution)/shard_map/ppermute | solution.py:63
  549.6 24.0 %collective-permute-start.98 = (bf16[512,768]{1,0:T(8,128)(2,1)}, bf16[512,768]{1,0:T(8,128)(2,1)}, u32[]{:S(2)}, u32[]{:S(2)}) collective-permute-start(bf16[512,768]{1,0:T(8,128)(2,1)} %pad_maximum_fusion.17), channel_id=1, source_target_pairs={{0,16},{1,17},{2,18},{3,19},{4,20},{5,21},{6,22},{7,23},{8,24},{9,... | collective-permute-start | bytes 2359304 | tf_op jit(solution)/shard_map/ppermute | solution.py:63
  558.9 50.2 %collective-permute-start.105 = (bf16[512,768]{1,0:T(8,128)(2,1)}, bf16[512,768]{1,0:T(8,128)(2,1)S(1)}, u32[]{:S(2)}, u32[]{:S(2)}) collective-permute-start(bf16[512,768]{1,0:T(8,128)(2,1)} %pad_maximum_fusion.17), channel_id=1, source_target_pairs={{0,8},{1,9},{2,10},{3,11},{4,12},{5,13},{6,14},{7,15},{8,0},{9,1},... | collective-permute-start | bytes 2359304 | tf_op jit(solution)/shard_map/ppermute | solution.py:63
  578.2 30.1 %collective-permute-start.104 = (bf16[96,2304]{1,0:T(8,128)(2,1)S(1)}, bf16[96,2304]{1,0:T(8,128)(2,1)S(1)}, u32[]{:S(2)}, u32[]{:S(2)}) collective-permute-start(bf16[96,2304]{1,0:T(8,128)(2,1)S(1)} %slice.1142), channel_id=1, source_target_pairs={{0,1},{1,0},{2,3},{3,2},{4,5},{5,4},{6,7},{7,6},{8,9},{9,8},{10,11... | collective-permute-start | bytes 1327112 | tf_op jit(solution)/shard_map/ppermute | solution.py:63
  579.2 29.1 %collective-permute-start.102 = (bf16[256,768]{1,0:T(8,128)(2,1)S(1)}, bf16[256,768]{1,0:T(8,128)(2,1)S(1)}, u32[]{:S(2)}, u32[]{:S(2)}) collective-permute-start(bf16[256,768]{1,0:T(8,128)(2,1)S(1)} %slice.956), channel_id=1, source_target_pairs={{0,1},{1,0},{2,3},{3,2},{4,5},{5,4},{6,7},{7,6},{8,9},{9,8},{10,11... | collective-permute-start | bytes 1179656 | tf_op jit(solution)/shard_map/ppermute | solution.py:63
  580.3 28.0 %collective-permute-start.103 = (bf16[256,768]{1,0:T(8,128)(2,1)S(1)}, bf16[256,768]{1,0:T(8,128)(2,1)S(1)}, u32[]{:S(2)}, u32[]{:S(2)}) collective-permute-start(bf16[256,768]{1,0:T(8,128)(2,1)S(1)} %slice.957), channel_id=1, source_target_pairs={{0,16},{1,17},{2,18},{3,19},{4,20},{5,21},{6,22},{7,23},{8,24},{9,... | collective-permute-start | bytes 1179656 | tf_op jit(solution)/shard_map/ppermute | solution.py:63
  581.2 27.9 %collective-permute-start.106 = (bf16[512,768]{1,0:T(8,128)(2,1)}, bf16[512,768]{1,0:T(8,128)(2,1)S(1)}, u32[]{:S(2)}, u32[]{:S(2)}) collective-permute-start(bf16[512,768]{1,0:T(8,128)(2,1)} %collective-permute-done.97), channel_id=1, source_target_pairs={{0,8},{1,9},{2,10},{3,11},{4,12},{5,13},{6,14},{7,15},{8,0},{9,1},... | collective-permute-start | bytes 2359304 | tf_op jit(solution)/shard_map/ppermute | solution.py:63
  (249 other events, 1871.5 us)
Sparse Core Ops, SparseCore 0:
  429.8 67.3 reduce-scatter.2
  553.1 91.5 reduce-scatter.4

commit v3 on v2

--- a/solution.py
+++ b/solution.py
@@ -364,7 +364,7 @@
     split = [None] * len(pairs)
     last_round = [None]
 
-    def begin_round(number, after, late=None):
+    def begin_round(number, after, late=()):
         pending = []
         for p in range(len(pairs)):
             k = number - 2 * p
@@ -377,8 +377,8 @@
         values = [entry[3] for entry in pending]
         if timed:
             values = list(lax.optimization_barrier((values, after, last_round[0]))[0])
-            if late is not None:
-                values[late[0]], _ = lax.optimization_barrier((values[late[0]], late[1]))
+            for index, wait in late:
+                values[index], _ = lax.optimization_barrier((values[index], wait))
         arrived = [sw(value, entry[2]) for value, entry in zip(values, pending)]
         last_round[0] = arrived
         return pending, values, arrived
@@ -395,15 +395,19 @@
             else:
                 split[p][side] = joined
 
+    ids_route = [geo.x_last[-2]] + [m for m in geo.x_last[:-2]] + [core]
     ids = token_ids.reshape(1, tokens)
-    ids = jnp.concatenate([ids] + [sw(ids, m * n) for m in range(1, geo.b)], axis=0)
-    first_ids = ids
-    ids = jnp.stack([ids] + [sw(ids, m) for m in range(1, n)], axis=1)
+    ids_stages = []
+    for mask in ids_route:
+        ids = jnp.concatenate([ids, sw(ids, mask)], axis=0)
+        ids_stages.append(ids)
+    first_ids, deep_ids = ids_stages[0], ids_stages[len(geo.zs).bit_length() - 1]
     target = me ^ jnp.array(geo.order, jnp.int32)
     t_seq = (target % n) // r
     t_rank = (target // n) * r + target % r
     halves = jnp.stack([t_rank, 2 * n - 1 - t_rank], axis=1)
     source = (t_seq[:, None] * n + halves // 2) ^ me
+    source = sum(((source // mask) % 2) * 2**k for k, mask in enumerate(ids_route))
     ids = jnp.take(ids.reshape(2 * count, half), (source * 2 + halves % 2).reshape(-1), axis=0).reshape(-1)
 
     vocab = embedding.shape[0]
@@ -412,9 +416,9 @@
     tables = [table] + [sw(table, m) for m in geo.high[1:]]
     tables = tables + [sw(part, core) for part in tables]
     owners = geo.high + [m ^ core for m in geo.high]
-    end_round(begin_round(0, first_ids), None)
-    end_round(begin_round(1, first_ids), None)
-    third = begin_round(2, first_ids)
+    end_round(begin_round(0, deep_ids), None)
+    end_round(begin_round(1, deep_ids), None)
+    third = begin_round(2, deep_ids)
     near = ids[: len(geo.low) * len(geo.zs) * tokens]
     picked = jnp.zeros((near.shape[0], D), F32)
     for m, part in zip(owners, tables):
@@ -425,7 +429,7 @@
     row = flat[0]
     for k in range(1, len(geo.low)):
         row = row + sw(flat[k], geo.low[k])
-    fourth = begin_round(3, picked, (1, row))
+    fourth = begin_round(3, picked, [(1, row), (2, row)])
     row = row.reshape(len(geo.zs), tokens, D)
     stream = row[0]
     for k in range(1, len(geo.zs)):
@@ -521,11 +525,6 @@
     quarter = D // 4
     quarters = [turn_x[:, k * quarter : (k + 1) * quarter] for k in range(4)]
 
-    rows_of = [
-        (i ^ (m // n)) * quarter + jnp.arange(quarter, dtype=jnp.int32) for m in (0, x_mask, core, x_mask ^ core)
-    ]
-    straight = [(feature[:, None] == rows[None, :]).astype(BF16) for rows in rows_of]
-
     def four_rows(values, quarters):
         tall = jnp.concatenate(values, axis=0)
         stay, to_x, to_core, to_both = (mm(tall, q).astype(BF16) for q in quarters)
@@ -558,7 +557,7 @@
                 moves.append((b * n + block, to))
         return moves
 
-    flat = cotangent.reshape(tokens, D)
+    flat, _ = lax.optimization_barrier((cotangent.reshape(tokens, D), stream))
     evens = lax.ppermute(flat[:half], AXES, half_moves(0))
     odds = lax.ppermute(flat[half:], AXES, half_moves(1))
     even_rank = rank % 2 == 0
@@ -627,11 +626,8 @@
     back_odd = [(b, a) for a, b in half_moves(1)]
     first = jnp.where(even_rank, final[:half], final[half:])
     second = jnp.where(even_rank, final[half:], final[:half])
-    output = jnp.concatenate(
-        [lax.ppermute(first, AXES, back_even), lax.ppermute(second, AXES, back_odd)], axis=0
-    ).reshape(cotangent.shape)
-
-    shares = [None] * LAYERS
+    output = [lax.ppermute(first, AXES, back_even), lax.ppermute(second, AXES, back_odd)]
+
     mixes = [None] * LAYERS
     gain_grads = [None] * LAYERS
     for l in reversed(range(LAYERS)):
@@ -642,39 +638,52 @@
         active_grad = [back_times(gf, outwards[l], a * D, D, turns[l]) for a in range(folds)]
         gz = pull(jnp.concatenate(active_grad, axis=1))[0].astype(BF16)
         normed_grad = back_times(gz, inwards[l], 0, ff, turns[1 - l])
-        gf_four = four_tokens(two_tokens(gf))
-        tall = four_rows([active[:, a * D : (a + 1) * D] for a in range(folds)] + [n2, attended], straight)
-        back_grad = [t_mm(part, gf_four) for part in tall[:folds]]
+        by_fold = [active[:, a * D : (a + 1) * D] for a in range(folds)]
+        gf_two = two_tokens(gf)
         if l == 0:
-            (tall_n1,) = four_rows([n1], quarters)
+            tall = four_rows(by_fold, quarters)
+            tall_n2, tall_out, tall_n1 = four_rows([n2, attended, n1], quarters)
         else:
             gz_two = two_tokens(gz)
+            tall = four_rows([n2] + by_fold, quarters)
         delta, gain_f_grad = norm_back(middle, gain_f, normed_grad)
         middle_grad = grad_stream + delta
         gy = middle_grad.astype(BF16)
         go = back_times(gy, attns[l], 3 * D, D, turns[l]).astype(BF16)
         if l == 0:
             gz_two = two_tokens(jnp.concatenate([gz, gy], axis=1))
-            go, attn_grad, back_grad = lax.optimization_barrier((go, attn_grad, back_grad))
+            go, gf_two = lax.optimization_barrier((go, gf_two))
+            gf_four = four_tokens(gf_two)
+            back_sum = Sum(side_by_side([t_mm(part, gf_four) for part in tall]), geo.x_last)
+            back_sum.step()
+            ffn_sum.step()
         gq, pre_grad, post_grad, parts = attend_back(
             sources, masks, rank_arg, queries, go, lse, pv, pieces, spread_pre[l], spread_post[l]
         )
         mixes[l] = (pre_grad, post_grad)
+        if l == 1:
+            parts, output = lax.optimization_barrier((parts, output))
+        if l == 0:
+            parts, gz_two, both_two = lax.optimization_barrier((parts, gz_two, both_two))
+            parts = tie(parts, [back_sum, ffn_sum])
         size = len(near_masks)
         sums = [parts[k].astype(F32) + sw(parts[size + k], core).astype(F32) for k in range(size)]
         others = [(sums[k].astype(BF16), near_masks[k]) for k in range(1, size)]
-        arrived = [sw(value, mask) for value, mask in others]
-        gz_two, _ = lax.optimization_barrier((gz_two, sums))
-        gz_four = four_tokens(gz_two)
         if l == 0:
-            pack = attn_grad + back_grad + [t_mm(tall[folds], gz_four[:, :ff]), t_mm(tall[folds + 1], gz_four[:, ff:])]
+            arrived = exchange(parts[0], [ffn_sum], others)
+            gz_two, both_two, _ = lax.optimization_barrier((gz_two, both_two, sums))
+            gz_four, both = four_tokens(gz_two), four_tokens(both_two)
+            attn_grad = [t_mm(tall_n1_one, both[:, : 3 * D]), t_mm(tall_out_one, both[:, 3 * D :])]
+            in_grad = [t_mm(tall_n2, gz_four[:, :ff]), t_mm(tall_out, gz_four[:, ff:])]
+            joined_sum = Sum(side_by_side(attn_grad + in_grad), geo.x_last)
+            arrived = tie(arrived, [joined_sum])
         else:
-            pack = back_grad + [t_mm(tall[folds], gz_four)]
-        pack = side_by_side(pack)
-        pack, arrived = lax.optimization_barrier((pack, arrived))
-        shares[l] = lax.psum_scatter(pack, "seq", scatter_dimension=0, tiled=True)
-        if l == 0:
-            shares[1], arrived = lax.optimization_barrier((shares[1], arrived))
+            arrived = [sw(value, mask) for value, mask in others]
+            gz_two, gf_two, _ = lax.optimization_barrier((gz_two, gf_two, sums))
+            gz_four, gf_four = four_tokens(gz_two), four_tokens(gf_two)
+            ffn_grad = [t_mm(tall[0], gz_four)] + [t_mm(part, gf_four) for part in tall[1:]]
+            ffn_sum = Sum(side_by_side(ffn_grad), geo.x_last)
+            arrived = tie(arrived, [ffn_sum])
         kv_grad = sums[0]
         for there in arrived:
             kv_grad = kv_grad + there.astype(F32)
@@ -683,9 +692,8 @@
         if l == 0:
             joint_zero = joint
         else:
-            both = four_tokens(two_tokens(jnp.concatenate([joint, gy], axis=1)))
-            (tall_n1,) = four_rows([n1], straight)
-            attn_grad = [t_mm(tall_n1, both[:, : 3 * D]), t_mm(tall[folds + 1], both[:, 3 * D :])]
+            both_two = two_tokens(jnp.concatenate([joint, gy], axis=1))
+            tall_n1_one, tall_out_one = four_rows([n1, attended], quarters)
         delta, gain_a_grad = norm_back(stream_in, gain_a, normed_grad)
         grad_stream = middle_grad + delta
         gain_grads[l] = (gain_a_grad, gain_f_grad)
@@ -701,34 +709,38 @@
     small_masks = bits(1, count)
 
     g0 = grad_stream.astype(BF16)
-    arrived = exchange(g0, [], [(joint_zero, x_mask)] + [(g0, m) for m in geo.zs[1:]])
+    arrived = exchange(g0, [joined_sum], [(joint_zero, x_mask)] + [(g0, m) for m in geo.zs[1:]])
     joint_four = four_tokens(jnp.concatenate([joint_zero, arrived[0]], axis=0))
     qkv_sum = Sum(t_mm(tall_n1, joint_four).astype(BF16), geo.x_last)
     rows = jnp.concatenate([g0] + arrived[1:], axis=0)
+
+    def share_small(after, sums, others=()):
+        nonlocal small
+        there = exchange(after, sums, list(others) + [(small, small_masks.pop())])
+        small = small + there[-1]
+        return there[:-1]
+
     if len(geo.plane) == 4:
         cut = rows.shape[0] // 2
         y, x = geo.plane[1], geo.plane[2]
-        by_y, by_x = exchange(rows, [], [(rows, y), (rows, x)])
-        both = exchange(by_x, [qkv_sum], [(by_x[:cut], y), (by_y[cut:], x)])
+        by_y, by_x = share_small(rows, [joined_sum, back_sum], [(rows, y), (rows, x)])
+        both = share_small(by_x, [qkv_sum, joined_sum], [(by_x[:cut], y), (by_y[cut:], x)])
         blocks = [rows, by_y, by_x] + both
     else:
-        blocks = [rows] + exchange(rows, [], [(rows, m) for m in geo.plane[1:]])
-        exchange(blocks[-1], [qkv_sum])
+        blocks = [rows] + share_small(rows, [joined_sum, back_sum], [(rows, m) for m in geo.plane[1:]])
+        share_small(blocks[-1], [qkv_sum, joined_sum])
     blocks = blocks + [sw(block, core) for block in blocks]
-
-    def share_small(after, sums):
-        nonlocal small
-        (there,) = exchange(after, sums, [(small, small_masks.pop())])
-        small = small + there
-
-    share_small(blocks, [qkv_sum])
+    share_small(blocks, [qkv_sum, back_sum, ffn_sum])
     own_names = me * vocab + line
+    blocks = jnp.concatenate(blocks, axis=0)
     embedding_grad = mm(
-        (own_names[:, None] == ids[None, :]).astype(BF16), jnp.concatenate(blocks, axis=0)
+        (own_names[:, None] == ids[None, :]).astype(BF16), blocks
     )
-    share_small(qkv_sum.value, [qkv_sum])
-    while small_masks:
-        share_small(qkv_sum.value, [])
+    while len(small_masks) > 2:
+        share_small(qkv_sum.value, [qkv_sum])
+    one_bit, two_bit = small_masks
+    one, two, both = exchange(qkv_sum.value, [qkv_sum], [(small, one_bit), (small, two_bit), (small, one_bit ^ two_bit)])
+    small = (small + one) + (two + both)
     small = small.reshape(-1)[:size]
     mix = small[: 2 * LAYERS * H * H].reshape(2, LAYERS, H, H)
     gain_sum = small[2 * LAYERS * H * H :].reshape(2, LAYERS, D)
@@ -741,18 +753,18 @@
         return jnp.concatenate([part[:, a * D : (a + 1) * D] for a in range(folds)], axis=0)
 
     qkv_share = qkv_sum.result()
-    one, zero = shares[1].astype(F32), shares[0].astype(F32)
-    attn_share, zero = zero[:, : 4 * D], zero[:, 4 * D :]
-    width = folds * D
+    one, joined, zero = ffn_sum.result(), joined_sum.result(), back_sum.result()
+    attn_share, in_share = joined[:, : 4 * D], joined[:, 4 * D :]
+    output = jnp.concatenate(output, axis=0).reshape(cotangent.shape)
     return (
         output,
         embedding_grad,
         gain_sum[0],
         jnp.stack([qkv_share, attn_share[:, : 3 * D]]),
-        jnp.stack([zero[:, width + ff :], attn_share[:, 3 * D :]]),
+        jnp.stack([in_share[:, ff:], attn_share[:, 3 * D :]]),
         gain_sum[1],
-        jnp.stack([in_order(zero[:, width : width + ff]), in_order(one[:, width:])]),
-        jnp.stack([back_order(zero[:, :width]), back_order(one[:, :width])]),
+        jnp.stack([in_order(in_share[:, :ff]), in_order(one[:, :ff])]),
+        jnp.stack([back_order(zero), back_order(one[:, ff:])]),
         mix[0],
         mix[1],
     )

time: 676 us -> 657 us (0.972)
  matrix products: 134 us -> 104 us
  starting transfers between devices: 92.9 us -> 117 us
  other arithmetic: 54.4 us -> 40.1 us
  between operations: 17.6 us -> 4.39 us
  local copies, waits for them, and re-layouts: 94.5 us -> 105 us
    ppermute x113 -> x118, starting transfers between devices: 87.4 us -> 109 us  [swap(): return lax.ppermute(value, AXES, [(p, p ^ mask) for p in range(count)])]
    dot_general x14, matrix products: 26.7 us -> 7.32 us  [t_mm(): lax.dot_general(a, b, (((0,), (0,)), ((), ())), preferred_element_type=F32)]
    dot_general x42, matrix products: 38.4 us -> 31.2 us  [mm_t(): lax.dot_general(a, b, (((1,), (1,)), ((), ())), preferred_element_type=F32)]
    slice x3 -> x12, local copies, waits for them, and re-layouts: 0.06 us -> 6.89 us  [outgoing(): return [(self.value[self.value.shape[0] // 2:], self.masks.pop())]]
    unnamed x405 -> x319, local copies, waits for them, and re-layouts: 36.7 us -> 42 us
    ppermute x113 -> x118, waiting for transfers between devices: 211 us -> 215 us  [swap(): return lax.ppermute(value, AXES, [(p, p ^ mask) for p in range(count)])]
  transfers between devices with their start and end apart: 119 -> 122, of which waited for: 41 -> 42; matrix products, arithmetic and copies ran while one was open for 38% -> 33% of each run, Pallas kernels for 9% -> 9%
where the time goes in v3:
time: 657 us; the launch traced here: 646 us
  waiting for transfers between devices  216 us (33%)
  starting transfers between devices  117 us (18%)
  local copies, waits for them, and re-layouts  105 us (16%)
  matrix products  104 us (16%)
  Pallas kernels  59.8 us (9%)
  other arithmetic  40.1 us (6%)
    ppermute x118, waiting for transfers between devices, swap(): return lax.ppermute(value, AXES, [(p, p ^ mask) for p in range(count)])  215 us
    ppermute x118, starting transfers between devices, swap(): return lax.ppermute(value, AXES, [(p, p ^ mask) for p in range(count)])  109 us
    dot_general x58, matrix products, mm(): return jnp.dot(a, b, preferred_element_type=F32)  65.3 us
    unnamed x319, local copies, waits for them, and re-layouts  42 us
    pallas_call x2, Pallas kernels, attend_back(): pl.pallas_call(functools.partial(backward_kernel, n, sources, count, mask...  36.4 us
    dot_general x42, matrix products, mm_t(): lax.dot_general(a, b, (((1,), (1,)), ((), ())), preferred_element_type=F32)  31.2 us
    pallas_call x2, Pallas kernels, attend(): pl.pallas_call(functools.partial(forward_kernel, n, sources, count, half)...  23.4 us
  transfers between devices with their start and end apart: 122, of which 42 were waited for; matrix products, arithmetic and copies ran while one was open for 33% of the time, Pallas kernels for 9%

profile of v3, /device:TPU:0, one launch (start us, length us, event | category | flops | bytes accessed | tf_op | source)
XLA Modules:
  0.0 645.6 jit_solution(17951728810826985931)
XLA Ops:
  0.7 3.0 collective-permute-start
  17.4 2.7 collective-permute-start.1
  33.4 2.9 collective-permute-start.12
  37.2 3.3 fusion.10
  40.5 9.4 %collective-permute-done.12 = bf16[24,6272]{1,0:T(8,128)(2,1)S(1)} collective-permute-done((bf16[24,6272]{1,0:T(8,128)(2,1)S(1)}, bf16[24,6272]{1,0:T(8,128)(2,1)S(1)}, u32[]{:S(2)}, u32[]{:S(2)}) %collective-permute-start.12) | collective-permute-done | bytes 301088 | tf_op jit(solution)/shard_map/ppermute | solution.py:63
  50.7 18.6 %collective-permute-done.5 = bf16[1004,768]{1,0:T(8,128)(2,1)} collective-permute-done((bf16[1004,768]{1,0:T(8,128)(2,1)}, bf16[1004,768]{1,0:T(8,128)(2,1)}, u32[]{:S(2)}, u32[]{:S(2)}) %collective-permute-start.5) | collective-permute-done | bytes 1542176 | tf_op jit(solution)/shard_map/ppermute | solution.py:63
  71.6 2.6 collective-permute-start.16
  74.2 3.3 fusion.8
  77.5 3.8 fusion.6
  83.4 4.3 collective-permute-done.16
  90.1 16.3 %collective-permute-done.8 = bf16[512,768]{1,0:T(8,128)(2,1)S(1)} collective-permute-done((bf16[512,768]{1,0:T(8,128)(2,1)S(1)}, bf16[512,768]{1,0:T(8,128)(2,1)S(1)}, u32[]{:S(2)}, u32[]{:S(2)}) %collective-permute-start.8) | collective-permute-done | bytes 786464 | tf_op jit(solution)/shard_map/ppermute | solution.py:63
  107.3 4.2 collective-permute-start.11
  113.2 4.1 collective-permute-done.11
  117.4 3.1 collective-permute-start.9
  120.5 13.3 %collective-permute-done.10 = bf16[128,768]{1,0:T(8,128)(2,1)S(1)} collective-permute-done((bf16[128,768]{1,0:T(8,128)(2,1)S(1)}, bf16[128,768]{1,0:T(8,128)(2,1)S(1)}, u32[]{:S(2)}, u32[]{:S(2)}) %collective-permute-start.10) | collective-permute-done | bytes 196640 | tf_op jit(solution)/shard_map/ppermute | solution.py:63
  133.8 2.9 collective-permute-done.9
  140.4 3.7 collective-permute-start.20
  145.2 5.6 collective-permute-start.68
  151.3 4.9 collective-permute-done.68
  171.7 3.6 collective-permute-done.33
  192.8 2.5 constant_dynamic-update-slice_fusion.20
  198.3 11.8 %attend.2 = (bf16[128,768]{1,0:T(8,128)(2,1)}, f32[2,8,768]{2,1,0:T(8,128)}, bf16[2,768,768]{2,1,0:T(8,128)(2,1)}) custom-call(s32[1]{0:T(128)} %bitcast.rank_ref, bf16[128,768]{1,0:T(8,128)(2,1)} %slice.1096.q_ref, f32[12,768]{1,0:T(8,128)} %mul.591.pre_ref, f32[12,768]{1,0:T(8,128)} %reshape.701.post_ref, bf16[128,1536]{1,0:T(8,128)(2,1)} %copy-done.43, ...), custom_call_target="tpu_custom_call" | custom-call | flops 10000000000 | bytes 8388608 | tf_op jit(solution)/shard_map/attend/pallas_call | solution.py:235
  228.2 12.4 %collective-permute-done.90 = bf16[768,192]{0,1:T(8,128)(2,1)S(1)} collective-permute-done((bf16[768,192]{0,1:T(8,128)(2,1)S(1)}, bf16[768,192]{0,1:T(8,128)(2,1)S(1)}, u32[]{:S(2)}, u32[]{:S(2)}) %collective-permute-start.90) | collective-permute-done | bytes 294944 | tf_op jit(solution)/shard_map/ppermute | solution.py:63
  258.9 4.4 collective-permute-done.50
  263.3 3.0 collective-permute-done.51
  268.5 5.8 collective-permute-done.42.rest_2_
  288.5 11.6 %attend.3 = (bf16[128,768]{1,0:T(8,128)(2,1)}, f32[2,8,768]{2,1,0:T(8,128)}, bf16[2,768,768]{2,1,0:T(8,128)(2,1)}) custom-call(s32[1]{0:T(128)} %bitcast.rank_ref, bf16[128,768]{1,0:T(8,128)(2,1)} %slice.1134.q_ref, f32[12,768]{1,0:T(8,128)} %mul.613.pre_ref, f32[12,768]{1,0:T(8,128)} %reshape.704.post_ref, bf16[128,1536]{1,0:T(8,128)(2,1)} %copy-done.44, ...), custom_call_target="tpu_custom_call" | custom-call | flops 10000000000 | bytes 8388608 | tf_op jit(solution)/shard_map/attend/pallas_call | solution.py:235
  307.0 5.9 collective-permute-done.52
  338.4 4.9 collective-permute-start.57
  349.0 18.4 %attend_back.2 = (bf16[128,768]{1,0:T(8,128)(2,1)}, f32[12,768]{1,0:T(8,128)}, f32[12,768]{1,0:T(8,128)}, bf16[128,1536]{1,0:T(8,128)(2,1)}, bf16[128,1536]{1,0:...) custom-call(s32[1]{0:T(128)} %bitcast.rank_ref, ...), custom_call_target="tpu_custom_call" | custom-call | flops 16000000000 | bytes 12582912 | tf_op jit(solution)/shard_map/attend_back/pallas_call | solution.py:266
  382.2 5.3 collective-permute-done.62
  387.5 9.3 %collective-permute-done.64 = bf16[128,1536]{1,0:T(8,128)(2,1)S(1)} collective-permute-done((bf16[128,1536]{1,0:T(8,128)(2,1)S(1)}, bf16[128,1536]{1,0:T(8,128)(2,1)S(1)}, u32[]{:S(2)}, u32[]{:S(2)}) %collective-permute-start.64) | collective-permute-done | bytes 393248 | tf_op jit(solution)/shard_map/ppermute | solution.py:63
  420.0 18.0 %attend_back.3 = (bf16[128,768]{1,0:T(8,128)(2,1)}, f32[12,768]{1,0:T(8,128)}, f32[12,768]{1,0:T(8,128)}, bf16[128,1536]{1,0:T(8,128)(2,1)}, bf16[128,1536]{1,0:...) custom-call(s32[1]{0:T(128)} %bitcast.rank_ref, ...), custom_call_target="tpu_custom_call" | custom-call | flops 16000000000 | bytes 12582912 | tf_op jit(solution)/shard_map/attend_back/pallas_call | solution.py:266
  442.2 12.1 %collective-permute-done.73 = bf16[128,3072]{1,0:T(8,128)(2,1)S(1)} collective-permute-done((bf16[128,3072]{1,0:T(8,128)(2,1)S(1)}, bf16[128,3072]{1,0:T(8,128)(2,1)S(1)}, u32[]{:S(2)}, u32[]{:S(2)}) %collective-permute-start.73) | collective-permute-done | bytes 786464 | tf_op jit(solution)/shard_map/ppermute | solution.py:63
  460.0 5.7 collective-permute-done.87
  467.0 3.1 collective-permute-done.81
  474.5 7.5 %collective-permute-done.83 = bf16[128,1536]{1,0:T(8,128)(2,1)S(1)} collective-permute-done((bf16[128,1536]{1,0:T(8,128)(2,1)S(1)}, bf16[128,1536]{1,0:T(8,128)(2,1)S(1)}, u32[]{:S(2)}, u32[]{:S(2)}) %collective-permute-start.83) | collective-permute-done | bytes 393248 | tf_op jit(solution)/shard_map/ppermute | solution.py:63
  484.0 8.4 %collective-permute-done.85 = bf16[128,1536]{1,0:T(8,128)(2,1)S(1)} collective-permute-done((bf16[128,1536]{1,0:T(8,128)(2,1)S(1)}, bf16[128,1536]{1,0:T(8,128)(2,1)S(1)}, u32[]{:S(2)}, u32[]{:S(2)}) %collective-permute-start.85) | collective-permute-done | bytes 393248 | tf_op jit(solution)/shard_map/ppermute | solution.py:63
  492.4 4.3 collective-permute-done.86
  529.9 4.9 collective-permute-done.95
  534.8 5.4 collective-permute-done.97
  555.1 6.2 collective-permute-done.100
  561.3 6.5 %collective-permute-done.102 = bf16[48,3072]{1,0:T(8,128)(2,1)S(1)} collective-permute-done((bf16[48,3072]{1,0:T(8,128)(2,1)S(1)}, bf16[48,3072]{1,0:T(8,128)(2,1)S(1)}, u32[]{:S(2)}, u32[]{:S(2)}) %collective-permute-start.102) | collective-permute-done | bytes 294944 | tf_op jit(solution)/shard_map/ppermute | solution.py:63
  579.4 8.1 %collective-permute-done.108 = bf16[24,6912]{1,0:T(8,128)(2,1)S(1)} collective-permute-done((bf16[24,6912]{1,0:T(8,128)(2,1)S(1)}, bf16[24,6912]{1,0:T(8,128)(2,1)S(1)}, u32[]{:S(2)}, u32[]{:S(2)}) %collective-permute-start.108) | collective-permute-done | bytes 331808 | tf_op jit(solution)/shard_map/ppermute | solution.py:63
  598.9 2.5 stack_reshape.6
  606.6 2.7 collective-permute-start.117
  612.8 11.3 %fusion = f32[1004,768]{1,0:T(8,128)} fusion(bf16[4096,768]{1,0:T(8,128)(2,1)} %constant_dynamic-update-slice_fusion.42, s32[4096]{0:T(1024)S(1)} %copy-done.109, s32[1004]{0:T(1024)S(1)} %copy-done.114), kind=kOutput, calls=%fused_computation.1 | convolution fusion | flops 6320734208 | bytes 9396144 | tf_op jit(solution)/shard_map/dot_general | solution.py:294
  624.2 4.1 collective-permute-done.117
  (873 shorter events, 319.7 us)
Async XLA Ops:
  0.7 16.7 %collective-permute-start = (s32[1,128]{1,0:T(1,128)}, s32[1,128]{1,0:T(1,128)S(1)}, u32[]{:S(2)}, u32[]{:S(2)}) collective-permute-start(s32[1,128]{1,0:T(1,128)} %param.14), channel_id=1, source_target_pairs={{0,16},{1,17},{2,18},{3,19},{4,20},{5,21},{6,22},{7,23},{8,24},{9,... | collective-permute-start | bytes 1544 | tf_op jit(solution)/shard_map/ppermute | solution.py:63
  32.7 44.8 %collective-permute-start.6 = (bf16[1004,768]{1,0:T(8,128)(2,1)}, bf16[1004,768]{1,0:T(8,128)(2,1)}, u32[]{:S(2)}, u32[]{:S(2)}) collective-permute-start(bf16[1004,768]{1,0:T(8,128)(2,1)} %param.15), channel_id=1, source_target_pairs={{0,8},{1,9},{2,10},{3,11},{4,12},{5,13},{6,14},{7,15},{8,0},{9,1},... | collective-permute-start | bytes 4626440 | tf_op jit(solution)/shard_map/ppermute | solution.py:63
  33.2 36.1 %collective-permute-start.5 = (bf16[1004,768]{1,0:T(8,128)(2,1)}, bf16[1004,768]{1,0:T(8,128)(2,1)}, u32[]{:S(2)}, u32[]{:S(2)}) collective-permute-start(bf16[1004,768]{1,0:T(8,128)(2,1)} %param.15), channel_id=1, source_target_pairs={{0,16},{1,17},{2,18},{3,19},{4,20},{5,21},{6,22},{7,23},{8,24},{9,... | collective-permute-start | bytes 4626440 | tf_op jit(solution)/shard_map/ppermute | solution.py:63
  49.9 19.5 %collective-permute-start.13 = (bf16[48,6272]{1,0:T(8,128)(2,1)S(1)}, bf16[48,6272]{1,0:T(8,128)(2,1)S(1)}, u32[]{:S(2)}, u32[]{:S(2)}) collective-permute-start(bf16[48,6272]{1,0:T(8,128)(2,1)S(1)} %pad_maximum_fusion.18), channel_id=1, source_target_pairs={{0,2},{1,3},{2,0},{3,1},{4,6},{5,7},{6,4},{7,5},{8,10},{9,11},{10,... | collective-permute-start | bytes 1806344 | tf_op jit(solution)/shard_map/ppermute | solution.py:63
  69.5 18.2 %collective-permute-start.14 = (bf16[96,3200]{1,0:T(8,128)(2,1)S(1)}, bf16[96,3200]{1,0:T(8,128)(2,1)S(1)}, u32[]{:S(2)}, u32[]{:S(2)}) collective-permute-start(bf16[96,3200]{1,0:T(8,128)(2,1)S(1)} %slice.1087), channel_id=1, source_target_pairs={{0,1},{1,0},{2,3},{3,2},{4,5},{5,4},{6,7},{7,6},{8,9},{9,8},{10,11... | collective-permute-start | bytes 1843208 | tf_op jit(solution)/shard_map/ppermute | solution.py:63
  87.8 18.6 %collective-permute-start.8 = (bf16[512,768]{1,0:T(8,128)(2,1)S(1)}, bf16[512,768]{1,0:T(8,128)(2,1)S(1)}, u32[]{:S(2)}, u32[]{:S(2)}) collective-permute-start(bf16[512,768]{1,0:T(8,128)(2,1)S(1)} %slice.1082), channel_id=1, source_target_pairs={{0,1},{1,0},{2,3},{3,2},{4,5},{5,4},{6,7},{7,6},{8,9},{9,8},{10,11... | collective-permute-start | bytes 2359304 | tf_op jit(solution)/shard_map/ppermute | solution.py:63
  88.4 50.7 %collective-permute-start.17 = (bf16[192,3200]{1,0:T(8,128)(2,1)S(1)}, bf16[192,3200]{1,0:T(8,128)(2,1)S(1)}, u32[]{:S(2)}, u32[]{:S(2)}) collective-permute-start(bf16[192,3200]{1,0:T(8,128)(2,1)S(1)} %pad_maximum_fusion.6), channel_id=1, source_target_pairs={{0,16},{1,17},{2,18},{3,19},{4,20},{5,21},{6,22},{7,23},{8,24},{9,... | collective-permute-start | bytes 3686408 | tf_op jit(solution)/shard_map/ppermute | solution.py:63
  106.6 32.6 %collective-permute-start.18 = (bf16[192,3072]{1,0:T(8,128)(2,1)S(1)}, bf16[192,3072]{1,0:T(8,128)(2,1)S(1)}, u32[]{:S(2)}, u32[]{:S(2)}) collective-permute-start(bf16[192,3072]{1,0:T(8,128)(2,1)S(1)} %pad_maximum_fusion.7), channel_id=1, source_target_pairs={{0,1},{1,0},{2,3},{3,2},{4,5},{5,4},{6,7},{7,6},{8,9},{9,8},{10,11... | collective-permute-start | bytes 3538952 | tf_op jit(solution)/shard_map/ppermute | solution.py:63
  112.7 26.5 %collective-permute-start.19 = (bf16[48,6144]{1,0:T(8,128)(2,1)S(1)}, bf16[48,6144]{1,0:T(8,128)(2,1)S(1)}, u32[]{:S(2)}, u32[]{:S(2)}) collective-permute-start(bf16[48,6144]{1,0:T(8,128)(2,1)S(1)} %pad_maximum_fusion.19), channel_id=1, source_target_pairs={{0,2},{1,3},{2,0},{3,1},{4,6},{5,7},{6,4},{7,5},{8,10},{9,11},{10,... | collective-permute-start | bytes 1769480 | tf_op jit(solution)/shard_map/ppermute | solution.py:63
  112.7 21.1 %collective-permute-start.10 = (bf16[128,768]{1,0:T(8,128)(2,1)S(1)}, bf16[128,768]{1,0:T(8,128)(2,1)S(1)}, u32[]{:S(2)}, u32[]{:S(2)}) collective-permute-start(bf16[128,768]{1,0:T(8,128)(2,1)S(1)} %get-tuple-element.400), channel_id=1, source_target_pairs={{0,4},{1,5},{2,6},{3,7},{4,0},{5,1},{6,2},{7,3},{8,12},{9,13},{10,... | collective-permute-start | bytes 589832 | tf_op jit(solution)/shard_map/ppermute | solution.py:63
  117.4 19.3 %collective-permute-start.9 = (bf16[128,768]{1,0:T(8,128)(2,1)S(1)}, bf16[128,768]{1,0:T(8,128)(2,1)S(1)}, u32[]{:S(2)}, u32[]{:S(2)}) collective-permute-start(bf16[128,768]{1,0:T(8,128)(2,1)S(1)} %get-tuple-element.398), channel_id=1, source_target_pairs={{0,2},{1,3},{2,0},{3,1},{4,6},{5,7},{6,4},{7,5},{8,10},{9,11},{10,... | collective-permute-start | bytes 589832 | tf_op jit(solution)/shard_map/ppermute | solution.py:63
  140.4 23.0 %collective-permute-start.20 = (bf16[384,3200]{1,0:T(8,128)(2,1)}, bf16[384,3200]{1,0:T(8,128)(2,1)}, u32[]{:S(2)}, u32[]{:S(2)}) collective-permute-start(bf16[384,3200]{1,0:T(8,128)(2,1)} %constant_dynamic-update-slice_fusion.8), channel_id=1, source_target_pairs={{0,8},{1,9},{2,10},{3,11},{4,12},{5,13},{6,14},{7,15},{8,0},{9,1},... | collective-permute-start | bytes 7372808 | tf_op jit(solution)/shard_map/ppermute | solution.py:63
  175.3 20.0 %collective-permute-start.25 = (bf16[128,1536]{1,0:T(8,128)(2,1)S(1)}, bf16[128,1536]{1,0:T(8,128)(2,1)S(1)}, u32[]{:S(2)}, u32[]{:S(2)}) collective-permute-start(bf16[128,1536]{1,0:T(8,128)(2,1)S(1)} %slice.1097.rest_0_), channel_id=1, source_target_pairs={{0,8},{1,9},{2,10},{3,11},{4,12},{5,13},{6,14},{7,15},{8,0},{9,1},... | collective-permute-start | bytes 1179656 | tf_op jit(solution)/shard_map/ppermute | solution.py:63
  195.3 20.4 %collective-permute-start.30 = (bf16[384,3072]{1,0:T(8,128)(2,1)S(1)}, bf16[384,3072]{1,0:T(8,128)(2,1)S(1)}, u32[]{:S(2)}, u32[]{:S(2)}) collective-permute-start(bf16[384,3072]{1,0:T(8,128)(2,1)S(1)} %constant_dynamic-update-slice_fusion.10), channel_id=1, source_target_pairs={{0,8},{1,9},{2,10},{3,11},{4,12},{5,13},{6,14},{7,15},{8,0},{9,1},... | collective-permute-start | bytes 7077896 | tf_op jit(solution)/shard_map/ppermute | solution.py:63
  195.8 45.6 %collective-permute-start.34 = (bf16[192,3072]{1,0:T(8,128)(2,1)}, bf16[192,3072]{1,0:T(8,128)(2,1)}, u32[]{:S(2)}, u32[]{:S(2)}) collective-permute-start(bf16[192,3072]{1,0:T(8,128)(2,1)} %pad_maximum_fusion.8), channel_id=1, source_target_pairs={{0,16},{1,17},{2,18},{3,19},{4,20},{5,21},{6,22},{7,23},{8,24},{9,... | collective-permute-start | bytes 3538952 | tf_op jit(solution)/shard_map/ppermute | solution.py:63
  196.7 44.7 %collective-permute-start.35 = (bf16[192,3072]{1,0:T(8,128)(2,1)}, bf16[192,3072]{1,0:T(8,128)(2,1)}, u32[]{:S(2)}, u32[]{:S(2)}) collective-permute-start(bf16[192,3072]{1,0:T(8,128)(2,1)} %pad_maximum_fusion.9), channel_id=1, source_target_pairs={{0,1},{1,0},{2,3},{3,2},{4,5},{5,4},{6,7},{7,6},{8,9},{9,8},{10,11... | collective-permute-start | bytes 3538952 | tf_op jit(solution)/shard_map/ppermute | solution.py:63
  197.5 43.9 %collective-permute-start.36 = (bf16[48,6144]{1,0:T(8,128)(2,1)}, bf16[48,6144]{1,0:T(8,128)(2,1)}, u32[]{:S(2)}, u32[]{:S(2)}) collective-permute-start(bf16[48,6144]{1,0:T(8,128)(2,1)} %pad_maximum_fusion.20), channel_id=1, source_target_pairs={{0,2},{1,3},{2,0},{3,1},{4,6},{5,7},{6,4},{7,5},{8,10},{9,11},{10,... | collective-permute-start | bytes 1769480 | tf_op jit(solution)/shard_map/ppermute | solution.py:63
  223.4 25.9 %collective-permute-start.74 = (bf16[1024,192]{0,1:T(8,128)(2,1)S(1)}, bf16[1024,192]{0,1:T(8,128)(2,1)S(1)}, u32[]{:S(2)}, u32[]{:S(2)}) collective-permute-start(bf16[1024,192]{0,1:T(8,128)(2,1)S(1)} %pad_maximum_fusion.31), channel_id=1, source_target_pairs={{0,16},{1,17},{2,18},{3,19},{4,20},{5,21},{6,22},{7,23},{8,24},{9,... | collective-permute-start | bytes 1179656 | tf_op jit(solution)/shard_map/ppermute | solution.py:63
  256.9 18.4 %collective-permute-start.41 = (bf16[128,1536]{1,0:T(8,128)(2,1)S(1)}, bf16[128,1536]{1,0:T(8,128)(2,1)S(1)}, u32[]{:S(2)}, u32[]{:S(2)}) collective-permute-start(bf16[128,1536]{1,0:T(8,128)(2,1)S(1)} %slice.1135.rest_0_), channel_id=1, source_target_pairs={{0,1},{1,0},{2,3},{3,2},{4,5},{5,4},{6,7},{7,6},{8,9},{9,8},{10,11... | collective-permute-start | bytes 1179656 | tf_op jit(solution)/shard_map/ppermute | solution.py:63
  258.9 25.2 %collective-permute-start.45 = (bf16[128,1536]{1,0:T(8,128)(2,1)S(1)}, bf16[128,1536]{1,0:T(8,128)(2,1)S(1)}, u32[]{:S(2)}, u32[]{:S(2)}) collective-permute-start(bf16[128,1536]{1,0:T(8,128)(2,1)S(1)} %slice.1135.rest_0_), channel_id=1, source_target_pairs={{0,8},{1,9},{2,10},{3,11},{4,12},{5,13},{6,14},{7,15},{8,0},{9,1},... | collective-permute-start | bytes 1179656 | tf_op jit(solution)/shard_map/ppermute | solution.py:63
  284.2 28.7 %collective-permute-start.52 = (bf16[192,3072]{1,0:T(8,128)(2,1)}, bf16[192,3072]{1,0:T(8,128)(2,1)}, u32[]{:S(2)}, u32[]{:S(2)}) collective-permute-start(bf16[192,3072]{1,0:T(8,128)(2,1)} %pad_maximum_fusion.10), channel_id=1, source_target_pairs={{0,16},{1,17},{2,18},{3,19},{4,20},{5,21},{6,22},{7,23},{8,24},{9,... | collective-permute-start | bytes 3538952 | tf_op jit(solution)/shard_map/ppermute | solution.py:63
  285.3 28.3 %collective-permute-start.53 = (bf16[192,3072]{1,0:T(8,128)(2,1)}, bf16[192,3072]{1,0:T(8,128)(2,1)}, u32[]{:S(2)}, u32[]{:S(2)}) collective-permute-start(bf16[192,3072]{1,0:T(8,128)(2,1)} %pad_maximum_fusion.11), channel_id=1, source_target_pairs={{0,1},{1,0},{2,3},{3,2},{4,5},{5,4},{6,7},{7,6},{8,9},{9,8},{10,11... | collective-permute-start | bytes 3538952 | tf_op jit(solution)/shard_map/ppermute | solution.py:63
  330.1 42.1 %collective-permute-start.67 = (bf16[128,3072]{1,0:T(8,128)(2,1)S(1)}, bf16[128,3072]{1,0:T(8,128)(2,1)}, u32[]{:S(2)}, u32[]{:S(2)}) collective-permute-start(bf16[128,3072]{1,0:T(8,128)(2,1)S(1)} %get-tuple-element.384), channel_id=1, source_target_pairs={{0,16},{1,17},{2,18},{3,19},{4,20},{5,21},{6,22},{7,23},{8,24},{9,... | collective-permute-start | bytes 2359304 | tf_op jit(solution)/shard_map/ppermute | solution.py:63
  337.8 29.6 %collective-permute-start.56 = (bf16[64,768]{1,0:T(8,128)(2,1)S(1)}, bf16[64,768]{1,0:T(8,128)(2,1)S(1)}, u32[]{:S(2)}, u32[]{:S(2)}) collective-permute-start(bf16[64,768]{1,0:T(8,128)(2,1)S(1)} %get-tuple-element.473), channel_id=1, source_target_pairs={{0,0},{8,1},{16,2},{24,3},{25,4},{17,5},{9,6},{1,7},{2,8},{10,9},{... | collective-permute-start | bytes 294920 | tf_op jit(solution)/shard_map/ppermute | solution.py:629
  338.4 29.0 %collective-permute-start.57 = (bf16[64,768]{1,0:T(8,128)(2,1)S(1)}, bf16[64,768]{1,0:T(8,128)(2,1)S(1)}, u32[]{:S(2)}, u32[]{:S(2)}) collective-permute-start(bf16[64,768]{1,0:T(8,128)(2,1)S(1)} %get-tuple-element.472), channel_id=1, source_target_pairs={{1,0},{9,1},{17,2},{25,3},{24,4},{16,5},{8,6},{0,7},{3,8},{11,9},{... | collective-permute-start | bytes 294920 | tf_op jit(solution)/shard_map/ppermute | solution.py:629
  344.1 26.9 %collective-permute-start.65 = (bf16[1280,192]{0,1:T(8,128)(2,1)}, bf16[1280,192]{0,1:T(8,128)(2,1)}, u32[]{:S(2)}, u32[]{:S(2)}) collective-permute-start(bf16[1280,192]{0,1:T(8,128)(2,1)} %pad_maximum_fusion.26), channel_id=1, source_target_pairs={{0,16},{1,17},{2,18},{3,19},{4,20},{5,21},{6,22},{7,23},{8,24},{9,... | collective-permute-start | bytes 1474568 | tf_op jit(solution)/shard_map/ppermute | solution.py:63
  370.5 26.3 %collective-permute-start.58 = (bf16[128,1536]{1,0:T(8,128)(2,1)}, bf16[128,1536]{1,0:T(8,128)(2,1)S(1)}, u32[]{:S(2)}, u32[]{:S(2)}) collective-permute-start(bf16[128,1536]{1,0:T(8,128)(2,1)} %get-tuple-element.228), channel_id=1, source_target_pairs={{0,8},{1,9},{2,10},{3,11},{4,12},{5,13},{6,14},{7,15},{8,0},{9,1},... | collective-permute-start | bytes 1179656 | tf_op jit(solution)/shard_map/ppermute | solution.py:63
  377.7 19.1 %collective-permute-start.64 = (bf16[128,1536]{1,0:T(8,128)(2,1)S(1)}, bf16[128,1536]{1,0:T(8,128)(2,1)S(1)}, u32[]{:S(2)}, u32[]{:S(2)}) collective-permute-start(bf16[128,1536]{1,0:T(8,128)(2,1)S(1)} %fusion.483), channel_id=1, source_target_pairs={{0,17},{1,16},{2,19},{3,18},{4,21},{5,20},{6,23},{7,22},{8,25},{9,... | collective-permute-start | bytes 1179656 | tf_op jit(solution)/shard_map/ppermute | solution.py:63
  401.4 18.4 %collective-permute-start.71 = (bf16[128,768]{1,0:T(8,128)(2,1)S(1)}, bf16[128,768]{1,0:T(8,128)(2,1)S(1)}, u32[]{:S(2)}, u32[]{:S(2)}) collective-permute-start(bf16[128,768]{1,0:T(8,128)(2,1)S(1)} %get-tuple-element.374), channel_id=1, source_target_pairs={{0,16},{1,17},{2,18},{3,19},{4,20},{5,21},{6,22},{7,23},{8,24},{9,... | collective-permute-start | bytes 589832 | tf_op jit(solution)/shard_map/ppermute | solution.py:63
  413.9 40.5 %collective-permute-start.72 = (bf16[128,3840]{1,0:T(8,128)(2,1)}, bf16[128,3840]{1,0:T(8,128)(2,1)}, u32[]{:S(2)}, u32[]{:S(2)}) collective-permute-start(bf16[128,3840]{1,0:T(8,128)(2,1)} %pad_maximum_fusion.14), channel_id=1, source_target_pairs={{0,16},{1,17},{2,18},{3,19},{4,20},{5,21},{6,22},{7,23},{8,24},{9,... | collective-permute-start | bytes 2949128 | tf_op jit(solution)/shard_map/ppermute | solution.py:63
  415.7 38.6 %collective-permute-start.73 = (bf16[128,3072]{1,0:T(8,128)(2,1)S(1)}, bf16[128,3072]{1,0:T(8,128)(2,1)S(1)}, u32[]{:S(2)}, u32[]{:S(2)}) collective-permute-start(bf16[128,3072]{1,0:T(8,128)(2,1)S(1)} %pad_maximum_fusion.16), channel_id=1, source_target_pairs={{0,16},{1,17},{2,18},{3,19},{4,20},{5,21},{6,22},{7,23},{8,24},{9,... | collective-permute-start | bytes 2359304 | tf_op jit(solution)/shard_map/ppermute | solution.py:63
  417.1 40.8 %collective-permute-start.78 = (bf16[96,6144]{1,0:T(8,128)(2,1)}, bf16[96,6144]{1,0:T(8,128)(2,1)S(1)}, u32[]{:S(2)}, u32[]{:S(2)}) collective-permute-start(bf16[96,6144]{1,0:T(8,128)(2,1)} %slice.1009), channel_id=1, source_target_pairs={{0,1},{1,0},{2,3},{3,2},{4,5},{5,4},{6,7},{7,6},{8,9},{9,8},{10,11... | collective-permute-start | bytes 3538952 | tf_op jit(solution)/shard_map/ppermute | solution.py:63
  419.9 18.2 %collective-permute-start.76 = (bf16[256,768]{1,0:T(8,128)(2,1)S(1)}, bf16[256,768]{1,0:T(8,128)(2,1)S(1)}, u32[]{:S(2)}, u32[]{:S(2)}) collective-permute-start(bf16[256,768]{1,0:T(8,128)(2,1)S(1)} %pad_maximum_fusion.30), channel_id=1, source_target_pairs={{0,8},{1,9},{2,10},{3,11},{4,12},{5,13},{6,14},{7,15},{8,0},{9,1},... | collective-permute-start | bytes 1179656 | tf_op jit(solution)/shard_map/ppermute | solution.py:63
  440.1 16.7 %collective-permute-start.77 = (bf16[96,3072]{1,0:T(8,128)(2,1)S(1)}, bf16[96,3072]{1,0:T(8,128)(2,1)S(1)}, u32[]{:S(2)}, u32[]{:S(2)}) collective-permute-start(bf16[96,3072]{1,0:T(8,128)(2,1)S(1)} %slice.1212), channel_id=1, source_target_pairs={{0,1},{1,0},{2,3},{3,2},{4,5},{5,4},{6,7},{7,6},{8,9},{9,8},{10,11... | collective-permute-start | bytes 1769480 | tf_op jit(solution)/shard_map/ppermute | solution.py:63
  465.8 30.9 %collective-permute-start.89 = (bf16[256,3072]{1,0:T(8,128)(2,1)S(1)}, bf16[256,3072]{1,0:T(8,128)(2,1)S(1)}, u32[]{:S(2)}, u32[]{:S(2)}) collective-permute-start(bf16[256,3072]{1,0:T(8,128)(2,1)S(1)} %pad_maximum_fusion.5), channel_id=1, source_target_pairs={{0,8},{1,9},{2,10},{3,11},{4,12},{5,13},{6,14},{7,15},{8,0},{9,1},... | collective-permute-start | bytes 4718600 | tf_op jit(solution)/shard_map/ppermute | solution.py:63
  471.9 26.4 %collective-permute-start.92 = (bf16[256,3840]{1,0:T(8,128)(2,1)S(1)}, bf16[256,3840]{1,0:T(8,128)(2,1)S(1)}, u32[]{:S(2)}, u32[]{:S(2)}) collective-permute-start(bf16[256,3840]{1,0:T(8,128)(2,1)S(1)} %pad_maximum_fusion.1), channel_id=1, source_target_pairs={{0,8},{1,9},{2,10},{3,11},{4,12},{5,13},{6,14},{7,15},{8,0},{9,1},... | collective-permute-start | bytes 5898248 | tf_op jit(solution)/shard_map/ppermute | solution.py:63
  473.8 18.6 %collective-permute-start.85 = (bf16[128,1536]{1,0:T(8,128)(2,1)S(1)}, bf16[128,1536]{1,0:T(8,128)(2,1)S(1)}, u32[]{:S(2)}, u32[]{:S(2)}) collective-permute-start(bf16[128,1536]{1,0:T(8,128)(2,1)S(1)} %fusion.486), channel_id=1, source_target_pairs={{0,17},{1,16},{2,19},{3,18},{4,21},{5,20},{6,23},{7,22},{8,25},{9,... | collective-permute-start | bytes 1179656 | tf_op jit(solution)/shard_map/ppermute | solution.py:63
  484.0 16.9 %collective-permute-start.79 = (bf16[128,1536]{1,0:T(8,128)(2,1)S(1)}, bf16[128,1536]{1,0:T(8,128)(2,1)S(1)}, u32[]{:S(2)}, u32[]{:S(2)}) collective-permute-start(bf16[128,1536]{1,0:T(8,128)(2,1)S(1)} %copy-done.126), channel_id=1, source_target_pairs={{0,8},{1,9},{2,10},{3,11},{4,12},{5,13},{6,14},{7,15},{8,0},{9,1},... | collective-permute-start | bytes 1179656 | tf_op jit(solution)/shard_map/ppermute | solution.py:63
  510.4 29.8 %collective-permute-start.97 = (bf16[96,6912]{1,0:T(8,128)(2,1)}, bf16[96,6912]{1,0:T(8,128)(2,1)}, u32[]{:S(2)}, u32[]{:S(2)}) collective-permute-start(bf16[96,6912]{1,0:T(8,128)(2,1)} %slice.1033), channel_id=1, source_target_pairs={{0,1},{1,0},{2,3},{3,2},{4,5},{5,4},{6,7},{7,6},{8,9},{9,8},{10,11... | collective-permute-start | bytes 3981320 | tf_op jit(solution)/shard_map/ppermute | solution.py:63
  511.4 23.4 %collective-permute-start.93 = (bf16[128,2304]{1,0:T(8,128)(2,1)}, bf16[128,2304]{1,0:T(8,128)(2,1)}, u32[]{:S(2)}, u32[]{:S(2)}) collective-permute-start(bf16[128,2304]{1,0:T(8,128)(2,1)} %pad_maximum_fusion.23), channel_id=1, source_target_pairs={{0,16},{1,17},{2,18},{3,19},{4,20},{5,21},{6,22},{7,23},{8,24},{9,... | collective-permute-start | bytes 1769480 | tf_op jit(solution)/shard_map/ppermute | solution.py:63
  543.1 24.7 %collective-permute-start.98 = (bf16[512,768]{1,0:T(8,128)(2,1)S(1)}, bf16[512,768]{1,0:T(8,128)(2,1)S(1)}, u32[]{:S(2)}, u32[]{:S(2)}) collective-permute-start(bf16[512,768]{1,0:T(8,128)(2,1)S(1)} %pad_maximum_fusion.17), channel_id=1, source_target_pairs={{0,1},{1,0},{2,3},{3,2},{4,5},{5,4},{6,7},{7,6},{8,9},{9,8},{10,11... | collective-permute-start | bytes 2359304 | tf_op jit(solution)/shard_map/ppermute | solution.py:63
  544.2 23.6 %collective-permute-start.99 = (bf16[512,768]{1,0:T(8,128)(2,1)S(1)}, bf16[512,768]{1,0:T(8,128)(2,1)}, u32[]{:S(2)}, u32[]{:S(2)}) collective-permute-start(bf16[512,768]{1,0:T(8,128)(2,1)S(1)} %pad_maximum_fusion.17), channel_id=1, source_target_pairs={{0,16},{1,17},{2,18},{3,19},{4,20},{5,21},{6,22},{7,23},{8,24},{9,... | collective-permute-start | bytes 2359304 | tf_op jit(solution)/shard_map/ppermute | solution.py:63
  548.0 19.9 %collective-permute-start.101 = (bf16[48,6912]{1,0:T(8,128)(2,1)S(1)}, bf16[48,6912]{1,0:T(8,128)(2,1)S(1)}, u32[]{:S(2)}, u32[]{:S(2)}) collective-permute-start(bf16[48,6912]{1,0:T(8,128)(2,1)S(1)} %slice.1235), channel_id=1, source_target_pairs={{0,2},{1,3},{2,0},{3,1},{4,6},{5,7},{6,4},{7,5},{8,10},{9,11},{10,... | collective-permute-start | bytes 1990664 | tf_op jit(solution)/shard_map/ppermute | solution.py:63
  548.6 19.2 %collective-permute-start.102 = (bf16[48,3072]{1,0:T(8,128)(2,1)S(1)}, bf16[48,3072]{1,0:T(8,128)(2,1)S(1)}, u32[]{:S(2)}, u32[]{:S(2)}) collective-permute-start(bf16[48,3072]{1,0:T(8,128)(2,1)S(1)} %copy-done.56), channel_id=1, source_target_pairs={{0,2},{1,3},{2,0},{3,1},{4,6},{5,7},{6,4},{7,5},{8,10},{9,11},{10,... | collective-permute-start | bytes 884744 | tf_op jit(solution)/shard_map/ppermute | solution.py:63
  603.5 20.6 %collective-permute-start.114 = (f32[32,128]{1,0:T(8,128)S(1)}, f32[32,128]{1,0:T(8,128)S(1)}, u32[]{:S(2)}, u32[]{:S(2)}) collective-permute-start(f32[32,128]{1,0:T(8,128)S(1)} %fusion.570), channel_id=1, source_target_pairs={{0,4},{1,5},{2,6},{3,7},{4,0},{5,1},{6,2},{7,3},{8,12},{9,13},{10,... | collective-permute-start | bytes 49160 | tf_op jit(solution)/shard_map/ppermute | solution.py:63
  604.6 19.5 %collective-permute-start.115 = (bf16[48,2304]{1,0:T(8,128)(2,1)S(1)}, bf16[48,2304]{1,0:T(8,128)(2,1)S(1)}, u32[]{:S(2)}, u32[]{:S(2)}) collective-permute-start(bf16[48,2304]{1,0:T(8,128)(2,1)S(1)} %copy-done.59), channel_id=1, source_target_pairs={{0,2},{1,3},{2,0},{3,1},{4,6},{5,7},{6,4},{7,5},{8,10},{9,11},{10,... | collective-permute-start | bytes 663560 | tf_op jit(solution)/shard_map/ppermute | solution.py:63
  606.3 17.8 %collective-permute-start.116 = (bf16[24,3072]{1,0:T(8,128)(2,1)S(1)}, bf16[24,3072]{1,0:T(8,128)(2,1)S(1)}, u32[]{:S(2)}, u32[]{:S(2)}) collective-permute-start(bf16[24,3072]{1,0:T(8,128)(2,1)S(1)} %copy-done.63), channel_id=1, source_target_pairs={{0,4},{1,5},{2,6},{3,7},{4,0},{5,1},{6,2},{7,3},{8,12},{9,13},{10,... | collective-permute-start | bytes 442376 | tf_op jit(solution)/shard_map/ppermute | solution.py:63
  606.6 21.7 %collective-permute-start.117 = (bf16[24,6144]{1,0:T(8,128)(2,1)S(1)}, bf16[24,6144]{1,0:T(8,128)(2,1)S(1)}, u32[]{:S(2)}, u32[]{:S(2)}) collective-permute-start(bf16[24,6144]{1,0:T(8,128)(2,1)S(1)} %copy-done.55), channel_id=1, source_target_pairs={{0,4},{1,5},{2,6},{3,7},{4,0},{5,1},{6,2},{7,3},{8,12},{9,13},{10,... | collective-permute-start | bytes 884744 | tf_op jit(solution)/shard_map/ppermute | solution.py:63
  (216 other events, 1643.9 us)

commit v4 on v3

--- a/solution.py
+++ b/solution.py
@@ -251,7 +251,7 @@
             pltpu.SemaphoreType.DMA((2 * n,)),
         ],
         compiler_params=LIMIT,
-        cost_estimate=pl.CostEstimate(flops=10**10, bytes_accessed=8 * 2**20, transcendentals=2**20),
+        cost_estimate=pl.CostEstimate(flops=10**8, bytes_accessed=8 * 2**20, transcendentals=2**20),
         name="attend",
     )(rank, queries, pre, post, *pieces)
 
@@ -556,14 +556,6 @@
                 to = geo.device(b, h if h < n else 2 * n - 1 - h)
                 moves.append((b * n + block, to))
         return moves
-
-    flat, _ = lax.optimization_barrier((cotangent.reshape(tokens, D), stream))
-    evens = lax.ppermute(flat[:half], AXES, half_moves(0))
-    odds = lax.ppermute(flat[half:], AXES, half_moves(1))
-    even_rank = rank % 2 == 0
-    grad_stream = jnp.where(
-        even_rank, jnp.concatenate([evens, odds], axis=0), jnp.concatenate([odds, evens], axis=0)
-    ).astype(F32)
 
     near_masks = list(geo.plane)
     masks = [geo.rank_mask(m) for m in near_masks] + [geo.rank_mask(m ^ core) for m in near_masks]
@@ -620,6 +612,14 @@
             end_round(seventh, stream)
             eighth = begin_round(7, stream)
         saved.append((stream_in, n1, queries, pieces, attended, lse, pv, middle, n2, hidden, active, wide))
+
+    flat, _ = lax.optimization_barrier((cotangent.reshape(tokens, D), saved[1][0]))
+    evens = lax.ppermute(flat[:half], AXES, half_moves(0))
+    odds = lax.ppermute(flat[half:], AXES, half_moves(1))
+    even_rank = rank % 2 == 0
+    grad_stream = jnp.where(
+        even_rank, jnp.concatenate([evens, odds], axis=0), jnp.concatenate([odds, evens], axis=0)
+    ).astype(F32)
 
     final = stream.astype(BF16)
     back_even = [(b, a) for a, b in half_moves(0)]

time: 657 us -> 646 us (0.983)
  local copies, waits for them, and re-layouts: 105 us -> 96 us
    unnamed x319 -> x327, local copies, waits for them, and re-layouts: 42 us -> 33.9 us
  transfers between devices with their start and end apart: 122 -> 122, of which waited for: 42 -> 41; matrix products, arithmetic and copies ran while one was open for 33% -> 32% of each run, Pallas kernels for 9% -> 9%
where the time goes in v4:
time: 646 us; the launch traced here: 635 us
  waiting for transfers between devices  215 us (33%)
  starting transfers between devices  114 us (18%)
  matrix products  107 us (17%)
  local copies, waits for them, and re-layouts  96 us (15%)
  Pallas kernels  59.8 us (9%)
  other arithmetic  37.6 us (6%)
    ppermute x118, waiting for transfers between devices, swap(): return lax.ppermute(value, AXES, [(p, p ^ mask) for p in range(count)])  211 us
    ppermute x118, starting transfers between devices, swap(): return lax.ppermute(value, AXES, [(p, p ^ mask) for p in range(count)])  106 us
    dot_general x58, matrix products, mm(): return jnp.dot(a, b, preferred_element_type=F32)  66.3 us
    pallas_call x2, Pallas kernels, attend_back(): pl.pallas_call(functools.partial(backward_kernel, n, sources, count, mask...  36.3 us
    unnamed x327, local copies, waits for them, and re-layouts  33.9 us
    dot_general x42, matrix products, mm_t(): lax.dot_general(a, b, (((1,), (1,)), ((), ())), preferred_element_type=F32)  33 us
    pallas_call x2, Pallas kernels, attend(): pl.pallas_call(functools.partial(forward_kernel, n, sources, count, half)...  23.5 us
  transfers between devices with their start and end apart: 122, of which 41 were waited for; matrix products, arithmetic and copies ran while one was open for 32% of the time, Pallas kernels for 9%

profile of v4, /device:TPU:0, one launch (start us, length us, event | category | flops | bytes accessed | tf_op | source)
XLA Modules:
  0.0 634.8 jit_solution(5882983817557570064)
XLA Ops:
  0.7 3.0 collective-permute-start
  14.1 2.7 collective-permute-start.1
  30.3 2.9 collective-permute-start.12
  34.1 3.3 fusion.10
  37.4 9.4 %collective-permute-done.12 = bf16[24,6272]{1,0:T(8,128)(2,1)S(1)} collective-permute-done((bf16[24,6272]{1,0:T(8,128)(2,1)S(1)}, bf16[24,6272]{1,0:T(8,128)(2,1)S(1)}, u32[]{:S(2)}, u32[]{:S(2)}) %collective-permute-start.12) | collective-permute-done | bytes 301088 | tf_op jit(solution)/shard_map/ppermute | solution.py:63
  47.6 18.6 %collective-permute-done.5 = bf16[1004,768]{1,0:T(8,128)(2,1)} collective-permute-done((bf16[1004,768]{1,0:T(8,128)(2,1)}, bf16[1004,768]{1,0:T(8,128)(2,1)}, u32[]{:S(2)}, u32[]{:S(2)}) %collective-permute-start.5) | collective-permute-done | bytes 1542176 | tf_op jit(solution)/shard_map/ppermute | solution.py:63
  68.5 2.6 collective-permute-start.16
  71.1 3.3 fusion.8
  74.4 2.4 fusion.6
  78.9 5.6 collective-permute-done.16
  86.9 16.4 %collective-permute-done.8 = bf16[512,768]{1,0:T(8,128)(2,1)S(1)} collective-permute-done((bf16[512,768]{1,0:T(8,128)(2,1)S(1)}, bf16[512,768]{1,0:T(8,128)(2,1)S(1)}, u32[]{:S(2)}, u32[]{:S(2)}) %collective-permute-start.8) | collective-permute-done | bytes 786464 | tf_op jit(solution)/shard_map/ppermute | solution.py:63
  104.2 4.3 collective-permute-start.11
  109.7 4.6 collective-permute-done.11
  114.3 3.1 collective-permute-start.9
  118.5 12.2 %collective-permute-done.10 = bf16[128,768]{1,0:T(8,128)(2,1)S(1)} collective-permute-done((bf16[128,768]{1,0:T(8,128)(2,1)S(1)}, bf16[128,768]{1,0:T(8,128)(2,1)S(1)}, u32[]{:S(2)}, u32[]{:S(2)}) %collective-permute-start.10) | collective-permute-done | bytes 196640 | tf_op jit(solution)/shard_map/ppermute | solution.py:63
  130.7 2.9 collective-permute-done.9
  152.0 4.8 collective-permute-done.33
  163.6 3.3 collective-permute-done.22.rest_2_
  177.3 11.9 %attend.2 = (bf16[128,768]{1,0:T(8,128)(2,1)}, f32[2,8,768]{2,1,0:T(8,128)}, bf16[2,768,768]{2,1,0:T(8,128)(2,1)}) custom-call(s32[1]{0:T(128)} %bitcast.rank_ref, bf16[128,768]{1,0:T(8,128)(2,1)} %slice.1096.q_ref, f32[12,768]{1,0:T(8,128)} %mul.591.pre_ref, f32[12,768]{1,0:T(8,128)} %reshape.701.post_ref, bf16[128,1536]{1,0:T(8,128)(2,1)} %copy-done.29, ...), custom_call_target="tpu_custom_call" | custom-call | flops 100000000 | bytes 8388608 | tf_op jit(solution)/shard_map/attend/pallas_call | solution.py:235
  209.2 12.5 %collective-permute-done.90 = bf16[768,192]{0,1:T(8,128)(2,1)S(1)} collective-permute-done((bf16[768,192]{0,1:T(8,128)(2,1)S(1)}, bf16[768,192]{0,1:T(8,128)(2,1)S(1)}, u32[]{:S(2)}, u32[]{:S(2)}) %collective-permute-start.90) | collective-permute-done | bytes 294944 | tf_op jit(solution)/shard_map/ppermute | solution.py:63
  240.0 4.4 collective-permute-done.50
  248.7 3.8 collective-permute-done.40
  252.5 3.8 collective-permute-start.68
  258.4 2.7 collective-permute-start.43
  267.1 2.5 constant_dynamic-update-slice_fusion.28
  272.8 2.8 collective-permute-start.53
  277.0 11.6 %attend.3 = (bf16[128,768]{1,0:T(8,128)(2,1)}, f32[2,8,768]{2,1,0:T(8,128)}, bf16[2,768,768]{2,1,0:T(8,128)(2,1)}) custom-call(s32[1]{0:T(128)} %bitcast.rank_ref, bf16[128,768]{1,0:T(8,128)(2,1)} %slice.1134.q_ref, f32[12,768]{1,0:T(8,128)} %mul.613.pre_ref, f32[12,768]{1,0:T(8,128)} %reshape.704.post_ref, bf16[128,1536]{1,0:T(8,128)(2,1)} %copy-done.30, ...), custom_call_target="tpu_custom_call" | custom-call | flops 100000000 | bytes 8388608 | tf_op jit(solution)/shard_map/attend/pallas_call | solution.py:235
  295.6 4.1 collective-permute-done.52
  327.7 5.4 collective-permute-start.57
  338.6 18.3 %attend_back.2 = (bf16[128,768]{1,0:T(8,128)(2,1)}, f32[12,768]{1,0:T(8,128)}, f32[12,768]{1,0:T(8,128)}, bf16[128,1536]{1,0:T(8,128)(2,1)}, bf16[128,1536]{1,0:...) custom-call(s32[1]{0:T(128)} %bitcast.rank_ref, ...), custom_call_target="tpu_custom_call" | custom-call | flops 16000000000 | bytes 12582912 | tf_op jit(solution)/shard_map/attend_back/pallas_call | solution.py:266
  371.8 4.3 collective-permute-done.62
  376.1 9.3 %collective-permute-done.64 = bf16[128,1536]{1,0:T(8,128)(2,1)S(1)} collective-permute-done((bf16[128,1536]{1,0:T(8,128)(2,1)S(1)}, bf16[128,1536]{1,0:T(8,128)(2,1)S(1)}, u32[]{:S(2)}, u32[]{:S(2)}) %collective-permute-start.64) | collective-permute-done | bytes 393248 | tf_op jit(solution)/shard_map/ppermute | solution.py:63
  396.0 2.7 convolution_convert_fusion.32
  408.0 18.0 %attend_back.3 = (bf16[128,768]{1,0:T(8,128)(2,1)}, f32[12,768]{1,0:T(8,128)}, f32[12,768]{1,0:T(8,128)}, bf16[128,1536]{1,0:T(8,128)(2,1)}, bf16[128,1536]{1,0:...) custom-call(s32[1]{0:T(128)} %bitcast.rank_ref, ...), custom_call_target="tpu_custom_call" | custom-call | flops 16000000000 | bytes 12582912 | tf_op jit(solution)/shard_map/attend_back/pallas_call | solution.py:266
  431.4 11.3 %collective-permute-done.73 = bf16[128,3072]{1,0:T(8,128)(2,1)} collective-permute-done((bf16[128,3072]{1,0:T(8,128)(2,1)}, bf16[128,3072]{1,0:T(8,128)(2,1)}, u32[]{:S(2)}, u32[]{:S(2)}) %collective-permute-start.73) | collective-permute-done | bytes 786464 | tf_op jit(solution)/shard_map/ppermute | solution.py:63
  448.8 5.6 collective-permute-done.87
  455.7 3.0 collective-permute-done.81
  463.2 7.5 %collective-permute-done.83 = bf16[128,1536]{1,0:T(8,128)(2,1)S(1)} collective-permute-done((bf16[128,1536]{1,0:T(8,128)(2,1)S(1)}, bf16[128,1536]{1,0:T(8,128)(2,1)S(1)}, u32[]{:S(2)}, u32[]{:S(2)}) %collective-permute-start.83) | collective-permute-done | bytes 393248 | tf_op jit(solution)/shard_map/ppermute | solution.py:63
  473.2 7.9 %collective-permute-done.85 = bf16[128,1536]{1,0:T(8,128)(2,1)S(1)} collective-permute-done((bf16[128,1536]{1,0:T(8,128)(2,1)S(1)}, bf16[128,1536]{1,0:T(8,128)(2,1)S(1)}, u32[]{:S(2)}, u32[]{:S(2)}) %collective-permute-start.85) | collective-permute-done | bytes 393248 | tf_op jit(solution)/shard_map/ppermute | solution.py:63
  481.1 4.3 collective-permute-done.86
  518.3 4.9 collective-permute-done.95
  523.2 5.7 collective-permute-done.97
  543.3 7.1 %collective-permute-done.100 = f32[32,128]{1,0:T(8,128)S(1)} collective-permute-done((f32[32,128]{1,0:T(8,128)S(1)}, f32[32,128]{1,0:T(8,128)S(1)}, u32[]{:S(2)}, u32[]{:S(2)}) %collective-permute-start.100) | collective-permute-done | bytes 16416 | tf_op jit(solution)/shard_map/ppermute | solution.py:63
  550.4 6.5 %collective-permute-done.102 = bf16[48,3072]{1,0:T(8,128)(2,1)S(1)} collective-permute-done((bf16[48,3072]{1,0:T(8,128)(2,1)S(1)}, bf16[48,3072]{1,0:T(8,128)(2,1)S(1)}, u32[]{:S(2)}, u32[]{:S(2)}) %collective-permute-start.102) | collective-permute-done | bytes 294944 | tf_op jit(solution)/shard_map/ppermute | solution.py:63
  569.7 6.9 %collective-permute-done.108 = bf16[24,6912]{1,0:T(8,128)(2,1)S(1)} collective-permute-done((bf16[24,6912]{1,0:T(8,128)(2,1)S(1)}, bf16[24,6912]{1,0:T(8,128)(2,1)S(1)}, u32[]{:S(2)}, u32[]{:S(2)}) %collective-permute-start.108) | collective-permute-done | bytes 331808 | tf_op jit(solution)/shard_map/ppermute | solution.py:63
  588.0 2.5 stack_reshape.6
  602.0 11.3 %fusion = f32[1004,768]{1,0:T(8,128)} fusion(bf16[4096,768]{1,0:T(8,128)(2,1)} %constant_dynamic-update-slice_fusion.42, s32[4096]{0:T(1024)S(1)} %copy-done.127, s32[1004]{0:T(1024)S(1)} %copy-done.132), kind=kOutput, calls=%fused_computation.1 | convolution fusion | flops 6320734208 | bytes 9396144 | tf_op jit(solution)/shard_map/dot_general | solution.py:294
  613.3 4.1 collective-permute-done.117
  (881 shorter events, 318.3 us)
Async XLA Ops:
  29.6 44.8 %collective-permute-start.6 = (bf16[1004,768]{1,0:T(8,128)(2,1)}, bf16[1004,768]{1,0:T(8,128)(2,1)S(1)}, u32[]{:S(2)}, u32[]{:S(2)}) collective-permute-start(bf16[1004,768]{1,0:T(8,128)(2,1)} %param.15), channel_id=1, source_target_pairs={{0,8},{1,9},{2,10},{3,11},{4,12},{5,13},{6,14},{7,15},{8,0},{9,1},... | collective-permute-start | bytes 4626440 | tf_op jit(solution)/shard_map/ppermute | solution.py:63
  30.1 36.1 %collective-permute-start.5 = (bf16[1004,768]{1,0:T(8,128)(2,1)}, bf16[1004,768]{1,0:T(8,128)(2,1)}, u32[]{:S(2)}, u32[]{:S(2)}) collective-permute-start(bf16[1004,768]{1,0:T(8,128)(2,1)} %param.15), channel_id=1, source_target_pairs={{0,16},{1,17},{2,18},{3,19},{4,20},{5,21},{6,22},{7,23},{8,24},{9,... | collective-permute-start | bytes 4626440 | tf_op jit(solution)/shard_map/ppermute | solution.py:63
  46.8 19.5 %collective-permute-start.13 = (bf16[48,6272]{1,0:T(8,128)(2,1)S(1)}, bf16[48,6272]{1,0:T(8,128)(2,1)S(1)}, u32[]{:S(2)}, u32[]{:S(2)}) collective-permute-start(bf16[48,6272]{1,0:T(8,128)(2,1)S(1)} %pad_maximum_fusion.18), channel_id=1, source_target_pairs={{0,2},{1,3},{2,0},{3,1},{4,6},{5,7},{6,4},{7,5},{8,10},{9,11},{10,... | collective-permute-start | bytes 1806344 | tf_op jit(solution)/shard_map/ppermute | solution.py:63
  66.4 18.2 %collective-permute-start.14 = (bf16[96,3200]{1,0:T(8,128)(2,1)S(1)}, bf16[96,3200]{1,0:T(8,128)(2,1)S(1)}, u32[]{:S(2)}, u32[]{:S(2)}) collective-permute-start(bf16[96,3200]{1,0:T(8,128)(2,1)S(1)} %slice.1087), channel_id=1, source_target_pairs={{0,1},{1,0},{2,3},{3,2},{4,5},{5,4},{6,7},{7,6},{8,9},{9,8},{10,11... | collective-permute-start | bytes 1843208 | tf_op jit(solution)/shard_map/ppermute | solution.py:63
  68.0 16.6 %collective-permute-start.15 = (bf16[96,3072]{1,0:T(8,128)(2,1)S(1)}, bf16[96,3072]{1,0:T(8,128)(2,1)S(1)}, u32[]{:S(2)}, u32[]{:S(2)}) collective-permute-start(bf16[96,3072]{1,0:T(8,128)(2,1)S(1)} %slice.1088), channel_id=1, source_target_pairs={{0,16},{1,17},{2,18},{3,19},{4,20},{5,21},{6,22},{7,23},{8,24},{9,... | collective-permute-start | bytes 1769480 | tf_op jit(solution)/shard_map/ppermute | solution.py:63
  84.7 18.6 %collective-permute-start.8 = (bf16[512,768]{1,0:T(8,128)(2,1)S(1)}, bf16[512,768]{1,0:T(8,128)(2,1)S(1)}, u32[]{:S(2)}, u32[]{:S(2)}) collective-permute-start(bf16[512,768]{1,0:T(8,128)(2,1)S(1)} %slice.1082), channel_id=1, source_target_pairs={{0,1},{1,0},{2,3},{3,2},{4,5},{5,4},{6,7},{7,6},{8,9},{9,8},{10,11... | collective-permute-start | bytes 2359304 | tf_op jit(solution)/shard_map/ppermute | solution.py:63
  85.3 48.5 %collective-permute-start.17 = (bf16[192,3200]{1,0:T(8,128)(2,1)S(1)}, bf16[192,3200]{1,0:T(8,128)(2,1)S(1)}, u32[]{:S(2)}, u32[]{:S(2)}) collective-permute-start(bf16[192,3200]{1,0:T(8,128)(2,1)S(1)} %pad_maximum_fusion.6), channel_id=1, source_target_pairs={{0,16},{1,17},{2,18},{3,19},{4,20},{5,21},{6,22},{7,23},{8,24},{9,... | collective-permute-start | bytes 3686408 | tf_op jit(solution)/shard_map/ppermute | solution.py:63
  103.4 30.4 %collective-permute-start.18 = (bf16[192,3072]{1,0:T(8,128)(2,1)S(1)}, bf16[192,3072]{1,0:T(8,128)(2,1)S(1)}, u32[]{:S(2)}, u32[]{:S(2)}) collective-permute-start(bf16[192,3072]{1,0:T(8,128)(2,1)S(1)} %pad_maximum_fusion.7), channel_id=1, source_target_pairs={{0,1},{1,0},{2,3},{3,2},{4,5},{5,4},{6,7},{7,6},{8,9},{9,8},{10,11... | collective-permute-start | bytes 3538952 | tf_op jit(solution)/shard_map/ppermute | solution.py:63
  109.1 24.7 %collective-permute-start.19 = (bf16[48,6144]{1,0:T(8,128)(2,1)S(1)}, bf16[48,6144]{1,0:T(8,128)(2,1)S(1)}, u32[]{:S(2)}, u32[]{:S(2)}) collective-permute-start(bf16[48,6144]{1,0:T(8,128)(2,1)S(1)} %pad_maximum_fusion.19), channel_id=1, source_target_pairs={{0,2},{1,3},{2,0},{3,1},{4,6},{5,7},{6,4},{7,5},{8,10},{9,11},{10,... | collective-permute-start | bytes 1769480 | tf_op jit(solution)/shard_map/ppermute | solution.py:63
  109.1 21.6 %collective-permute-start.10 = (bf16[128,768]{1,0:T(8,128)(2,1)S(1)}, bf16[128,768]{1,0:T(8,128)(2,1)S(1)}, u32[]{:S(2)}, u32[]{:S(2)}) collective-permute-start(bf16[128,768]{1,0:T(8,128)(2,1)S(1)} %get-tuple-element.400), channel_id=1, source_target_pairs={{0,4},{1,5},{2,6},{3,7},{4,0},{5,1},{6,2},{7,3},{8,12},{9,13},{10,... | collective-permute-start | bytes 589832 | tf_op jit(solution)/shard_map/ppermute | solution.py:63
  114.3 19.3 %collective-permute-start.9 = (bf16[128,768]{1,0:T(8,128)(2,1)S(1)}, bf16[128,768]{1,0:T(8,128)(2,1)S(1)}, u32[]{:S(2)}, u32[]{:S(2)}) collective-permute-start(bf16[128,768]{1,0:T(8,128)(2,1)S(1)} %get-tuple-element.398), channel_id=1, source_target_pairs={{0,2},{1,3},{2,0},{3,1},{4,6},{5,7},{6,4},{7,5},{8,10},{9,11},{10,... | collective-permute-start | bytes 589832 | tf_op jit(solution)/shard_map/ppermute | solution.py:63
  137.6 19.7 %collective-permute-start.31 = (bf16[96,3072]{1,0:T(8,128)(2,1)}, bf16[96,3072]{1,0:T(8,128)(2,1)}, u32[]{:S(2)}, u32[]{:S(2)}) collective-permute-start(bf16[96,3072]{1,0:T(8,128)(2,1)} %get-tuple-element.192), channel_id=1, source_target_pairs={{0,1},{1,0},{2,3},{3,2},{4,5},{5,4},{6,7},{7,6},{8,9},{9,8},{10,11... | collective-permute-start | bytes 1769480 | tf_op jit(solution)/shard_map/ppermute | solution.py:63
  139.1 18.2 %collective-permute-start.32 = (bf16[96,3072]{1,0:T(8,128)(2,1)S(1)}, bf16[96,3072]{1,0:T(8,128)(2,1)}, u32[]{:S(2)}, u32[]{:S(2)}) collective-permute-start(bf16[96,3072]{1,0:T(8,128)(2,1)S(1)} %get-tuple-element.193), channel_id=1, source_target_pairs={{0,16},{1,17},{2,18},{3,19},{4,20},{5,21},{6,22},{7,23},{8,24},{9,... | collective-permute-start | bytes 1769480 | tf_op jit(solution)/shard_map/ppermute | solution.py:63
  142.6 52.2 %collective-permute-start.30 = (bf16[384,3072]{1,0:T(8,128)(2,1)S(1)}, bf16[384,3072]{1,0:T(8,128)(2,1)}, u32[]{:S(2)}, u32[]{:S(2)}) collective-permute-start(bf16[384,3072]{1,0:T(8,128)(2,1)S(1)} %constant_dynamic-update-slice_fusion.10), channel_id=1, source_target_pairs={{0,8},{1,9},{2,10},{3,11},{4,12},{5,13},{6,14},{7,15},{8,0},{9,1},... | collective-permute-start | bytes 7077896 | tf_op jit(solution)/shard_map/ppermute | solution.py:63
  174.4 48.1 %collective-permute-start.34 = (bf16[192,3072]{1,0:T(8,128)(2,1)S(1)}, bf16[192,3072]{1,0:T(8,128)(2,1)}, u32[]{:S(2)}, u32[]{:S(2)}) collective-permute-start(bf16[192,3072]{1,0:T(8,128)(2,1)S(1)} %pad_maximum_fusion.8), channel_id=1, source_target_pairs={{0,16},{1,17},{2,18},{3,19},{4,20},{5,21},{6,22},{7,23},{8,24},{9,... | collective-permute-start | bytes 3538952 | tf_op jit(solution)/shard_map/ppermute | solution.py:63
  175.0 47.5 %collective-permute-start.35 = (bf16[192,3072]{1,0:T(8,128)(2,1)S(1)}, bf16[192,3072]{1,0:T(8,128)(2,1)}, u32[]{:S(2)}, u32[]{:S(2)}) collective-permute-start(bf16[192,3072]{1,0:T(8,128)(2,1)S(1)} %pad_maximum_fusion.9), channel_id=1, source_target_pairs={{0,1},{1,0},{2,3},{3,2},{4,5},{5,4},{6,7},{7,6},{8,9},{9,8},{10,11... | collective-permute-start | bytes 3538952 | tf_op jit(solution)/shard_map/ppermute | solution.py:63
  176.5 46.0 %collective-permute-start.36 = (bf16[48,6144]{1,0:T(8,128)(2,1)}, bf16[48,6144]{1,0:T(8,128)(2,1)}, u32[]{:S(2)}, u32[]{:S(2)}) collective-permute-start(bf16[48,6144]{1,0:T(8,128)(2,1)} %pad_maximum_fusion.20), channel_id=1, source_target_pairs={{0,2},{1,3},{2,0},{3,1},{4,6},{5,7},{6,4},{7,5},{8,10},{9,11},{10,... | collective-permute-start | bytes 1769480 | tf_op jit(solution)/shard_map/ppermute | solution.py:63
  204.3 25.5 %collective-permute-start.74 = (bf16[1024,192]{0,1:T(8,128)(2,1)S(1)}, bf16[1024,192]{0,1:T(8,128)(2,1)S(1)}, u32[]{:S(2)}, u32[]{:S(2)}) collective-permute-start(bf16[1024,192]{0,1:T(8,128)(2,1)S(1)} %pad_maximum_fusion.31), channel_id=1, source_target_pairs={{0,16},{1,17},{2,18},{3,19},{4,20},{5,21},{6,22},{7,23},{8,24},{9,... | collective-permute-start | bytes 1179656 | tf_op jit(solution)/shard_map/ppermute | solution.py:63
  237.8 23.3 %collective-permute-start.41 = (bf16[128,1536]{1,0:T(8,128)(2,1)S(1)}, bf16[128,1536]{1,0:T(8,128)(2,1)S(1)}, u32[]{:S(2)}, u32[]{:S(2)}) collective-permute-start(bf16[128,1536]{1,0:T(8,128)(2,1)S(1)} %slice.1135.rest_0_), channel_id=1, source_target_pairs={{0,1},{1,0},{2,3},{3,2},{4,5},{5,4},{6,7},{7,6},{8,9},{9,8},{10,11... | collective-permute-start | bytes 1179656 | tf_op jit(solution)/shard_map/ppermute | solution.py:63
  239.4 19.0 %collective-permute-start.42 = (bf16[128,1536]{1,0:T(8,128)(2,1)S(1)}, bf16[128,1536]{1,0:T(8,128)(2,1)S(1)}, u32[]{:S(2)}, u32[]{:S(2)}) collective-permute-start(bf16[128,1536]{1,0:T(8,128)(2,1)S(1)} %slice.1135.rest_0_), channel_id=1, source_target_pairs={{0,16},{1,17},{2,18},{3,19},{4,20},{5,21},{6,22},{7,23},{8,24},{9,... | collective-permute-start | bytes 1179656 | tf_op jit(solution)/shard_map/ppermute | solution.py:63
  239.9 31.1 %collective-permute-start.45 = (bf16[128,1536]{1,0:T(8,128)(2,1)S(1)}, bf16[128,1536]{1,0:T(8,128)(2,1)S(1)}, u32[]{:S(2)}, u32[]{:S(2)}) collective-permute-start(bf16[128,1536]{1,0:T(8,128)(2,1)S(1)} %slice.1135.rest_0_), channel_id=1, source_target_pairs={{0,8},{1,9},{2,10},{3,11},{4,12},{5,13},{6,14},{7,15},{8,0},{9,1},... | collective-permute-start | bytes 1179656 | tf_op jit(solution)/shard_map/ppermute | solution.py:63
  271.0 28.7 %collective-permute-start.52 = (bf16[192,3072]{1,0:T(8,128)(2,1)}, bf16[192,3072]{1,0:T(8,128)(2,1)}, u32[]{:S(2)}, u32[]{:S(2)}) collective-permute-start(bf16[192,3072]{1,0:T(8,128)(2,1)} %pad_maximum_fusion.10), channel_id=1, source_target_pairs={{0,16},{1,17},{2,18},{3,19},{4,20},{5,21},{6,22},{7,23},{8,24},{9,... | collective-permute-start | bytes 3538952 | tf_op jit(solution)/shard_map/ppermute | solution.py:63
  272.8 29.2 %collective-permute-start.53 = (bf16[192,3072]{1,0:T(8,128)(2,1)S(1)}, bf16[192,3072]{1,0:T(8,128)(2,1)}, u32[]{:S(2)}, u32[]{:S(2)}) collective-permute-start(bf16[192,3072]{1,0:T(8,128)(2,1)S(1)} %pad_maximum_fusion.11), channel_id=1, source_target_pairs={{0,1},{1,0},{2,3},{3,2},{4,5},{5,4},{6,7},{7,6},{8,9},{9,8},{10,11... | collective-permute-start | bytes 3538952 | tf_op jit(solution)/shard_map/ppermute | solution.py:63
  318.5 43.5 %collective-permute-start.67 = (bf16[128,3072]{1,0:T(8,128)(2,1)S(1)}, bf16[128,3072]{1,0:T(8,128)(2,1)S(1)}, u32[]{:S(2)}, u32[]{:S(2)}) collective-permute-start(bf16[128,3072]{1,0:T(8,128)(2,1)S(1)} %get-tuple-element.384), channel_id=1, source_target_pairs={{0,16},{1,17},{2,18},{3,19},{4,20},{5,21},{6,22},{7,23},{8,24},{9,... | collective-permute-start | bytes 2359304 | tf_op jit(solution)/shard_map/ppermute | solution.py:63
  326.2 30.8 %collective-permute-start.56 = (bf16[64,768]{1,0:T(8,128)(2,1)}, bf16[64,768]{1,0:T(8,128)(2,1)S(1)}, u32[]{:S(2)}, u32[]{:S(2)}) collective-permute-start(bf16[64,768]{1,0:T(8,128)(2,1)} %get-tuple-element.473), channel_id=1, source_target_pairs={{0,0},{8,1},{16,2},{24,3},{25,4},{17,5},{9,6},{1,7},{2,8},{10,9},{... | collective-permute-start | bytes 294920 | tf_op jit(solution)/shard_map/ppermute | solution.py:629
  327.7 29.3 %collective-permute-start.57 = (bf16[64,768]{1,0:T(8,128)(2,1)S(1)}, bf16[64,768]{1,0:T(8,128)(2,1)S(1)}, u32[]{:S(2)}, u32[]{:S(2)}) collective-permute-start(bf16[64,768]{1,0:T(8,128)(2,1)S(1)} %get-tuple-element.472), channel_id=1, source_target_pairs={{1,0},{9,1},{17,2},{25,3},{24,4},{16,5},{8,6},{0,7},{3,8},{11,9},{... | collective-permute-start | bytes 294920 | tf_op jit(solution)/shard_map/ppermute | solution.py:629
  334.0 26.6 %collective-permute-start.65 = (bf16[1280,192]{0,1:T(8,128)(2,1)}, bf16[1280,192]{0,1:T(8,128)(2,1)}, u32[]{:S(2)}, u32[]{:S(2)}) collective-permute-start(bf16[1280,192]{0,1:T(8,128)(2,1)} %pad_maximum_fusion.26), channel_id=1, source_target_pairs={{0,16},{1,17},{2,18},{3,19},{4,20},{5,21},{6,22},{7,23},{8,24},{9,... | collective-permute-start | bytes 1474568 | tf_op jit(solution)/shard_map/ppermute | solution.py:63
  360.1 25.3 %collective-permute-start.58 = (bf16[128,1536]{1,0:T(8,128)(2,1)}, bf16[128,1536]{1,0:T(8,128)(2,1)S(1)}, u32[]{:S(2)}, u32[]{:S(2)}) collective-permute-start(bf16[128,1536]{1,0:T(8,128)(2,1)} %get-tuple-element.228), channel_id=1, source_target_pairs={{0,8},{1,9},{2,10},{3,11},{4,12},{5,13},{6,14},{7,15},{8,0},{9,1},... | collective-permute-start | bytes 1179656 | tf_op jit(solution)/shard_map/ppermute | solution.py:63
  366.7 18.6 %collective-permute-start.64 = (bf16[128,1536]{1,0:T(8,128)(2,1)S(1)}, bf16[128,1536]{1,0:T(8,128)(2,1)S(1)}, u32[]{:S(2)}, u32[]{:S(2)}) collective-permute-start(bf16[128,1536]{1,0:T(8,128)(2,1)S(1)} %fusion.483), channel_id=1, source_target_pairs={{0,17},{1,16},{2,19},{3,18},{4,21},{5,20},{6,23},{7,22},{8,25},{9,... | collective-permute-start | bytes 1179656 | tf_op jit(solution)/shard_map/ppermute | solution.py:63
  389.9 17.9 %collective-permute-start.71 = (bf16[128,768]{1,0:T(8,128)(2,1)S(1)}, bf16[128,768]{1,0:T(8,128)(2,1)S(1)}, u32[]{:S(2)}, u32[]{:S(2)}) collective-permute-start(bf16[128,768]{1,0:T(8,128)(2,1)S(1)} %get-tuple-element.374), channel_id=1, source_target_pairs={{0,16},{1,17},{2,18},{3,19},{4,20},{5,21},{6,22},{7,23},{8,24},{9,... | collective-permute-start | bytes 589832 | tf_op jit(solution)/shard_map/ppermute | solution.py:63
  402.6 41.5 %collective-permute-start.72 = (bf16[128,3840]{1,0:T(8,128)(2,1)S(1)}, bf16[128,3840]{1,0:T(8,128)(2,1)}, u32[]{:S(2)}, u32[]{:S(2)}) collective-permute-start(bf16[128,3840]{1,0:T(8,128)(2,1)S(1)} %pad_maximum_fusion.14), channel_id=1, source_target_pairs={{0,16},{1,17},{2,18},{3,19},{4,20},{5,21},{6,22},{7,23},{8,24},{9,... | collective-permute-start | bytes 2949128 | tf_op jit(solution)/shard_map/ppermute | solution.py:63
  404.3 38.4 %collective-permute-start.73 = (bf16[128,3072]{1,0:T(8,128)(2,1)}, bf16[128,3072]{1,0:T(8,128)(2,1)}, u32[]{:S(2)}, u32[]{:S(2)}) collective-permute-start(bf16[128,3072]{1,0:T(8,128)(2,1)} %pad_maximum_fusion.16), channel_id=1, source_target_pairs={{0,16},{1,17},{2,18},{3,19},{4,20},{5,21},{6,22},{7,23},{8,24},{9,... | collective-permute-start | bytes 2359304 | tf_op jit(solution)/shard_map/ppermute | solution.py:63
  404.7 41.9 %collective-permute-start.78 = (bf16[96,6144]{1,0:T(8,128)(2,1)S(1)}, bf16[96,6144]{1,0:T(8,128)(2,1)S(1)}, u32[]{:S(2)}, u32[]{:S(2)}) collective-permute-start(bf16[96,6144]{1,0:T(8,128)(2,1)S(1)} %slice.1009), channel_id=1, source_target_pairs={{0,1},{1,0},{2,3},{3,2},{4,5},{5,4},{6,7},{7,6},{8,9},{9,8},{10,11... | collective-permute-start | bytes 3538952 | tf_op jit(solution)/shard_map/ppermute | solution.py:63
  407.9 18.2 %collective-permute-start.76 = (bf16[256,768]{1,0:T(8,128)(2,1)S(1)}, bf16[256,768]{1,0:T(8,128)(2,1)}, u32[]{:S(2)}, u32[]{:S(2)}) collective-permute-start(bf16[256,768]{1,0:T(8,128)(2,1)S(1)} %pad_maximum_fusion.30), channel_id=1, source_target_pairs={{0,8},{1,9},{2,10},{3,11},{4,12},{5,13},{6,14},{7,15},{8,0},{9,1},... | collective-permute-start | bytes 1179656 | tf_op jit(solution)/shard_map/ppermute | solution.py:63
  454.5 30.9 %collective-permute-start.89 = (bf16[256,3072]{1,0:T(8,128)(2,1)S(1)}, bf16[256,3072]{1,0:T(8,128)(2,1)S(1)}, u32[]{:S(2)}, u32[]{:S(2)}) collective-permute-start(bf16[256,3072]{1,0:T(8,128)(2,1)S(1)} %pad_maximum_fusion.5), channel_id=1, source_target_pairs={{0,8},{1,9},{2,10},{3,11},{4,12},{5,13},{6,14},{7,15},{8,0},{9,1},... | collective-permute-start | bytes 4718600 | tf_op jit(solution)/shard_map/ppermute | solution.py:63
  461.1 25.9 %collective-permute-start.92 = (bf16[256,3840]{1,0:T(8,128)(2,1)S(1)}, bf16[256,3840]{1,0:T(8,128)(2,1)S(1)}, u32[]{:S(2)}, u32[]{:S(2)}) collective-permute-start(bf16[256,3840]{1,0:T(8,128)(2,1)S(1)} %pad_maximum_fusion.1), channel_id=1, source_target_pairs={{0,8},{1,9},{2,10},{3,11},{4,12},{5,13},{6,14},{7,15},{8,0},{9,1},... | collective-permute-start | bytes 5898248 | tf_op jit(solution)/shard_map/ppermute | solution.py:63
  463.0 18.1 %collective-permute-start.85 = (bf16[128,1536]{1,0:T(8,128)(2,1)S(1)}, bf16[128,1536]{1,0:T(8,128)(2,1)S(1)}, u32[]{:S(2)}, u32[]{:S(2)}) collective-permute-start(bf16[128,1536]{1,0:T(8,128)(2,1)S(1)} %fusion.486), channel_id=1, source_target_pairs={{0,17},{1,16},{2,19},{3,18},{4,21},{5,20},{6,23},{7,22},{8,25},{9,... | collective-permute-start | bytes 1179656 | tf_op jit(solution)/shard_map/ppermute | solution.py:63
  499.0 29.8 %collective-permute-start.97 = (bf16[96,6912]{1,0:T(8,128)(2,1)}, bf16[96,6912]{1,0:T(8,128)(2,1)}, u32[]{:S(2)}, u32[]{:S(2)}) collective-permute-start(bf16[96,6912]{1,0:T(8,128)(2,1)} %slice.1033), channel_id=1, source_target_pairs={{0,1},{1,0},{2,3},{3,2},{4,5},{5,4},{6,7},{7,6},{8,9},{9,8},{10,11... | collective-permute-start | bytes 3981320 | tf_op jit(solution)/shard_map/ppermute | solution.py:63
  500.6 22.6 %collective-permute-start.93 = (bf16[128,2304]{1,0:T(8,128)(2,1)}, bf16[128,2304]{1,0:T(8,128)(2,1)}, u32[]{:S(2)}, u32[]{:S(2)}) collective-permute-start(bf16[128,2304]{1,0:T(8,128)(2,1)} %pad_maximum_fusion.23), channel_id=1, source_target_pairs={{0,16},{1,17},{2,18},{3,19},{4,20},{5,21},{6,22},{7,23},{8,24},{9,... | collective-permute-start | bytes 1769480 | tf_op jit(solution)/shard_map/ppermute | solution.py:63
  531.7 25.2 %collective-permute-start.98 = (bf16[512,768]{1,0:T(8,128)(2,1)S(1)}, bf16[512,768]{1,0:T(8,128)(2,1)S(1)}, u32[]{:S(2)}, u32[]{:S(2)}) collective-permute-start(bf16[512,768]{1,0:T(8,128)(2,1)S(1)} %pad_maximum_fusion.17), channel_id=1, source_target_pairs={{0,1},{1,0},{2,3},{3,2},{4,5},{5,4},{6,7},{7,6},{8,9},{9,8},{10,11... | collective-permute-start | bytes 2359304 | tf_op jit(solution)/shard_map/ppermute | solution.py:63
  533.3 23.6 %collective-permute-start.99 = (bf16[512,768]{1,0:T(8,128)(2,1)S(1)}, bf16[512,768]{1,0:T(8,128)(2,1)}, u32[]{:S(2)}, u32[]{:S(2)}) collective-permute-start(bf16[512,768]{1,0:T(8,128)(2,1)S(1)} %pad_maximum_fusion.17), channel_id=1, source_target_pairs={{0,16},{1,17},{2,18},{3,19},{4,20},{5,21},{6,22},{7,23},{8,24},{9,... | collective-permute-start | bytes 2359304 | tf_op jit(solution)/shard_map/ppermute | solution.py:63
  537.1 19.9 %collective-permute-start.101 = (bf16[48,6912]{1,0:T(8,128)(2,1)S(1)}, bf16[48,6912]{1,0:T(8,128)(2,1)S(1)}, u32[]{:S(2)}, u32[]{:S(2)}) collective-permute-start(bf16[48,6912]{1,0:T(8,128)(2,1)S(1)} %slice.1235), channel_id=1, source_target_pairs={{0,2},{1,3},{2,0},{3,1},{4,6},{5,7},{6,4},{7,5},{8,10},{9,11},{10,... | collective-permute-start | bytes 1990664 | tf_op jit(solution)/shard_map/ppermute | solution.py:63
  537.7 19.3 %collective-permute-start.102 = (bf16[48,3072]{1,0:T(8,128)(2,1)S(1)}, bf16[48,3072]{1,0:T(8,128)(2,1)S(1)}, u32[]{:S(2)}, u32[]{:S(2)}) collective-permute-start(bf16[48,3072]{1,0:T(8,128)(2,1)S(1)} %copy-done.71), channel_id=1, source_target_pairs={{0,2},{1,3},{2,0},{3,1},{4,6},{5,7},{6,4},{7,5},{8,10},{9,11},{10,... | collective-permute-start | bytes 884744 | tf_op jit(solution)/shard_map/ppermute | solution.py:63
  560.1 16.5 %collective-permute-start.104 = (bf16[256,768]{1,0:T(8,128)(2,1)S(1)}, bf16[256,768]{1,0:T(8,128)(2,1)}, u32[]{:S(2)}, u32[]{:S(2)}) collective-permute-start(bf16[256,768]{1,0:T(8,128)(2,1)S(1)} %slice.1037), channel_id=1, source_target_pairs={{0,1},{1,0},{2,3},{3,2},{4,5},{5,4},{6,7},{7,6},{8,9},{9,8},{10,11... | collective-permute-start | bytes 1179656 | tf_op jit(solution)/shard_map/ppermute | solution.py:63
  592.6 20.7 %collective-permute-start.114 = (f32[32,128]{1,0:T(8,128)S(1)}, f32[32,128]{1,0:T(8,128)S(1)}, u32[]{:S(2)}, u32[]{:S(2)}) collective-permute-start(f32[32,128]{1,0:T(8,128)S(1)} %fusion.570), channel_id=1, source_target_pairs={{0,4},{1,5},{2,6},{3,7},{4,0},{5,1},{6,2},{7,3},{8,12},{9,13},{10,... | collective-permute-start | bytes 49160 | tf_op jit(solution)/shard_map/ppermute | solution.py:63
  594.7 18.6 %collective-permute-start.115 = (bf16[48,2304]{1,0:T(8,128)(2,1)S(1)}, bf16[48,2304]{1,0:T(8,128)(2,1)S(1)}, u32[]{:S(2)}, u32[]{:S(2)}) collective-permute-start(bf16[48,2304]{1,0:T(8,128)(2,1)S(1)} %copy-done.74), channel_id=1, source_target_pairs={{0,2},{1,3},{2,0},{3,1},{4,6},{5,7},{6,4},{7,5},{8,10},{9,11},{10,... | collective-permute-start | bytes 663560 | tf_op jit(solution)/shard_map/ppermute | solution.py:63
  595.5 17.8 %collective-permute-start.116 = (bf16[24,3072]{1,0:T(8,128)(2,1)S(1)}, bf16[24,3072]{1,0:T(8,128)(2,1)S(1)}, u32[]{:S(2)}, u32[]{:S(2)}) collective-permute-start(bf16[24,3072]{1,0:T(8,128)(2,1)S(1)} %copy-done.89), channel_id=1, source_target_pairs={{0,4},{1,5},{2,6},{3,7},{4,0},{5,1},{6,2},{7,3},{8,12},{9,13},{10,... | collective-permute-start | bytes 442376 | tf_op jit(solution)/shard_map/ppermute | solution.py:63
  596.2 21.3 %collective-permute-start.117 = (bf16[24,6144]{1,0:T(8,128)(2,1)S(1)}, bf16[24,6144]{1,0:T(8,128)(2,1)S(1)}, u32[]{:S(2)}, u32[]{:S(2)}) collective-permute-start(bf16[24,6144]{1,0:T(8,128)(2,1)S(1)} %copy-done.70), channel_id=1, source_target_pairs={{0,4},{1,5},{2,6},{3,7},{4,0},{5,1},{6,2},{7,3},{8,12},{9,13},{10,... | collective-permute-start | bytes 884744 | tf_op jit(solution)/shard_map/ppermute | solution.py:63
  (220 other events, 1741.2 us)

commit v5 on v4

--- a/solution.py
+++ b/solution.py
@@ -613,7 +613,7 @@
             eighth = begin_round(7, stream)
         saved.append((stream_in, n1, queries, pieces, attended, lse, pv, middle, n2, hidden, active, wide))
 
-    flat, _ = lax.optimization_barrier((cotangent.reshape(tokens, D), saved[1][0]))
+    flat, _ = lax.optimization_barrier((cotangent.reshape(tokens, D), saved[1][2]))
     evens = lax.ppermute(flat[:half], AXES, half_moves(0))
     odds = lax.ppermute(flat[half:], AXES, half_moves(1))
     even_rank = rank % 2 == 0

time: 646 us -> 645 us (level)
  no operation moved by 1% of the time
where the time goes in v5:
time: 645 us; the launch traced here: 634 us
  waiting for transfers between devices  214 us (33%)
  starting transfers between devices  114 us (18%)
  matrix products  108 us (17%)
  local copies, waits for them, and re-layouts  96 us (15%)
  Pallas kernels  59.8 us (9%)
  other arithmetic  37.5 us (6%)
    ppermute x118, waiting for transfers between devices, swap(): return lax.ppermute(value, AXES, [(p, p ^ mask) for p in range(count)])  210 us
    ppermute x118, starting transfers between devices, swap(): return lax.ppermute(value, AXES, [(p, p ^ mask) for p in range(count)])  106 us
    dot_general x58, matrix products, mm(): return jnp.dot(a, b, preferred_element_type=F32)  66.7 us
    pallas_call x2, Pallas kernels, attend_back(): pl.pallas_call(functools.partial(backward_kernel, n, sources, count, mask...  36.3 us
    unnamed x327, local copies, waits for them, and re-layouts  33.9 us
    dot_general x42, matrix products, mm_t(): lax.dot_general(a, b, (((1,), (1,)), ((), ())), preferred_element_type=F32)  33 us
    pallas_call x2, Pallas kernels, attend(): pl.pallas_call(functools.partial(forward_kernel, n, sources, count, half)...  23.5 us
  transfers between devices with their start and end apart: 122, of which 41 were waited for; matrix products, arithmetic and copies ran while one was open for 32% of the time, Pallas kernels for 9%

profile of v5, /device:TPU:0, one launch (start us, length us, event | category | flops | bytes accessed | tf_op | source)
XLA Modules:
  0.0 634.1 jit_solution(16307852600844543092)
XLA Ops:
  0.7 3.0 collective-permute-start
  14.1 2.7 collective-permute-start.1
  30.3 2.9 collective-permute-start.12
  34.1 3.3 fusion.10
  37.4 9.4 %collective-permute-done.12 = bf16[24,6272]{1,0:T(8,128)(2,1)S(1)} collective-permute-done((bf16[24,6272]{1,0:T(8,128)(2,1)S(1)}, bf16[24,6272]{1,0:T(8,128)(2,1)S(1)}, u32[]{:S(2)}, u32[]{:S(2)}) %collective-permute-start.12) | collective-permute-done | bytes 301088 | tf_op jit(solution)/shard_map/ppermute | solution.py:63
  47.6 18.6 %collective-permute-done.5 = bf16[1004,768]{1,0:T(8,128)(2,1)} collective-permute-done((bf16[1004,768]{1,0:T(8,128)(2,1)}, bf16[1004,768]{1,0:T(8,128)(2,1)}, u32[]{:S(2)}, u32[]{:S(2)}) %collective-permute-start.5) | collective-permute-done | bytes 1542176 | tf_op jit(solution)/shard_map/ppermute | solution.py:63
  68.5 2.6 collective-permute-start.16
  71.1 3.3 fusion.8
  79.0 5.6 collective-permute-done.16
  87.0 16.4 %collective-permute-done.8 = bf16[512,768]{1,0:T(8,128)(2,1)S(1)} collective-permute-done((bf16[512,768]{1,0:T(8,128)(2,1)S(1)}, bf16[512,768]{1,0:T(8,128)(2,1)S(1)}, u32[]{:S(2)}, u32[]{:S(2)}) %collective-permute-start.8) | collective-permute-done | bytes 786464 | tf_op jit(solution)/shard_map/ppermute | solution.py:63
  104.2 4.3 collective-permute-start.11
  109.7 4.6 collective-permute-done.11
  114.3 3.1 collective-permute-start.9
  118.5 12.2 %collective-permute-done.10 = bf16[128,768]{1,0:T(8,128)(2,1)S(1)} collective-permute-done((bf16[128,768]{1,0:T(8,128)(2,1)S(1)}, bf16[128,768]{1,0:T(8,128)(2,1)S(1)}, u32[]{:S(2)}, u32[]{:S(2)}) %collective-permute-start.10) | collective-permute-done | bytes 196640 | tf_op jit(solution)/shard_map/ppermute | solution.py:63
  130.7 2.9 collective-permute-done.9
  152.0 4.8 collective-permute-done.33
  163.6 3.3 collective-permute-done.22.rest_2_
  177.3 11.9 %attend.2 = (bf16[128,768]{1,0:T(8,128)(2,1)}, f32[2,8,768]{2,1,0:T(8,128)}, bf16[2,768,768]{2,1,0:T(8,128)(2,1)}) custom-call(s32[1]{0:T(128)} %bitcast.rank_ref, bf16[128,768]{1,0:T(8,128)(2,1)} %slice.1096.q_ref, f32[12,768]{1,0:T(8,128)} %mul.591.pre_ref, f32[12,768]{1,0:T(8,128)} %reshape.701.post_ref, bf16[128,1536]{1,0:T(8,128)(2,1)} %copy-done.29, ...), custom_call_target="tpu_custom_call" | custom-call | flops 100000000 | bytes 8388608 | tf_op jit(solution)/shard_map/attend/pallas_call | solution.py:235
  209.1 12.5 %collective-permute-done.90 = bf16[768,192]{0,1:T(8,128)(2,1)S(1)} collective-permute-done((bf16[768,192]{0,1:T(8,128)(2,1)S(1)}, bf16[768,192]{0,1:T(8,128)(2,1)S(1)}, u32[]{:S(2)}, u32[]{:S(2)}) %collective-permute-start.90) | collective-permute-done | bytes 294944 | tf_op jit(solution)/shard_map/ppermute | solution.py:63
  240.6 3.7 collective-permute-done.50
  248.7 3.8 collective-permute-done.40
  252.5 3.7 collective-permute-start.68
  258.4 2.7 collective-permute-start.43
  267.1 2.4 constant_dynamic-update-slice_fusion.28
  272.1 2.8 collective-permute-start.53
  276.3 11.6 %attend.3 = (bf16[128,768]{1,0:T(8,128)(2,1)}, f32[2,8,768]{2,1,0:T(8,128)}, bf16[2,768,768]{2,1,0:T(8,128)(2,1)}) custom-call(s32[1]{0:T(128)} %bitcast.rank_ref, bf16[128,768]{1,0:T(8,128)(2,1)} %slice.1134.q_ref, f32[12,768]{1,0:T(8,128)} %mul.613.pre_ref, f32[12,768]{1,0:T(8,128)} %reshape.704.post_ref, bf16[128,1536]{1,0:T(8,128)(2,1)} %copy-done.30, ...), custom_call_target="tpu_custom_call" | custom-call | flops 100000000 | bytes 8388608 | tf_op jit(solution)/shard_map/attend/pallas_call | solution.py:235
  288.0 2.5 convolution_convert_fusion.27
  295.2 3.8 collective-permute-done.52
  327.0 5.4 collective-permute-start.57
  337.9 18.3 %attend_back.2 = (bf16[128,768]{1,0:T(8,128)(2,1)}, f32[12,768]{1,0:T(8,128)}, f32[12,768]{1,0:T(8,128)}, bf16[128,1536]{1,0:T(8,128)(2,1)}, bf16[128,1536]{1,0:...) custom-call(s32[1]{0:T(128)} %bitcast.rank_ref, ...), custom_call_target="tpu_custom_call" | custom-call | flops 16000000000 | bytes 12582912 | tf_op jit(solution)/shard_map/attend_back/pallas_call | solution.py:266
  371.1 4.3 collective-permute-done.62
  375.4 9.3 %collective-permute-done.64 = bf16[128,1536]{1,0:T(8,128)(2,1)S(1)} collective-permute-done((bf16[128,1536]{1,0:T(8,128)(2,1)S(1)}, bf16[128,1536]{1,0:T(8,128)(2,1)S(1)}, u32[]{:S(2)}, u32[]{:S(2)}) %collective-permute-start.64) | collective-permute-done | bytes 393248 | tf_op jit(solution)/shard_map/ppermute | solution.py:63
  395.3 2.7 convolution_convert_fusion.32
  407.2 18.0 %attend_back.3 = (bf16[128,768]{1,0:T(8,128)(2,1)}, f32[12,768]{1,0:T(8,128)}, f32[12,768]{1,0:T(8,128)}, bf16[128,1536]{1,0:T(8,128)(2,1)}, bf16[128,1536]{1,0:...) custom-call(s32[1]{0:T(128)} %bitcast.rank_ref, ...), custom_call_target="tpu_custom_call" | custom-call | flops 16000000000 | bytes 12582912 | tf_op jit(solution)/shard_map/attend_back/pallas_call | solution.py:266
  430.7 11.3 %collective-permute-done.73 = bf16[128,3072]{1,0:T(8,128)(2,1)} collective-permute-done((bf16[128,3072]{1,0:T(8,128)(2,1)}, bf16[128,3072]{1,0:T(8,128)(2,1)}, u32[]{:S(2)}, u32[]{:S(2)}) %collective-permute-start.73) | collective-permute-done | bytes 786464 | tf_op jit(solution)/shard_map/ppermute | solution.py:63
  448.1 5.6 collective-permute-done.87
  455.0 3.0 collective-permute-done.81
  462.5 7.5 %collective-permute-done.83 = bf16[128,1536]{1,0:T(8,128)(2,1)S(1)} collective-permute-done((bf16[128,1536]{1,0:T(8,128)(2,1)S(1)}, bf16[128,1536]{1,0:T(8,128)(2,1)S(1)}, u32[]{:S(2)}, u32[]{:S(2)}) %collective-permute-start.83) | collective-permute-done | bytes 393248 | tf_op jit(solution)/shard_map/ppermute | solution.py:63
  472.5 7.9 %collective-permute-done.85 = bf16[128,1536]{1,0:T(8,128)(2,1)S(1)} collective-permute-done((bf16[128,1536]{1,0:T(8,128)(2,1)S(1)}, bf16[128,1536]{1,0:T(8,128)(2,1)S(1)}, u32[]{:S(2)}, u32[]{:S(2)}) %collective-permute-start.85) | collective-permute-done | bytes 393248 | tf_op jit(solution)/shard_map/ppermute | solution.py:63
  480.4 4.3 collective-permute-done.86
  517.5 4.9 collective-permute-done.95
  522.5 5.7 collective-permute-done.97
  542.6 7.1 %collective-permute-done.100 = f32[32,128]{1,0:T(8,128)S(1)} collective-permute-done((f32[32,128]{1,0:T(8,128)S(1)}, f32[32,128]{1,0:T(8,128)S(1)}, u32[]{:S(2)}, u32[]{:S(2)}) %collective-permute-start.100) | collective-permute-done | bytes 16416 | tf_op jit(solution)/shard_map/ppermute | solution.py:63
  549.7 6.5 %collective-permute-done.102 = bf16[48,3072]{1,0:T(8,128)(2,1)S(1)} collective-permute-done((bf16[48,3072]{1,0:T(8,128)(2,1)S(1)}, bf16[48,3072]{1,0:T(8,128)(2,1)S(1)}, u32[]{:S(2)}, u32[]{:S(2)}) %collective-permute-start.102) | collective-permute-done | bytes 294944 | tf_op jit(solution)/shard_map/ppermute | solution.py:63
  568.9 6.9 %collective-permute-done.108 = bf16[24,6912]{1,0:T(8,128)(2,1)S(1)} collective-permute-done((bf16[24,6912]{1,0:T(8,128)(2,1)S(1)}, bf16[24,6912]{1,0:T(8,128)(2,1)S(1)}, u32[]{:S(2)}, u32[]{:S(2)}) %collective-permute-start.108) | collective-permute-done | bytes 331808 | tf_op jit(solution)/shard_map/ppermute | solution.py:63
  587.2 2.5 stack_reshape.6
  601.2 11.3 %fusion = f32[1004,768]{1,0:T(8,128)} fusion(bf16[4096,768]{1,0:T(8,128)(2,1)} %constant_dynamic-update-slice_fusion.42, s32[4096]{0:T(1024)S(1)} %copy-done.127, s32[1004]{0:T(1024)S(1)} %copy-done.132), kind=kOutput, calls=%fused_computation.1 | convolution fusion | flops 6320734208 | bytes 9396144 | tf_op jit(solution)/shard_map/dot_general | solution.py:294
  612.6 4.1 collective-permute-done.117
  (881 shorter events, 318.5 us)
Async XLA Ops:
  29.6 44.8 %collective-permute-start.6 = (bf16[1004,768]{1,0:T(8,128)(2,1)}, bf16[1004,768]{1,0:T(8,128)(2,1)S(1)}, u32[]{:S(2)}, u32[]{:S(2)}) collective-permute-start(bf16[1004,768]{1,0:T(8,128)(2,1)} %param.15), channel_id=1, source_target_pairs={{0,8},{1,9},{2,10},{3,11},{4,12},{5,13},{6,14},{7,15},{8,0},{9,1},... | collective-permute-start | bytes 4626440 | tf_op jit(solution)/shard_map/ppermute | solution.py:63
  30.1 36.1 %collective-permute-start.5 = (bf16[1004,768]{1,0:T(8,128)(2,1)}, bf16[1004,768]{1,0:T(8,128)(2,1)}, u32[]{:S(2)}, u32[]{:S(2)}) collective-permute-start(bf16[1004,768]{1,0:T(8,128)(2,1)} %param.15), channel_id=1, source_target_pairs={{0,16},{1,17},{2,18},{3,19},{4,20},{5,21},{6,22},{7,23},{8,24},{9,... | collective-permute-start | bytes 4626440 | tf_op jit(solution)/shard_map/ppermute | solution.py:63
  46.8 19.5 %collective-permute-start.13 = (bf16[48,6272]{1,0:T(8,128)(2,1)S(1)}, bf16[48,6272]{1,0:T(8,128)(2,1)S(1)}, u32[]{:S(2)}, u32[]{:S(2)}) collective-permute-start(bf16[48,6272]{1,0:T(8,128)(2,1)S(1)} %pad_maximum_fusion.18), channel_id=1, source_target_pairs={{0,2},{1,3},{2,0},{3,1},{4,6},{5,7},{6,4},{7,5},{8,10},{9,11},{10,... | collective-permute-start | bytes 1806344 | tf_op jit(solution)/shard_map/ppermute | solution.py:63
  66.4 18.2 %collective-permute-start.14 = (bf16[96,3200]{1,0:T(8,128)(2,1)S(1)}, bf16[96,3200]{1,0:T(8,128)(2,1)S(1)}, u32[]{:S(2)}, u32[]{:S(2)}) collective-permute-start(bf16[96,3200]{1,0:T(8,128)(2,1)S(1)} %slice.1087), channel_id=1, source_target_pairs={{0,1},{1,0},{2,3},{3,2},{4,5},{5,4},{6,7},{7,6},{8,9},{9,8},{10,11... | collective-permute-start | bytes 1843208 | tf_op jit(solution)/shard_map/ppermute | solution.py:63
  68.0 16.6 %collective-permute-start.15 = (bf16[96,3072]{1,0:T(8,128)(2,1)S(1)}, bf16[96,3072]{1,0:T(8,128)(2,1)S(1)}, u32[]{:S(2)}, u32[]{:S(2)}) collective-permute-start(bf16[96,3072]{1,0:T(8,128)(2,1)S(1)} %slice.1088), channel_id=1, source_target_pairs={{0,16},{1,17},{2,18},{3,19},{4,20},{5,21},{6,22},{7,23},{8,24},{9,... | collective-permute-start | bytes 1769480 | tf_op jit(solution)/shard_map/ppermute | solution.py:63
  84.7 18.6 %collective-permute-start.8 = (bf16[512,768]{1,0:T(8,128)(2,1)S(1)}, bf16[512,768]{1,0:T(8,128)(2,1)S(1)}, u32[]{:S(2)}, u32[]{:S(2)}) collective-permute-start(bf16[512,768]{1,0:T(8,128)(2,1)S(1)} %slice.1082), channel_id=1, source_target_pairs={{0,1},{1,0},{2,3},{3,2},{4,5},{5,4},{6,7},{7,6},{8,9},{9,8},{10,11... | collective-permute-start | bytes 2359304 | tf_op jit(solution)/shard_map/ppermute | solution.py:63
  85.4 48.5 %collective-permute-start.17 = (bf16[192,3200]{1,0:T(8,128)(2,1)S(1)}, bf16[192,3200]{1,0:T(8,128)(2,1)S(1)}, u32[]{:S(2)}, u32[]{:S(2)}) collective-permute-start(bf16[192,3200]{1,0:T(8,128)(2,1)S(1)} %pad_maximum_fusion.6), channel_id=1, source_target_pairs={{0,16},{1,17},{2,18},{3,19},{4,20},{5,21},{6,22},{7,23},{8,24},{9,... | collective-permute-start | bytes 3686408 | tf_op jit(solution)/shard_map/ppermute | solution.py:63
  103.4 30.4 %collective-permute-start.18 = (bf16[192,3072]{1,0:T(8,128)(2,1)S(1)}, bf16[192,3072]{1,0:T(8,128)(2,1)S(1)}, u32[]{:S(2)}, u32[]{:S(2)}) collective-permute-start(bf16[192,3072]{1,0:T(8,128)(2,1)S(1)} %pad_maximum_fusion.7), channel_id=1, source_target_pairs={{0,1},{1,0},{2,3},{3,2},{4,5},{5,4},{6,7},{7,6},{8,9},{9,8},{10,11... | collective-permute-start | bytes 3538952 | tf_op jit(solution)/shard_map/ppermute | solution.py:63
  109.1 24.7 %collective-permute-start.19 = (bf16[48,6144]{1,0:T(8,128)(2,1)S(1)}, bf16[48,6144]{1,0:T(8,128)(2,1)S(1)}, u32[]{:S(2)}, u32[]{:S(2)}) collective-permute-start(bf16[48,6144]{1,0:T(8,128)(2,1)S(1)} %pad_maximum_fusion.19), channel_id=1, source_target_pairs={{0,2},{1,3},{2,0},{3,1},{4,6},{5,7},{6,4},{7,5},{8,10},{9,11},{10,... | collective-permute-start | bytes 1769480 | tf_op jit(solution)/shard_map/ppermute | solution.py:63
  109.1 21.6 %collective-permute-start.10 = (bf16[128,768]{1,0:T(8,128)(2,1)S(1)}, bf16[128,768]{1,0:T(8,128)(2,1)S(1)}, u32[]{:S(2)}, u32[]{:S(2)}) collective-permute-start(bf16[128,768]{1,0:T(8,128)(2,1)S(1)} %get-tuple-element.400), channel_id=1, source_target_pairs={{0,4},{1,5},{2,6},{3,7},{4,0},{5,1},{6,2},{7,3},{8,12},{9,13},{10,... | collective-permute-start | bytes 589832 | tf_op jit(solution)/shard_map/ppermute | solution.py:63
  114.3 19.3 %collective-permute-start.9 = (bf16[128,768]{1,0:T(8,128)(2,1)S(1)}, bf16[128,768]{1,0:T(8,128)(2,1)S(1)}, u32[]{:S(2)}, u32[]{:S(2)}) collective-permute-start(bf16[128,768]{1,0:T(8,128)(2,1)S(1)} %get-tuple-element.398), channel_id=1, source_target_pairs={{0,2},{1,3},{2,0},{3,1},{4,6},{5,7},{6,4},{7,5},{8,10},{9,11},{10,... | collective-permute-start | bytes 589832 | tf_op jit(solution)/shard_map/ppermute | solution.py:63
  137.6 19.7 %collective-permute-start.31 = (bf16[96,3072]{1,0:T(8,128)(2,1)}, bf16[96,3072]{1,0:T(8,128)(2,1)}, u32[]{:S(2)}, u32[]{:S(2)}) collective-permute-start(bf16[96,3072]{1,0:T(8,128)(2,1)} %get-tuple-element.192), channel_id=1, source_target_pairs={{0,1},{1,0},{2,3},{3,2},{4,5},{5,4},{6,7},{7,6},{8,9},{9,8},{10,11... | collective-permute-start | bytes 1769480 | tf_op jit(solution)/shard_map/ppermute | solution.py:63
  139.1 18.2 %collective-permute-start.32 = (bf16[96,3072]{1,0:T(8,128)(2,1)S(1)}, bf16[96,3072]{1,0:T(8,128)(2,1)}, u32[]{:S(2)}, u32[]{:S(2)}) collective-permute-start(bf16[96,3072]{1,0:T(8,128)(2,1)S(1)} %get-tuple-element.193), channel_id=1, source_target_pairs={{0,16},{1,17},{2,18},{3,19},{4,20},{5,21},{6,22},{7,23},{8,24},{9,... | collective-permute-start | bytes 1769480 | tf_op jit(solution)/shard_map/ppermute | solution.py:63
  142.6 52.2 %collective-permute-start.30 = (bf16[384,3072]{1,0:T(8,128)(2,1)S(1)}, bf16[384,3072]{1,0:T(8,128)(2,1)}, u32[]{:S(2)}, u32[]{:S(2)}) collective-permute-start(bf16[384,3072]{1,0:T(8,128)(2,1)S(1)} %constant_dynamic-update-slice_fusion.10), channel_id=1, source_target_pairs={{0,8},{1,9},{2,10},{3,11},{4,12},{5,13},{6,14},{7,15},{8,0},{9,1},... | collective-permute-start | bytes 7077896 | tf_op jit(solution)/shard_map/ppermute | solution.py:63
  174.4 48.0 %collective-permute-start.34 = (bf16[192,3072]{1,0:T(8,128)(2,1)S(1)}, bf16[192,3072]{1,0:T(8,128)(2,1)}, u32[]{:S(2)}, u32[]{:S(2)}) collective-permute-start(bf16[192,3072]{1,0:T(8,128)(2,1)S(1)} %pad_maximum_fusion.8), channel_id=1, source_target_pairs={{0,16},{1,17},{2,18},{3,19},{4,20},{5,21},{6,22},{7,23},{8,24},{9,... | collective-permute-start | bytes 3538952 | tf_op jit(solution)/shard_map/ppermute | solution.py:63
  175.0 47.4 %collective-permute-start.35 = (bf16[192,3072]{1,0:T(8,128)(2,1)S(1)}, bf16[192,3072]{1,0:T(8,128)(2,1)}, u32[]{:S(2)}, u32[]{:S(2)}) collective-permute-start(bf16[192,3072]{1,0:T(8,128)(2,1)S(1)} %pad_maximum_fusion.9), channel_id=1, source_target_pairs={{0,1},{1,0},{2,3},{3,2},{4,5},{5,4},{6,7},{7,6},{8,9},{9,8},{10,11... | collective-permute-start | bytes 3538952 | tf_op jit(solution)/shard_map/ppermute | solution.py:63
  176.6 45.9 %collective-permute-start.36 = (bf16[48,6144]{1,0:T(8,128)(2,1)}, bf16[48,6144]{1,0:T(8,128)(2,1)}, u32[]{:S(2)}, u32[]{:S(2)}) collective-permute-start(bf16[48,6144]{1,0:T(8,128)(2,1)} %pad_maximum_fusion.20), channel_id=1, source_target_pairs={{0,2},{1,3},{2,0},{3,1},{4,6},{5,7},{6,4},{7,5},{8,10},{9,11},{10,... | collective-permute-start | bytes 1769480 | tf_op jit(solution)/shard_map/ppermute | solution.py:63
  204.3 25.5 %collective-permute-start.74 = (bf16[1024,192]{0,1:T(8,128)(2,1)S(1)}, bf16[1024,192]{0,1:T(8,128)(2,1)S(1)}, u32[]{:S(2)}, u32[]{:S(2)}) collective-permute-start(bf16[1024,192]{0,1:T(8,128)(2,1)S(1)} %pad_maximum_fusion.31), channel_id=1, source_target_pairs={{0,16},{1,17},{2,18},{3,19},{4,20},{5,21},{6,22},{7,23},{8,24},{9,... | collective-permute-start | bytes 1179656 | tf_op jit(solution)/shard_map/ppermute | solution.py:63
  238.5 22.6 %collective-permute-start.41 = (bf16[128,1536]{1,0:T(8,128)(2,1)S(1)}, bf16[128,1536]{1,0:T(8,128)(2,1)S(1)}, u32[]{:S(2)}, u32[]{:S(2)}) collective-permute-start(bf16[128,1536]{1,0:T(8,128)(2,1)S(1)} %slice.1135.rest_0_), channel_id=1, source_target_pairs={{0,1},{1,0},{2,3},{3,2},{4,5},{5,4},{6,7},{7,6},{8,9},{9,8},{10,11... | collective-permute-start | bytes 1179656 | tf_op jit(solution)/shard_map/ppermute | solution.py:63
  240.1 18.3 %collective-permute-start.42 = (bf16[128,1536]{1,0:T(8,128)(2,1)S(1)}, bf16[128,1536]{1,0:T(8,128)(2,1)S(1)}, u32[]{:S(2)}, u32[]{:S(2)}) collective-permute-start(bf16[128,1536]{1,0:T(8,128)(2,1)S(1)} %slice.1135.rest_0_), channel_id=1, source_target_pairs={{0,16},{1,17},{2,18},{3,19},{4,20},{5,21},{6,22},{7,23},{8,24},{9,... | collective-permute-start | bytes 1179656 | tf_op jit(solution)/shard_map/ppermute | solution.py:63
  240.6 29.7 %collective-permute-start.45 = (bf16[128,1536]{1,0:T(8,128)(2,1)S(1)}, bf16[128,1536]{1,0:T(8,128)(2,1)S(1)}, u32[]{:S(2)}, u32[]{:S(2)}) collective-permute-start(bf16[128,1536]{1,0:T(8,128)(2,1)S(1)} %slice.1135.rest_0_), channel_id=1, source_target_pairs={{0,8},{1,9},{2,10},{3,11},{4,12},{5,13},{6,14},{7,15},{8,0},{9,1},... | collective-permute-start | bytes 1179656 | tf_op jit(solution)/shard_map/ppermute | solution.py:63
  270.3 28.7 %collective-permute-start.52 = (bf16[192,3072]{1,0:T(8,128)(2,1)}, bf16[192,3072]{1,0:T(8,128)(2,1)}, u32[]{:S(2)}, u32[]{:S(2)}) collective-permute-start(bf16[192,3072]{1,0:T(8,128)(2,1)} %pad_maximum_fusion.10), channel_id=1, source_target_pairs={{0,16},{1,17},{2,18},{3,19},{4,20},{5,21},{6,22},{7,23},{8,24},{9,... | collective-permute-start | bytes 3538952 | tf_op jit(solution)/shard_map/ppermute | solution.py:63
  272.1 29.2 %collective-permute-start.53 = (bf16[192,3072]{1,0:T(8,128)(2,1)S(1)}, bf16[192,3072]{1,0:T(8,128)(2,1)}, u32[]{:S(2)}, u32[]{:S(2)}) collective-permute-start(bf16[192,3072]{1,0:T(8,128)(2,1)S(1)} %pad_maximum_fusion.11), channel_id=1, source_target_pairs={{0,1},{1,0},{2,3},{3,2},{4,5},{5,4},{6,7},{7,6},{8,9},{9,8},{10,11... | collective-permute-start | bytes 3538952 | tf_op jit(solution)/shard_map/ppermute | solution.py:63
  317.7 43.5 %collective-permute-start.67 = (bf16[128,3072]{1,0:T(8,128)(2,1)S(1)}, bf16[128,3072]{1,0:T(8,128)(2,1)S(1)}, u32[]{:S(2)}, u32[]{:S(2)}) collective-permute-start(bf16[128,3072]{1,0:T(8,128)(2,1)S(1)} %get-tuple-element.384), channel_id=1, source_target_pairs={{0,16},{1,17},{2,18},{3,19},{4,20},{5,21},{6,22},{7,23},{8,24},{9,... | collective-permute-start | bytes 2359304 | tf_op jit(solution)/shard_map/ppermute | solution.py:63
  325.5 30.8 %collective-permute-start.56 = (bf16[64,768]{1,0:T(8,128)(2,1)}, bf16[64,768]{1,0:T(8,128)(2,1)S(1)}, u32[]{:S(2)}, u32[]{:S(2)}) collective-permute-start(bf16[64,768]{1,0:T(8,128)(2,1)} %get-tuple-element.473), channel_id=1, source_target_pairs={{0,0},{8,1},{16,2},{24,3},{25,4},{17,5},{9,6},{1,7},{2,8},{10,9},{... | collective-permute-start | bytes 294920 | tf_op jit(solution)/shard_map/ppermute | solution.py:629
  327.0 29.3 %collective-permute-start.57 = (bf16[64,768]{1,0:T(8,128)(2,1)S(1)}, bf16[64,768]{1,0:T(8,128)(2,1)S(1)}, u32[]{:S(2)}, u32[]{:S(2)}) collective-permute-start(bf16[64,768]{1,0:T(8,128)(2,1)S(1)} %get-tuple-element.472), channel_id=1, source_target_pairs={{1,0},{9,1},{17,2},{25,3},{24,4},{16,5},{8,6},{0,7},{3,8},{11,9},{... | collective-permute-start | bytes 294920 | tf_op jit(solution)/shard_map/ppermute | solution.py:629
  333.3 26.7 %collective-permute-start.65 = (bf16[1280,192]{0,1:T(8,128)(2,1)}, bf16[1280,192]{0,1:T(8,128)(2,1)}, u32[]{:S(2)}, u32[]{:S(2)}) collective-permute-start(bf16[1280,192]{0,1:T(8,128)(2,1)} %pad_maximum_fusion.26), channel_id=1, source_target_pairs={{0,16},{1,17},{2,18},{3,19},{4,20},{5,21},{6,22},{7,23},{8,24},{9,... | collective-permute-start | bytes 1474568 | tf_op jit(solution)/shard_map/ppermute | solution.py:63
  359.4 25.3 %collective-permute-start.58 = (bf16[128,1536]{1,0:T(8,128)(2,1)}, bf16[128,1536]{1,0:T(8,128)(2,1)S(1)}, u32[]{:S(2)}, u32[]{:S(2)}) collective-permute-start(bf16[128,1536]{1,0:T(8,128)(2,1)} %get-tuple-element.228), channel_id=1, source_target_pairs={{0,8},{1,9},{2,10},{3,11},{4,12},{5,13},{6,14},{7,15},{8,0},{9,1},... | collective-permute-start | bytes 1179656 | tf_op jit(solution)/shard_map/ppermute | solution.py:63
  366.0 18.6 %collective-permute-start.64 = (bf16[128,1536]{1,0:T(8,128)(2,1)S(1)}, bf16[128,1536]{1,0:T(8,128)(2,1)S(1)}, u32[]{:S(2)}, u32[]{:S(2)}) collective-permute-start(bf16[128,1536]{1,0:T(8,128)(2,1)S(1)} %fusion.483), channel_id=1, source_target_pairs={{0,17},{1,16},{2,19},{3,18},{4,21},{5,20},{6,23},{7,22},{8,25},{9,... | collective-permute-start | bytes 1179656 | tf_op jit(solution)/shard_map/ppermute | solution.py:63
  389.2 17.9 %collective-permute-start.71 = (bf16[128,768]{1,0:T(8,128)(2,1)S(1)}, bf16[128,768]{1,0:T(8,128)(2,1)S(1)}, u32[]{:S(2)}, u32[]{:S(2)}) collective-permute-start(bf16[128,768]{1,0:T(8,128)(2,1)S(1)} %get-tuple-element.374), channel_id=1, source_target_pairs={{0,16},{1,17},{2,18},{3,19},{4,20},{5,21},{6,22},{7,23},{8,24},{9,... | collective-permute-start | bytes 589832 | tf_op jit(solution)/shard_map/ppermute | solution.py:63
  401.8 41.5 %collective-permute-start.72 = (bf16[128,3840]{1,0:T(8,128)(2,1)S(1)}, bf16[128,3840]{1,0:T(8,128)(2,1)}, u32[]{:S(2)}, u32[]{:S(2)}) collective-permute-start(bf16[128,3840]{1,0:T(8,128)(2,1)S(1)} %pad_maximum_fusion.14), channel_id=1, source_target_pairs={{0,16},{1,17},{2,18},{3,19},{4,20},{5,21},{6,22},{7,23},{8,24},{9,... | collective-permute-start | bytes 2949128 | tf_op jit(solution)/shard_map/ppermute | solution.py:63
  403.6 38.4 %collective-permute-start.73 = (bf16[128,3072]{1,0:T(8,128)(2,1)}, bf16[128,3072]{1,0:T(8,128)(2,1)}, u32[]{:S(2)}, u32[]{:S(2)}) collective-permute-start(bf16[128,3072]{1,0:T(8,128)(2,1)} %pad_maximum_fusion.16), channel_id=1, source_target_pairs={{0,16},{1,17},{2,18},{3,19},{4,20},{5,21},{6,22},{7,23},{8,24},{9,... | collective-permute-start | bytes 2359304 | tf_op jit(solution)/shard_map/ppermute | solution.py:63
  404.0 41.9 %collective-permute-start.78 = (bf16[96,6144]{1,0:T(8,128)(2,1)S(1)}, bf16[96,6144]{1,0:T(8,128)(2,1)S(1)}, u32[]{:S(2)}, u32[]{:S(2)}) collective-permute-start(bf16[96,6144]{1,0:T(8,128)(2,1)S(1)} %slice.1009), channel_id=1, source_target_pairs={{0,1},{1,0},{2,3},{3,2},{4,5},{5,4},{6,7},{7,6},{8,9},{9,8},{10,11... | collective-permute-start | bytes 3538952 | tf_op jit(solution)/shard_map/ppermute | solution.py:63
  407.1 18.2 %collective-permute-start.76 = (bf16[256,768]{1,0:T(8,128)(2,1)S(1)}, bf16[256,768]{1,0:T(8,128)(2,1)}, u32[]{:S(2)}, u32[]{:S(2)}) collective-permute-start(bf16[256,768]{1,0:T(8,128)(2,1)S(1)} %pad_maximum_fusion.30), channel_id=1, source_target_pairs={{0,8},{1,9},{2,10},{3,11},{4,12},{5,13},{6,14},{7,15},{8,0},{9,1},... | collective-permute-start | bytes 1179656 | tf_op jit(solution)/shard_map/ppermute | solution.py:63
  453.8 30.9 %collective-permute-start.89 = (bf16[256,3072]{1,0:T(8,128)(2,1)S(1)}, bf16[256,3072]{1,0:T(8,128)(2,1)S(1)}, u32[]{:S(2)}, u32[]{:S(2)}) collective-permute-start(bf16[256,3072]{1,0:T(8,128)(2,1)S(1)} %pad_maximum_fusion.5), channel_id=1, source_target_pairs={{0,8},{1,9},{2,10},{3,11},{4,12},{5,13},{6,14},{7,15},{8,0},{9,1},... | collective-permute-start | bytes 4718600 | tf_op jit(solution)/shard_map/ppermute | solution.py:63
  460.3 25.9 %collective-permute-start.92 = (bf16[256,3840]{1,0:T(8,128)(2,1)S(1)}, bf16[256,3840]{1,0:T(8,128)(2,1)S(1)}, u32[]{:S(2)}, u32[]{:S(2)}) collective-permute-start(bf16[256,3840]{1,0:T(8,128)(2,1)S(1)} %pad_maximum_fusion.1), channel_id=1, source_target_pairs={{0,8},{1,9},{2,10},{3,11},{4,12},{5,13},{6,14},{7,15},{8,0},{9,1},... | collective-permute-start | bytes 5898248 | tf_op jit(solution)/shard_map/ppermute | solution.py:63
  462.3 18.1 %collective-permute-start.85 = (bf16[128,1536]{1,0:T(8,128)(2,1)S(1)}, bf16[128,1536]{1,0:T(8,128)(2,1)S(1)}, u32[]{:S(2)}, u32[]{:S(2)}) collective-permute-start(bf16[128,1536]{1,0:T(8,128)(2,1)S(1)} %fusion.486), channel_id=1, source_target_pairs={{0,17},{1,16},{2,19},{3,18},{4,21},{5,20},{6,23},{7,22},{8,25},{9,... | collective-permute-start | bytes 1179656 | tf_op jit(solution)/shard_map/ppermute | solution.py:63
  498.3 29.8 %collective-permute-start.97 = (bf16[96,6912]{1,0:T(8,128)(2,1)}, bf16[96,6912]{1,0:T(8,128)(2,1)}, u32[]{:S(2)}, u32[]{:S(2)}) collective-permute-start(bf16[96,6912]{1,0:T(8,128)(2,1)} %slice.1033), channel_id=1, source_target_pairs={{0,1},{1,0},{2,3},{3,2},{4,5},{5,4},{6,7},{7,6},{8,9},{9,8},{10,11... | collective-permute-start | bytes 3981320 | tf_op jit(solution)/shard_map/ppermute | solution.py:63
  499.9 22.6 %collective-permute-start.93 = (bf16[128,2304]{1,0:T(8,128)(2,1)}, bf16[128,2304]{1,0:T(8,128)(2,1)}, u32[]{:S(2)}, u32[]{:S(2)}) collective-permute-start(bf16[128,2304]{1,0:T(8,128)(2,1)} %pad_maximum_fusion.23), channel_id=1, source_target_pairs={{0,16},{1,17},{2,18},{3,19},{4,20},{5,21},{6,22},{7,23},{8,24},{9,... | collective-permute-start | bytes 1769480 | tf_op jit(solution)/shard_map/ppermute | solution.py:63
  531.0 25.2 %collective-permute-start.98 = (bf16[512,768]{1,0:T(8,128)(2,1)S(1)}, bf16[512,768]{1,0:T(8,128)(2,1)S(1)}, u32[]{:S(2)}, u32[]{:S(2)}) collective-permute-start(bf16[512,768]{1,0:T(8,128)(2,1)S(1)} %pad_maximum_fusion.17), channel_id=1, source_target_pairs={{0,1},{1,0},{2,3},{3,2},{4,5},{5,4},{6,7},{7,6},{8,9},{9,8},{10,11... | collective-permute-start | bytes 2359304 | tf_op jit(solution)/shard_map/ppermute | solution.py:63
  532.6 23.6 %collective-permute-start.99 = (bf16[512,768]{1,0:T(8,128)(2,1)S(1)}, bf16[512,768]{1,0:T(8,128)(2,1)}, u32[]{:S(2)}, u32[]{:S(2)}) collective-permute-start(bf16[512,768]{1,0:T(8,128)(2,1)S(1)} %pad_maximum_fusion.17), channel_id=1, source_target_pairs={{0,16},{1,17},{2,18},{3,19},{4,20},{5,21},{6,22},{7,23},{8,24},{9,... | collective-permute-start | bytes 2359304 | tf_op jit(solution)/shard_map/ppermute | solution.py:63
  536.3 19.9 %collective-permute-start.101 = (bf16[48,6912]{1,0:T(8,128)(2,1)S(1)}, bf16[48,6912]{1,0:T(8,128)(2,1)S(1)}, u32[]{:S(2)}, u32[]{:S(2)}) collective-permute-start(bf16[48,6912]{1,0:T(8,128)(2,1)S(1)} %slice.1235), channel_id=1, source_target_pairs={{0,2},{1,3},{2,0},{3,1},{4,6},{5,7},{6,4},{7,5},{8,10},{9,11},{10,... | collective-permute-start | bytes 1990664 | tf_op jit(solution)/shard_map/ppermute | solution.py:63
  536.9 19.3 %collective-permute-start.102 = (bf16[48,3072]{1,0:T(8,128)(2,1)S(1)}, bf16[48,3072]{1,0:T(8,128)(2,1)S(1)}, u32[]{:S(2)}, u32[]{:S(2)}) collective-permute-start(bf16[48,3072]{1,0:T(8,128)(2,1)S(1)} %copy-done.70), channel_id=1, source_target_pairs={{0,2},{1,3},{2,0},{3,1},{4,6},{5,7},{6,4},{7,5},{8,10},{9,11},{10,... | collective-permute-start | bytes 884744 | tf_op jit(solution)/shard_map/ppermute | solution.py:63
  559.4 16.5 %collective-permute-start.104 = (bf16[256,768]{1,0:T(8,128)(2,1)S(1)}, bf16[256,768]{1,0:T(8,128)(2,1)}, u32[]{:S(2)}, u32[]{:S(2)}) collective-permute-start(bf16[256,768]{1,0:T(8,128)(2,1)S(1)} %slice.1037), channel_id=1, source_target_pairs={{0,1},{1,0},{2,3},{3,2},{4,5},{5,4},{6,7},{7,6},{8,9},{9,8},{10,11... | collective-permute-start | bytes 1179656 | tf_op jit(solution)/shard_map/ppermute | solution.py:63
  591.9 20.7 %collective-permute-start.114 = (f32[32,128]{1,0:T(8,128)S(1)}, f32[32,128]{1,0:T(8,128)S(1)}, u32[]{:S(2)}, u32[]{:S(2)}) collective-permute-start(f32[32,128]{1,0:T(8,128)S(1)} %fusion.570), channel_id=1, source_target_pairs={{0,4},{1,5},{2,6},{3,7},{4,0},{5,1},{6,2},{7,3},{8,12},{9,13},{10,... | collective-permute-start | bytes 49160 | tf_op jit(solution)/shard_map/ppermute | solution.py:63
  593.9 18.6 %collective-permute-start.115 = (bf16[48,2304]{1,0:T(8,128)(2,1)S(1)}, bf16[48,2304]{1,0:T(8,128)(2,1)S(1)}, u32[]{:S(2)}, u32[]{:S(2)}) collective-permute-start(bf16[48,2304]{1,0:T(8,128)(2,1)S(1)} %copy-done.73), channel_id=1, source_target_pairs={{0,2},{1,3},{2,0},{3,1},{4,6},{5,7},{6,4},{7,5},{8,10},{9,11},{10,... | collective-permute-start | bytes 663560 | tf_op jit(solution)/shard_map/ppermute | solution.py:63
  594.7 17.8 %collective-permute-start.116 = (bf16[24,3072]{1,0:T(8,128)(2,1)S(1)}, bf16[24,3072]{1,0:T(8,128)(2,1)S(1)}, u32[]{:S(2)}, u32[]{:S(2)}) collective-permute-start(bf16[24,3072]{1,0:T(8,128)(2,1)S(1)} %copy-done.89), channel_id=1, source_target_pairs={{0,4},{1,5},{2,6},{3,7},{4,0},{5,1},{6,2},{7,3},{8,12},{9,13},{10,... | collective-permute-start | bytes 442376 | tf_op jit(solution)/shard_map/ppermute | solution.py:63
  595.4 21.2 %collective-permute-start.117 = (bf16[24,6144]{1,0:T(8,128)(2,1)S(1)}, bf16[24,6144]{1,0:T(8,128)(2,1)S(1)}, u32[]{:S(2)}, u32[]{:S(2)}) collective-permute-start(bf16[24,6144]{1,0:T(8,128)(2,1)S(1)} %copy-done.69), channel_id=1, source_target_pairs={{0,4},{1,5},{2,6},{3,7},{4,0},{5,1},{6,2},{7,3},{8,12},{9,13},{10,... | collective-permute-start | bytes 884744 | tf_op jit(solution)/shard_map/ppermute | solution.py:63
  (220 other events, 1726.9 us)
